TPU v7x, 32 devices: a whole 2x2x4 slice. The times are simulated.
32 devices in a mesh: dp: 4 (over y, core), expert: 8 (over z, x).
Axes of the slice: x: 2, y: 2, z: 4, core: 2. Of those that a mesh axis runs over, the one named last changes fastest.
Arguments:
- cotangent: bfloat16 [4096, 2048], P(('dp', 'expert')), may hold values from -6 to 6
- gate_prob: bfloat16 [4096, 8], P(('dp', 'expert')), may hold values from 0.029907227 to 0.3984375
- routes: int32 [4096, 8], P(('dp', 'expert')), may hold values from 0 to 15, all different within a row; in each aligned block of 128 rows (0 to 127, 128 to 255, ...) at most 96 rows name the same one
- hidden: bfloat16 [4, 16, 8, 96, 768], P('dp', 'expert'), may hold values from -0.3984375 to 0.3984375
- down_weight: bfloat16 [16, 768, 2048], P('expert'), may hold values from -0.21875 to 0.21875
- sign_seed: int32 [2048], replicated, may hold values from 0 to 1
Outputs:
- grad_hidden: bfloat16 [4, 16, 8, 96, 768], P('dp', 'expert')
- grad_prob: float32 [4096, 8], P(('dp', 'expert'))
- grad_weight: float32 [2048, 16, 768], P('dp', 'expert')
Inputs may be any that keep to these rules, and one draw needn't show every extreme that they name: `routes`: each row names 8 different experts; in each device's block of 128 tokens no expert is named by more than 96 tokens, and in some block one expert is named by exactly 96.
All inputs are finite; a program needn't handle non-finite values.
Results may differ from a plain program's by a relative error of at most 0.015.
Values may be sent and summed in bfloat16 or wider, within the bound.
No kernel may reach another device: no remote copies, remote signals or barrier semaphores. Data moves between devices by JAX's collectives and lax.ppermute only.
A program may use at most 128 MiB of HBM per device.

v0:
```python
import math

import jax
import jax.numpy as jnp
from jax import lax
from jax.sharding import PartitionSpec as P

BLOCK = 128


def hadamard(length):
    index_vec = jnp.arange(length, dtype=jnp.int32)
    anded = jnp.bitwise_and(index_vec[:, None], index_vec[None, :])
    parity = jnp.zeros((length, length), jnp.int32)
    for shift_by in range(max(length.bit_length() - 1, 1)):
        parity = parity + jnp.bitwise_and(jnp.right_shift(anded, shift_by), 1)
    return (1.0 - 2.0 * (parity % 2).astype(jnp.float32)) / math.sqrt(length)


def block_slots(routes, experts_all):
    hit_count = jnp.sum(
        (routes[:, :, None] == jnp.arange(experts_all, dtype=jnp.int32)).astype(jnp.int32),
        axis=1,
        dtype=jnp.int32,
    )
    before = jnp.cumsum(hit_count, axis=0, dtype=jnp.int32) - hit_count
    return jnp.take_along_axis(before, routes, axis=1)


def rotate(grad_term, sign_vec):
    row_total = grad_term.shape[0]
    shaped = grad_term.reshape(row_total // BLOCK, BLOCK, -1) * sign_vec.reshape(
        row_total // BLOCK, BLOCK, 1
    )
    turned = jnp.einsum("ij,bjx->bix", hadamard(BLOCK), shaped, precision=lax.Precision.HIGHEST)
    return turned.reshape(grad_term.shape)


def shards(cotangent, gate_prob, routes, hidden, down_weight, sign_seed):
    experts_here = down_weight.shape[0]
    sources = lax.axis_size("expert")
    capacity = hidden.shape[3]
    tok_rows, top_count = routes.shape
    features = cotangent.shape[1]
    hidden_units = hidden.shape[4]
    experts_all = experts_here * sources
    total_slots = experts_here * sources * capacity
    slot_rank = block_slots(routes, experts_all)
    slot_index = (routes % experts_here * sources + routes // experts_here) * capacity + slot_rank
    pair_count = tok_rows * top_count
    pair_table = jnp.full((total_slots,), pair_count, jnp.int32)
    pair_table = pair_table.at[slot_index.reshape(-1)].set(jnp.arange(pair_count, dtype=jnp.int32))
    send_grad = jnp.take(cotangent, pair_table // top_count, axis=0, mode="fill", fill_value=0)
    send_grad = send_grad.reshape(experts_here, sources, capacity, features)
    send_prob = jnp.take(gate_prob.reshape(-1), pair_table, axis=0, mode="fill", fill_value=0)
    send_prob = send_prob.reshape(experts_here, sources, capacity)
    recv_grad, recv_prob = (
        lax.all_to_all(send_grad, "expert", split_axis=1, concat_axis=1, tiled=True),
        lax.all_to_all(send_prob, "expert", split_axis=1, concat_axis=1, tiled=True),
    )
    slot_rows = sources * capacity
    grad_rows = recv_grad.reshape(experts_here, slot_rows, features)
    prob_rows = recv_prob.reshape(experts_here, slot_rows).astype(jnp.float32)[:, :, None]
    saved_rows = hidden.reshape(experts_here, slot_rows, hidden_units)
    back_grad = jnp.einsum(
        "erd,efd->erf", grad_rows, down_weight, preferred_element_type=jnp.float32
    )
    grad_hidden = (prob_rows * back_grad).astype(jnp.bfloat16).reshape(hidden.shape)
    slot_grad = jnp.sum(back_grad * saved_rows.astype(jnp.float32), axis=2).reshape(
        experts_here, sources, capacity
    )
    returned = lax.all_to_all(slot_grad, "expert", split_axis=1, concat_axis=1, tiled=True)
    grad_prob = returned.reshape(-1)[slot_index]
    weighted = (prob_rows * saved_rows.astype(jnp.float32)).astype(jnp.bfloat16)
    sign_vec = (2 * sign_seed - 1).astype(jnp.float32)
    product = jnp.einsum("erd,erf->def", grad_rows, weighted, preferred_element_type=jnp.float32)
    grad_weight = lax.psum_scatter(
        rotate(product, sign_vec).astype(jnp.bfloat16), "dp", scatter_dimension=0, tiled=True
    ).astype(jnp.float32)
    return (grad_hidden, grad_prob, grad_weight)


def solution(mesh):
    in_specs = (
        P(("dp", "expert"), None),
        P(("dp", "expert"), None),
        P(("dp", "expert"), None),
        P("dp", "expert", None, None, None),
        P("expert", None, None),
        P(),
    )
    out_specs = (
        P("dp", "expert", None, None, None),
        P(("dp", "expert"), None),
        P("dp", "expert", None),
    )
    return jax.shard_map(shards, mesh=mesh, in_specs=in_specs, out_specs=out_specs, check_vma=False)
```

profile of v0, /device:TPU:0, one launch (start us, length us, event | category | flops | bytes accessed | tf_op | source)
XLA Modules:
  0.0 334.8 jit_solution(7294323501822735035)
XLA Ops:
  7.2 0.0 copy-start
  7.2 0.8 convert_reduce_fusion
  7.9 0.7 bitcast_or_fusion
  8.6 0.1 copy.85
  8.7 0.2 reduce_window_sum.11
  8.9 0.1 copy.87
  9.0 0.1 reshape.136
  9.1 0.0 copy-start.3
  9.1 0.0 copy-start.5
  9.1 7.1 %gather_fusion.3 = s32[1024]{0:T(1024)S(1)} fusion(s32[128,16]{1,0:T(8,128)S(1)} %sub.26, s32[1024]{0:T(1024)S(1)} %reshape.136), kind=kCustom, calls=%fused_computation.3 | custom fusion | bytes 16384 | tf_op jit(solution)/shard_map/jit(take_along_axis)/gather | solution.py:27
  16.2 0.1 reshape.139
  16.4 0.1 copy.89
  16.5 0.1 reshape.103
  16.6 4.3 %scatter_custom_fusion = s32[1536]{0:T(1024)S(1)} fusion(s32[1024]{0:T(1024)S(1)} %bitcast.33, s32[1024]{0:T(1024)S(1)} %iota.14, s32[]{:T(128)} %constant.77.clone.1), kind=kCustom, calls=%fused_computation.72 | custom fusion | bytes 6148 | tf_op jit(solution)/shard_map/scatter | solution.py:52
  21.0 0.1 copy.90
  21.1 0.1 reshape.104
  21.2 9.5 %gather_fusion = bf16[1536]{0:T(1024)(128)(2,1)S(1)} fusion(bf16[1024]{0:T(1024)(128)(2,1)S(1)} %reshape.104, s32[2048]{0:T(1024)S(1)} %pad_clamp_fusion.1), kind=kCustom, calls=%fused_computation | custom fusion | bytes 12288 | tf_op jit(solution)/shard_map/jit(_take)/gather | solution.py:55
  30.7 0.1 select_n.72
  30.8 0.6 copy.91
  31.4 7.3 %all-to-all-start = ((bf16[2,8,96]{2,0,1:T(2,128)(2,1)}), bf16[2,8,96]{2,0,1:T(2,128)(2,1)S(1)}, u32[]{:S(2)}, u32[]{:S(2)}) async-start(bf16[2,8,96]{2,0,1:T(2,128)(2,1)} %copy.91), calls=%async_computation | async-start | bytes 8192 | tf_op jit(solution)/shard_map/all_to_all | solution.py:59
  38.7 0.1 broadcast_in_dim.42
  38.8 7.1 %gather_fusion.1 = bf16[1536,2048]{1,0:T(8,128)(2,1)} fusion(bf16[128,2048]{1,0:T(8,128)(2,1)S(1)} %copy-done, s32[2048]{0:T(1024)S(1)} %pad_clamp_fusion), kind=kCustom, calls=%fused_computation.1 | custom fusion | bytes 12589056 | tf_op jit(solution)/shard_map/jit(_take)/gather | solution.py:53
  45.8 6.6 %copy_select_fusion = bf16[2,8,96,2048]{3,2,0,1:T(8,128)(2,1)} fusion(bf16[2,8,96,2048]{3,2,1,0:T(8,128)(2,1)} %bitcast.29, pred[2,8,96]{2,0,1:T(4,128)(4,1)S(1)} %copy.93), kind=kLoop, calls=%fused_computation.7 | loop fusion | flops 3145728 | bytes 12584448 | tf_op jit(solution)/shard_map/jit(_take)/select_n | solution.py:53
  52.4 0.0 all-to-all-done
  52.4 6.1 %all-to-all-start.1 = ((bf16[2,8,96,2048]{3,2,0,1:T(8,128)(2,1)}), bf16[2,8,96,2048]{3,2,0,1:T(8,128)(2,1)}, u32[]{:S(2)}, u32[]{:S(2)}) async-start(bf16[2,8,96,2048]{3,2,0,1:T(8,128)(2,1)} %copy_select_fusion), calls=%async_computation.1 | async-start | bytes 12582912 | tf_op jit(solution)/shard_map/all_to_all | solution.py:58
  58.5 0.2 reduce-scatter.2.cloned.1.call-start
  58.8 0.1 reshape.110
  58.9 137.3 %all-to-all-done.1 = bf16[2,8,96,2048]{3,2,0,1:T(8,128)(2,1)} async-done(((bf16[2,8,96,2048]{3,2,0,1:T(8,128)(2,1)}), bf16[2,8,96,2048]{3,2,0,1:T(8,128)(2,1)}, u32[]{:S(2)}, u32[]{:S(2)}) %all-to-all-start.1) | async-done | bytes 6291488 | tf_op jit(solution)/shard_map/all_to_all | solution.py:58
  196.2 3.4 %copy.95 = bf16[2,8,96,2048]{3,2,1,0:T(8,128)(2,1)S(1)} copy(bf16[2,8,96,2048]{3,2,0,1:T(8,128)(2,1)} %all-to-all-done.1) | data formatting | bytes 12582912 | tf_op jit(solution)/shard_map/all_to_all | solution.py:58
  199.6 8.3 %fusion.4 = f32[2,768,2048]{2,1,0:T(8,128)} fusion(bf16[2,768,2048]{2,1,0:T(8,128)(2,1)S(1)} %bitcast.31, bf16[2,768,768]{2,1,0:T(8,128)(2,1)S(1)} %bitcast.34, f32[2,768]{1,0:T(2,128)S(1)} %reshape.110), kind=kOutput, calls=%fused_computation.15 | convolution fusion | flops 4835377152 | bytes 21239808 | tf_op jit(solution)/shard_map/erd,erf->def/dot_general | solution.py:76
  207.9 12.1 %copy.105 = f32[192,8,16,128]{3,2,1,0:T(8,128)} copy(f32[192,8,16,128]{3,1,2,0:T(8,128)} %bitcast.30) | data formatting | bytes 25165824
  220.1 16.4 %convert_bitcast_fusion = bf16[16,128,1536]{1,2,0:T(8,128)(2,1)S(1)} fusion(f32[16,128,1536]{1,0,2:T(8,128)} %bitcast.28, f32[16,128]{1,0:T(8,128)S(1)} %convert_bitcast_fusion.1), kind=kOutput, calls=%fused_computation.8 | convolution fusion | flops 4838719488 | bytes 18882560 | tf_op jit(solution)/shard_map/ij,bjx->bix/dot_general | solution.py:35
  236.5 18.5 %copy.101 = bf16[16,128,1536]{1,0,2:T(8,128)(2,1)} copy(bf16[16,128,1536]{1,2,0:T(8,128)(2,1)S(1)} %convert_bitcast_fusion) | data formatting | bytes 12582912 | tf_op jit(solution)/shard_map/convert_element_type | solution.py:78
  255.0 10.3 %convert_element_type.55 = bf16[2048,2,768]{0,2,1:T(8,128)(2,1)} reshape(bf16[16,128,1536]{1,0,2:T(8,128)(2,1)} %copy.101) | data formatting | bytes 12582912 | tf_op jit(solution)/shard_map/convert_element_type | solution.py:78
  265.2 0.0 reduce-scatter.2.cloned.1.call-update
  265.3 0.1 copy.98
  265.4 0.1 reshape.130
  265.5 10.4 %fusion.2 = (f32[2,768]{1,0:T(2,128)S(1)}, bf16[2,768,768]{2,1,0:T(8,128)(2,1)}) fusion(bf16[2,768,768]{2,1,0:T(8,128)(2,1)S(1)} %bitcast.35, f32[2,768]{1,0:T(2,128)S(1)} %reshape.110, bf16[2,768,2048]{2,1,0:T(8,128)(2,1)} %bitcast.32, bf16[2,768,2048]{2,1,0:T(8,128)(2,1)} %param.10), kind=kOutput, calls=%fused_computation.12 | convolution fusion | flops 4837734912 | bytes 17313792 | tf_op jit(solution)/shard_map/erd,efd->erf/dot_general | solution.py:65
  275.9 0.1 reshape.107
  276.0 0.6 copy.96
  276.6 3.6 %all-to-all-start.2 = ((f32[2,8,96]{2,0,1:T(2,128)}), f32[2,8,96]{2,0,1:T(2,128)S(1)}, u32[]{:S(2)}, u32[]{:S(2)}) async-start(f32[2,8,96]{2,0,1:T(2,128)} %copy.96), calls=%async_computation.2 | async-start | bytes 16384 | tf_op jit(solution)/shard_map/all_to_all | solution.py:72
  280.2 6.5 %all-to-all-done.2 = f32[2,8,96]{2,0,1:T(2,128)S(1)} async-done(((f32[2,8,96]{2,0,1:T(2,128)}), f32[2,8,96]{2,0,1:T(2,128)S(1)}, u32[]{:S(2)}, u32[]{:S(2)}) %all-to-all-start.2) | async-done | bytes 6176 | tf_op jit(solution)/shard_map/all_to_all | solution.py:72
  286.7 0.1 reshape.108
  286.8 6.1 %gather_fusion.2 = f32[1024]{0:T(1024)S(1)} fusion(f32[1536]{0:T(1024)S(1)} %reshape.108, s32[1024]{0:T(1024)S(1)} %broadcast_clamp_fusion), kind=kCustom, calls=%fused_computation.2 | custom fusion | bytes 12288 | tf_op jit(solution)/shard_map/gather | solution.py:73
  293.0 0.1 reshape.129
  293.0 0.7 copy.102
  293.7 29.2 %reduce-scatter.2.cloned.1.call-done = bf16[512,2,768]{0,2,1:T(8,128)(2,1)} async-done(((bf16[2048,2,768]{0,2,1:T(8,128)(2,1)}), bf16[512,2,768]{0,2,1:T(8,128)(2,1)}) %reduce-scatter.2.cloned.1.call-update) | async-done | bytes 1572880 | tf_op jit(solution)/shard_map/reduce_scatter | solution.py:77
  322.9 5.1 %copy.103 = f32[512,2,768]{2,1,0:T(2,128)} copy(bf16[512,2,768]{0,2,1:T(8,128)(2,1)} %reduce-scatter.2.cloned.1.call-done) | data formatting | bytes 4718592
  (26 shorter events, 0.2 us)
Async XLA Ops:
  7.2 31.6 %copy-start = (bf16[128,2048]{1,0:T(8,128)(2,1)S(1)}, bf16[128,2048]{1,0:T(8,128)(2,1)}, u32[]{:S(2)}) copy-start(bf16[128,2048]{1,0:T(8,128)(2,1)} %param.6) | copy-start | bytes 1572868
  9.1 7.2 %copy-start.3 = (s32[128,8]{0,1:T(8,128)S(1)}, s32[128,8]{0,1:T(8,128)}, u32[]{:S(2)}) copy-start(s32[128,8]{0,1:T(8,128)} %param.8) | copy-start | bytes 12292
  9.1 11.8 %copy-start.5 = (bf16[128,8]{0,1:T(8,128)(2,1)S(1)}, bf16[128,8]{0,1:T(8,128)(2,1)}, u32[]{:S(2)}) copy-start(bf16[128,8]{0,1:T(8,128)(2,1)} %param.7) | copy-start | bytes 6148
  31.4 21.0 %all-to-all-start = ((bf16[2,8,96]{2,0,1:T(2,128)(2,1)}), bf16[2,8,96]{2,0,1:T(2,128)(2,1)S(1)}, u32[]{:S(2)}, u32[]{:S(2)}) async-start(bf16[2,8,96]{2,0,1:T(2,128)(2,1)} %copy.91), calls=%async_computation | async-start | bytes 8192 | tf_op jit(solution)/shard_map/all_to_all | solution.py:59
  52.4 6.4 %copy-start.4 = (s32[2048]{0:T(1024)S(1)}, s32[2048]{0:T(1024)}, u32[]{:S(2)}) copy-start(s32[2048]{0:T(1024)} %param.11) | copy-start | bytes 24580
  52.4 143.8 %all-to-all-start.1 = ((bf16[2,8,96,2048]{3,2,0,1:T(8,128)(2,1)}), bf16[2,8,96,2048]{3,2,0,1:T(8,128)(2,1)}, u32[]{:S(2)}, u32[]{:S(2)}) async-start(bf16[2,8,96,2048]{3,2,0,1:T(8,128)(2,1)} %copy_select_fusion), calls=%async_computation.1 | async-start | bytes 12582912 | tf_op jit(solution)/shard_map/all_to_all | solution.py:58
  58.5 264.3 %reduce-scatter.2.cloned.1.call-start = ((), (), s32[]{:S(2)}) async-start(), calls=%async_computation.4 | async-start | bytes 7864320 | tf_op jit(solution)/shard_map/reduce_scatter | solution.py:77
  58.9 140.7 %copy-start.6 = (bf16[1,2,8,96,768]{4,3,2,1,0:T(8,128)(2,1)S(1)}, bf16[1,2,8,96,768]{4,3,2,1,0:T(8,128)(2,1)}, u32[]{:S(2)}) copy-start(bf16[1,2,8,96,768]{4,3,2,1,0:T(8,128)(2,1)} %param.9) | copy-start | bytes 7077892
  199.6 8.4 %copy-start.2 = (bf16[2,8,96,2048]{3,2,1,0:T(8,128)(2,1)}, bf16[2,8,96,2048]{3,2,1,0:T(8,128)(2,1)S(1)}, u32[]{:S(2)}) copy-start(bf16[2,8,96,2048]{3,2,1,0:T(8,128)(2,1)S(1)} %copy.95) | copy-start | bytes 18874372
  276.6 10.1 %all-to-all-start.2 = ((f32[2,8,96]{2,0,1:T(2,128)}), f32[2,8,96]{2,0,1:T(2,128)S(1)}, u32[]{:S(2)}, u32[]{:S(2)}) async-start(f32[2,8,96]{2,0,1:T(2,128)} %copy.96), calls=%async_computation.2 | async-start | bytes 16384 | tf_op jit(solution)/shard_map/all_to_all | solution.py:72
  286.8 41.2 %copy-start.1 = (bf16[128,2048]{1,0:T(8,128)(2,1)S(1)}, bf16[128,2048]{1,0:T(8,128)(2,1)}, u32[]{:S(2)}) copy-start(bf16[128,2048]{1,0:T(8,128)(2,1)} %param.6) | copy-start | bytes 1572868
Sparse Core Ops, SparseCore 0:
  265.4 57.4 reduce-scatter.1
where the time goes:
time: 336 us; the launch traced here: 335 us
  waiting for transfers between devices  173 us (51%)
  local copies, waits for them, and re-layouts  86.9 us (26%)
  matrix products  35.1 us (10%)
  starting transfers between devices  17.2 us (5%)
  between operations  14.2 us (4%)
  other arithmetic  8.3 us (2%)
    all_to_all x1, waiting for transfers between devices, shards(): lax.all_to_all(send_grad, 'expert', split_axis=1, concat_axis=1, tiled=True)  137 us
    reduce_scatter x1, waiting for transfers between devices, shards(): lax.psum_scatter(rotate(product, sign_vec).astype(jnp.bfloat16), 'dp', sc...  29.2 us
    convert_element_type x2, local copies, waits for them, and re-layouts, shards(): rotate(product, sign_vec).astype(jnp.bfloat16)  28.8 us
    unnamed x18, local copies, waits for them, and re-layouts  18.1 us
    dot_general x1, matrix products, rotate(): jnp.einsum('ij,bjx->bix', hadamard(BLOCK), shaped, precision=lax.Precisio...  16.4 us
    dot_general x1, matrix products, shards(): jnp.einsum('erd,efd->erf', grad_rows, down_weight, preferred_element_type...  10.4 us
    gather x1, local copies, waits for them, and re-layouts, shards(): jnp.take(gate_prob.reshape(-1), pair_table, axis=0, mode='fill', fill_val...  9.46 us
    dot_general x1, matrix products, shards(): jnp.einsum('erd,erf->def', grad_rows, weighted, preferred_element_type=jn...  8.35 us
  transfers between devices with their start and end apart: 4, of which 3 were waited for; matrix products, arithmetic and copies ran while one was open for 10% of the time, Pallas kernels for 0%

commit v1 on v0

v1 whole, which is shorter than its diff:
```python
import functools
import math

import jax
import jax.numpy as jnp
from jax import lax
from jax.experimental import pallas as pl
from jax.experimental.pallas import tpu as pltpu
from jax.sharding import PartitionSpec as P

BLOCK = 128
LANES = 128
CORES = 2
NO_SLOT = 512.0
VMEM = 56 * 1024 * 1024
F32 = jnp.float32
BF16 = jnp.bfloat16


ANY = pl.BlockSpec(memory_space=pl.ANY)
SMEM = pl.BlockSpec(memory_space=pltpu.SMEM)


def params(limit=VMEM):
    return pltpu.CompilerParams(vmem_limit_bytes=limit)


def dot(a, b, contract=((1,), (0,))):
    return lax.dot_general(a, b, (contract, ((), ())), preferred_element_type=F32)


def iota(shape, axis):
    return lax.broadcasted_iota(jnp.int32, shape, axis)


def pack_kernel(pieces, replicas, cot_ref, gate_ref, route_ref, *out_refs):
    rows_own = cot_ref.shape[1] // replicas
    for out_ref, (start, width) in zip(out_refs, pieces):
        for q in range(replicas):
            at = q * rows_own + start
            out_ref[:, q * width : (q + 1) * width] = cot_ref[:, at : at + width]
    tokens = cot_ref.shape[0]
    line = iota((LANES, tokens), 0)
    half = LANES // 2
    gate = jnp.zeros((LANES, tokens), F32)
    hit = jnp.zeros((LANES, tokens), F32)
    for k in range(route_ref.shape[0]):
        named = route_ref[k : k + 1, :]
        gate = gate + jnp.where(named == line, gate_ref[k : k + 1, :].astype(F32), 0.0)
        hit = hit + jnp.where(named == line - half, 1.0, 0.0)
    earlier = (iota((tokens, tokens), 0) < iota((tokens, tokens), 1)).astype(F32).astype(BF16)
    rank = dot(hit.astype(BF16), earlier)
    table = jnp.where(line < half, gate, jnp.where(hit > 0, rank, NO_SLOT))
    first = out_refs[0]
    first[:, first.shape[1] - tokens :] = table.astype(BF16)


def pack(cotangent, gate_prob, routes, pieces, replicas):
    tokens = cotangent.shape[0]
    widths = [replicas * width for _, width in pieces]
    widths[0] += tokens
    return pl.pallas_call(
        functools.partial(pack_kernel, pieces, replicas),
        out_shape=[jax.ShapeDtypeStruct((tokens, width), BF16) for width in widths],
        compiler_params=params(),
        name="pack",
    )(cotangent, gate_prob.T, routes.T)


EDGE, MIDDLE = ((0, 1), (1, 0), (2, 3), (3, 2)), ((1, 2), (2, 1))
OUTWARD, INWARD = ((1, 0), (2, 3)), ((0, 1), (3, 2))


def along(value, pairs):
    return lax.ppermute(value, "expert", [(2 * a + x, 2 * b + x) for a, b in pairs for x in (0, 1)])


def across(value, rows):
    return lax.ppermute(value, "expert", [(2 * a + x, 2 * a + 1 - x) for a in rows for x in (0, 1)])


def fence(*values):
    return lax.optimization_barrier(values)


def line_slots():
    place = lax.axis_index("expert")
    line, side = place // 2, place % 2
    middle = (line == 1) | (line == 2)
    near = line ^ 1
    far = jnp.where(middle, 3 - line, 3 - near)
    last = far ^ 1
    lines = [line, near, far, far, last, last]
    valid = [True, True, middle, ~middle, middle, ~middle]
    same = [jnp.where(ok, 2 * at + side, -1) for at, ok in zip(lines, valid)]
    other = [jnp.where(ok, 2 * at + 1 - side, -1) for at, ok in zip(lines, valid)]
    return jnp.stack(same + other).astype(jnp.int32)


def load_parts(slots_ref, refs, tokens, dst_ref, sem):
    def each(action):
        for i, ref in enumerate(refs):

            @pl.when(slots_ref[i] >= 0)
            def _():
                at = pl.multiple_of(slots_ref[i] * tokens, tokens)
                action(pltpu.make_async_copy(ref, dst_ref.at[pl.ds(at, ref.shape[0]), :], sem.at[i]))

    each(lambda copy: copy.start())
    each(lambda copy: copy.wait())


def owner_of(j, groups):
    place = lax.axis_index("dp")
    chip, core = place // CORES, place % CORES
    owner_core = (1 - core) if j < groups else core
    return lax.rem(chip + j % groups + 1, groups) * CORES + owner_core


def hits(table, expert, experts_here, cap_rows):
    rank = table[experts_here + expert : experts_here + expert + 1, :]
    return iota((cap_rows, table.shape[1]), 0).astype(F32) == rank


def route_kernel(first, count, bands, width, groups, cap, slots_ref, *refs):
    parts, refs = refs[:count], refs[count:]
    if first:
        hidden_ref, refs = refs[0], refs[1:]
    else:
        weighted_ref, table_ref, refs = refs[0], refs[1], refs[2:]
    outs, refs = refs[: len(bands)], refs[len(bands) :]
    routed_out, refs = refs[0], refs[1:]
    if first:
        weighted_ref, table_ref, refs = refs[0], refs[1], refs[2:]
    rows, routed, part_sem, out_sem = refs
    expert = pl.program_id(0)
    experts_here, slots, columns = routed.shape
    sources, _, tokens = table_ref.shape
    cap_rows = slots // sources
    keep = pltpu.make_async_copy(routed, routed_out, out_sem)

    @pl.when(expert == 0)
    def _():
        load_parts(slots_ref, parts, tokens, rows, part_sem)
        if first:
            base = lax.axis_index("expert") * experts_here
            row, lane = iota((8, LANES), 0), iota((8, LANES), 1)
            wanted = base + jnp.where(row < experts_here, row, row - experts_here + LANES // 2)
            chosen = ((lane == wanted) & (row < 2 * experts_here)).astype(F32).astype(BF16)

        def fill(s, carry):
            at = pl.multiple_of(s * tokens, tokens)
            if first:
                table = dot(chosen, rows[pl.ds(at, tokens), columns : columns + tokens])
                table_ref[s] = table
            else:
                table = table_ref[s]
            picked = [hits(table, e, experts_here, cap_rows).astype(F32).astype(BF16) for e in range(experts_here)]
            got = dot(jnp.concatenate(picked, axis=0), rows[pl.ds(at, tokens), :columns]).astype(BF16)
            to = pl.multiple_of(s * cap_rows, cap_rows)
            for e in range(experts_here):
                routed[e, pl.ds(to, cap_rows), :] = got[e * cap_rows : (e + 1) * cap_rows, :]
            return carry

        lax.fori_loop(0, sources, fill, 0, unroll=sources <= 8)
        keep.start()

    if first:

        def weigh(s, carry):
            table = table_ref[s]
            line = iota(table.shape, 0)
            rank = jnp.sum(jnp.where(line == experts_here + expert, table, 0.0), axis=0, keepdims=True)
            prob = jnp.sum(jnp.where(line == expert, table, 0.0), axis=0, keepdims=True)
            hit = iota((cap, tokens), 0).astype(F32) == rank
            of_slot = jnp.sum(jnp.where(hit, prob, 0.0), axis=1, keepdims=True)
            scaled = of_slot * hidden_ref[0, s].astype(F32)
            if cap_rows > cap:
                scaled = jnp.concatenate([scaled, jnp.zeros((cap_rows - cap, scaled.shape[1]), F32)], axis=0)
            weighted_ref[0, pl.ds(pl.multiple_of(s * cap_rows, cap_rows), cap_rows), :] = scaled.astype(BF16)
            return carry

        lax.fori_loop(0, sources, weigh, 0, unroll=sources <= 8)

    grad_bands(routed.at[expert], weighted_ref, outs, bands, width, groups)

    @pl.when(expert == experts_here - 1)
    def _():
        keep.wait()


def grad_bands(routed, weighted_ref, outs, bands, width, groups):
    taken = []
    for band in bands:
        for j in band:
            at = pl.multiple_of(owner_of(j, groups) * width, LANES)
            taken.append(routed[:, pl.ds(at, width)])
    made = dot(jnp.concatenate(taken, axis=1), weighted_ref[0], ((0,), (0,))).astype(BF16)
    at = 0
    for out_ref, band in zip(outs, bands):
        out_ref[...] = made[at : at + len(band) * width, :]
        at += len(band) * width


def band_outputs(bands, width, experts_here, units):
    specs = [pl.BlockSpec((len(band) * width, units), lambda e: (0, e)) for band in bands]
    shapes = [jax.ShapeDtypeStruct((len(band) * width, experts_here * units), BF16) for band in bands]
    return specs, shapes


def route(parts, slots, width, bands, groups, tokens, hidden=None, weighted=None, table=None, cap=None):
    first = weighted is None
    if first:
        experts_here, sources, cap, units = hidden.shape
        cap_rows = -(-cap // 16) * 16
        slot_rows = sources * cap_rows
    else:
        experts_here, slot_rows, units = weighted.shape
        sources = table.shape[0]
    columns = parts[0].shape[1] - (tokens if first else 0)
    weighted_spec = pl.BlockSpec((1, slot_rows, units), lambda e: (e, 0, 0))
    table_spec = pl.BlockSpec((sources, 8, tokens), lambda e: (0, 0, 0))
    band_specs, band_shapes = band_outputs(bands, width, experts_here, units)
    routed_shape = jax.ShapeDtypeStruct((experts_here, slot_rows, columns), BF16)
    if first:
        operands = [hidden]
        in_specs = [pl.BlockSpec((1, sources, cap, units), lambda e: (e, 0, 0, 0))]
        more_specs = [weighted_spec, table_spec]
        more_shapes = [
            jax.ShapeDtypeStruct((experts_here, slot_rows, units), BF16),
            jax.ShapeDtypeStruct((sources, 8, tokens), F32),
        ]
    else:
        operands, in_specs, more_specs, more_shapes = [weighted, table], [weighted_spec, table_spec], [], []
    return pl.pallas_call(
        functools.partial(route_kernel, first, len(parts), bands, width, groups, cap),
        grid=(experts_here,),
        in_specs=[SMEM] + [ANY] * len(parts) + in_specs,
        out_specs=band_specs + [ANY] + more_specs,
        out_shape=band_shapes + [routed_shape] + more_shapes,
        scratch_shapes=[
            pltpu.VMEM((sources * tokens, parts[0].shape[1]), BF16),
            pltpu.VMEM((experts_here, slot_rows, columns), BF16),
            pltpu.SemaphoreType.DMA((len(parts),)),
            pltpu.SemaphoreType.DMA,
        ],
        compiler_params=params(),
        cost_estimate=pl.CostEstimate(
            flops=2 * slot_rows * experts_here * columns * (tokens + units),
            bytes_accessed=4 * slot_rows * experts_here * columns,
            transcendentals=0,
        ),
        name="route",
    )(slots, *parts, *operands)


def rest_kernel(bands, width, groups, routed_ref, weighted_ref, *outs):
    grad_bands(routed_ref.at[0], weighted_ref, outs, bands, width, groups)


def rest(routed, weighted, bands, width, groups):
    experts_here, slot_rows, columns = routed.shape
    units = weighted.shape[2]
    band_specs, band_shapes = band_outputs(bands, width, experts_here, units)
    return pl.pallas_call(
        functools.partial(rest_kernel, bands, width, groups),
        grid=(experts_here,),
        in_specs=[
            pl.BlockSpec((1, slot_rows, columns), lambda e: (e, 0, 0)),
            pl.BlockSpec((1, slot_rows, units), lambda e: (e, 0, 0)),
        ],
        out_specs=band_specs,
        out_shape=band_shapes,
        compiler_params=params(),
        cost_estimate=pl.CostEstimate(
            flops=slot_rows * experts_here * columns * units,
            bytes_accessed=4 * slot_rows * experts_here * columns,
            transcendentals=0,
        ),
        name="rest",
    )(routed, weighted)


def back_kernel(pieces, replicas, *refs):
    routed, refs = refs[: len(pieces)], refs[len(pieces) :]
    table_ref, weight_ref, hidden_ref, grad_ref, prob_ref, held = refs
    expert = pl.program_id(0)
    experts_here = pl.num_programs(0)
    _, sources, cap, units = hidden_ref.shape
    tokens = table_ref.shape[2]
    cap_rows = held.shape[0] // sources
    columns = []
    for q in range(replicas):
        for ref, (_, width) in zip(routed, pieces):
            columns.append(ref[0, :, q * width : (q + 1) * width])
    held[...] = dot(jnp.concatenate(columns, axis=1), weight_ref[0], ((1,), (1,)))

    def finish(s, carry):
        mine = held[pl.ds(pl.multiple_of(s * cap_rows, cap_rows), cap), :]
        table = table_ref[s]
        line = iota(table.shape, 0)
        rank = jnp.sum(jnp.where(line == experts_here + expert, table, 0.0), axis=0, keepdims=True)
        prob = jnp.sum(jnp.where(line == expert, table, 0.0), axis=0, keepdims=True)
        hit = iota((cap, tokens), 0).astype(F32) == rank
        of_slot = jnp.sum(jnp.where(hit, prob, 0.0), axis=1, keepdims=True)
        grad_ref[0, pl.ds(s, 1)] = (of_slot * mine).astype(BF16)[None]
        inner = jnp.sum(mine * hidden_ref[0, s].astype(F32), axis=1, keepdims=True)
        prob_ref[pl.ds(s, 1), pl.ds(expert, 1), :] = jnp.sum(jnp.where(hit, inner, 0.0), axis=0, keepdims=True)[None]
        return carry

    lax.fori_loop(0, sources, finish, 0, unroll=sources <= 8)


def back(routed, table, weight, hidden, pieces, replicas):
    experts_here, sources, cap, units = hidden.shape
    features = weight.shape[2]
    tokens = table.shape[2]
    slot_rows = routed[0].shape[1]
    return pl.pallas_call(
        functools.partial(back_kernel, pieces, replicas),
        grid=(experts_here,),
        in_specs=[pl.BlockSpec((1,) + part.shape[1:], lambda e: (e, 0, 0)) for part in routed]
        + [
            pl.BlockSpec(table.shape, lambda e: (0, 0, 0)),
            pl.BlockSpec((1, units, features), lambda e: (e, 0, 0)),
            pl.BlockSpec((1, sources, cap, units), lambda e: (e, 0, 0, 0)),
        ],
        out_specs=[
            pl.BlockSpec((1, sources, cap, units), lambda e: (e, 0, 0, 0)),
            pl.BlockSpec((sources, experts_here, tokens), lambda e: (0, 0, 0)),
        ],
        out_shape=[
            jax.ShapeDtypeStruct(hidden.shape, BF16),
            jax.ShapeDtypeStruct((sources, experts_here, tokens), F32),
        ],
        scratch_shapes=[pltpu.VMEM((slot_rows, units), F32)],
        compiler_params=params(),
        cost_estimate=pl.CostEstimate(
            flops=2 * experts_here * slot_rows * features * units,
            bytes_accessed=2 * (weight.size + 2 * hidden.size + experts_here * slot_rows * features),
            transcendentals=0,
        ),
        name="back",
    )(*routed, table, weight, hidden)


def rotate_kernel(count, experts_here, turn_ref, *refs):
    parts, out_ref = refs[:count], refs[-1]
    units = parts[0].shape[1] // experts_here
    total = parts[0][...].astype(F32)
    for ref in parts[1:]:
        total = total + ref[...].astype(F32)
    side = jnp.concatenate([total[:, e * units : (e + 1) * units] for e in range(experts_here)], axis=0)
    high = side.astype(BF16)
    low = (side - high.astype(F32)).astype(BF16)
    turn = turn_ref[0]
    turned = (dot(turn, high) + dot(turn, low)) * (1.0 / math.sqrt(BLOCK))
    out_ref[...] = turned.reshape(out_ref.shape)


def rotate(parts, turns, first_block, rows_out, experts_here, filled):
    rows, lines = parts[0].shape
    units = lines // experts_here
    extra = [] if filled is None else [filled]
    return pl.pallas_call(
        functools.partial(rotate_kernel, len(parts), experts_here),
        grid=(rows // BLOCK,),
        in_specs=[pl.BlockSpec((1,) + turns.shape[1:], lambda b: (first_block + b, 0, 0))]
        + [pl.BlockSpec((BLOCK, lines), lambda b: (b, 0)) for _ in parts]
        + [ANY] * len(extra),
        out_specs=pl.BlockSpec((BLOCK, experts_here, units), lambda b: (first_block + b, 0, 0)),
        out_shape=jax.ShapeDtypeStruct((rows_out, experts_here, units), F32),
        input_output_aliases={1 + len(parts): 0} if extra else {},
        compiler_params=params(),
        name="rotate",
    )(turns, *parts, *extra)


def turn_matrices(sign_seed, rows_own, experts_here):
    row = jnp.arange(BLOCK * experts_here, dtype=jnp.int32)
    anded = (row // experts_here)[:, None] & (row % BLOCK)[None, :]
    parity = sum(((anded >> shift) & 1) for shift in range(BLOCK.bit_length() - 1)) & 1
    same = (row % experts_here)[:, None] == (row // BLOCK)[None, :]
    matrix = jnp.where(same, 1 - 2 * parity, 0)
    own = lax.dynamic_slice_in_dim(2 * sign_seed - 1, lax.axis_index("dp") * rows_own, rows_own)
    signs = jnp.tile(own.reshape(-1, 1, BLOCK), (1, 1, experts_here))
    return (matrix[None] * signs).astype(BF16)


def shards(cotangent, gate_prob, routes, hidden, down_weight, sign_seed):
    tokens, features = cotangent.shape
    sources, replicas = lax.axis_size("expert"), lax.axis_size("dp")
    groups = replicas // CORES
    experts_here, units = down_weight.shape[0], down_weight.shape[1]
    rows_own = features // replicas
    saved = hidden[0]
    cap = saved.shape[2]
    width = rows_own // 2
    pieces = [(0, width), (width, width)]
    turns = turn_matrices(sign_seed, rows_own, experts_here)
    sent = pack(cotangent, gate_prob, routes, pieces, replicas)
    away_bands = [tuple(range(groups - 1)), tuple(range(groups, 2 * groups - 1))]
    here_bands = [(groups - 1,), (2 * groups - 1,)]

    def swap(value):
        return lax.ppermute(value, "dp", [(i, i ^ 1) for i in range(replicas)])

    def to_chips(value):
        moved = []
        for k in range(1, groups):
            pairs = [(i, (i // CORES + k) % groups * CORES + i % CORES) for i in range(replicas)]
            moved.append(lax.ppermute(value[(k - 1) * width : k * width], "dp", pairs))
        return moved

    def add(a, b):
        return (a.astype(F32) + b.astype(F32)).astype(BF16)

    def route_first(parts, slots):
        return route(parts, slots, width, away_bands + here_bands, groups, tokens, hidden=saved)

    if sources == 8:
        a, b = sent
        slots = line_slots()
        a_x0, a_s1, a_s2 = fence(across(a, range(4)), along(a, EDGE), along(a, MIDDLE))
        a_x1, a_s3, a_s4 = fence(across(a_s1, range(4)), along(a_s1, MIDDLE), along(a_s2, OUTWARD))
        a_x2, a_x4, a_s5 = fence(across(a_s2, (1, 2)), across(a_s4, (0, 3)), along(a_s3, OUTWARD))
        a_x3, a_x5, b, b_s1, b_s2 = fence(
            across(a_s3, (1, 2)), across(a_s5, (0, 3)), b, along(b, EDGE), along(b, MIDDLE)
        )
        a_parts = [a, a_s1, a_s2, a_s4, a_s3, a_s5, a_x0, a_x1, a_x2, a_x4, a_x3, a_x5]
        made = route_first(a_parts, slots)
        b_x0, b_s3, b_s4, *made = fence(across(b, range(4)), along(b_s1, MIDDLE), along(b_s2, OUTWARD), *made)
        away_send, away_keep, here_send, here_keep, routed_a, weighted, table = made
        away_got, here_got = swap(away_send), swap(here_send)
        away_sum = add(away_got, away_keep)
        b_x3, b_x4, b_w, b_s5, away_sum, here_got = fence(
            across(b_s3, (1, 2)), across(b_s4, (0, 3)), along(b_x0, INWARD), along(b_s3, OUTWARD), away_sum, here_got
        )
        final_a = [here_keep, here_got] + to_chips(away_sum)
        b_x2, b_x1, b_w5 = fence(across(b_s2, (1, 2)), across(b_s1, (0, 3)), along(b_x3, OUTWARD))
        b_parts = [b, b_s1, b_s2, b_s4, b_s3, b_s5, b_x0, b_x1, b_w, b_x2, b_x4, b_x3, b_w5]
        middle = (slots[2] >= 0)
        b_slots = jnp.concatenate(
            [
                slots[:7],
                jnp.where(middle, -1, slots[7:8]),
                jnp.where(middle, slots[7:8], -1),
                slots[8:],
            ]
        )
    else:
        a, b = [lax.all_gather(part, "expert", axis=0, tiled=True) for part in sent]
        slots = b_slots = jnp.zeros((1,), jnp.int32)
        a_parts, b_parts = [a], [b]
        made = route_first(a_parts, slots)
        away_send, away_keep, here_send, here_keep, routed_a, weighted, table = made
        final_a = [here_keep, swap(here_send)] + to_chips(add(swap(away_send), away_keep))

    away_send, away_keep, routed_b = route(
        b_parts, b_slots, width, away_bands, groups, tokens, weighted=weighted, table=table, cap=cap
    )
    arrived = to_chips(add(swap(away_send), away_keep))
    here_send, here_keep = rest(routed_b, weighted, here_bands, width, groups)
    final_b = [here_keep, swap(here_send)] + arrived

    grad_hidden, grad_slots = back([routed_a, routed_b], table, down_weight, saved, pieces, replicas)
    returned = lax.all_to_all(grad_slots, "expert", split_axis=0, concat_axis=0, tiled=True)
    of_token = returned.reshape(-1, 1, tokens)
    named = routes.T[None] == jnp.arange(of_token.shape[0], dtype=jnp.int32)[:, None, None]
    grad_prob = jnp.sum(jnp.where(named, of_token, 0.0), axis=0).T

    out = rotate(final_a, turns, 0, rows_own, experts_here, None)
    out = rotate(final_b, turns, width // BLOCK, rows_own, experts_here, out)
    return (grad_hidden[None], grad_prob, out)


def solution(mesh):
    in_specs = (
        P(("dp", "expert"), None),
        P(("dp", "expert"), None),
        P(("dp", "expert"), None),
        P("dp", "expert", None, None, None),
        P("expert", None, None),
        P(),
    )
    out_specs = (
        P("dp", "expert", None, None, None),
        P(("dp", "expert"), None),
        P("dp", "expert", None),
    )
    return jax.shard_map(shards, mesh=mesh, in_specs=in_specs, out_specs=out_specs, check_vma=False)
```

time: 336 us -> 142 us (0.42)
  waiting for transfers between devices: 173 us -> 48.1 us
  local copies, waits for them, and re-layouts: 86.9 us -> 3.02 us
  Pallas kernels: 0 us -> 40 us
  matrix products: 35.1 us -> 0 us
  starting transfers between devices: 17.2 us -> 44.8 us
  between operations: 14.2 us -> 1.19 us
  other arithmetic: 8.3 us -> 4.09 us
    all_to_all x3 -> x1, waiting for transfers between devices: 144 us -> 5.6 us  [shards(): lax.all_to_all(grad_slots, 'expert', split_axis=0, concat_axis=0, tiled=T...]
    ppermute x0 -> x29, waiting for transfers between devices: none -> 42.5 us  [the longest x12 20.3 us: along(): lax.ppermute(value, 'expert', [(2 * a + x, 2 * b + x) for a, b in pairs f...]
    ppermute x0 -> x29, starting transfers between devices: none -> 40.2 us  [the longest x11 19.4 us: across(): lax.ppermute(value, 'expert', [(2 * a + x, 2 * a + 1 - x) for a in rows f...]
    pallas_call x0 -> x7, Pallas kernels: none -> 40 us  [the longest x2 17 us: route(): pl.pallas_call(functools.partial(route_kernel, first, len(parts), bands,...]
    dot_general x3 -> x0, matrix products: 35.1 us -> none  [the longest x1 16.4 us: rotate(): jnp.einsum('ij,bjx->bix', hadamard(BLOCK), shaped, precision=lax.Precisio...]
    gather x9 -> x0, local copies, waits for them, and re-layouts: 30.1 us -> none  [the longest x1 9.46 us: shards(): jnp.take(gate_prob.reshape(-1), pair_table, axis=0, mode='fill', fill_val...]
    reduce_scatter x1 -> x0, waiting for transfers between devices: 29.2 us -> none  [shards(): lax.psum_scatter(rotate(product, sign_vec).astype(jnp.bfloat16), 'dp', sc...]
    convert_element_type x3 -> x0, local copies, waits for them, and re-layouts: 28.9 us -> none  [the longest x2 28.8 us: shards(): rotate(product, sign_vec).astype(jnp.bfloat16)]
  transfers between devices with their start and end apart: 4 -> 30, of which waited for: 3 -> 13; matrix products, arithmetic and copies ran while one was open for 10% -> 4% of each run, Pallas kernels for 0% -> 20%
where the time goes in v1:
time: 142 us; the launch traced here: 141 us
  waiting for transfers between devices  48.1 us (34%)
  starting transfers between devices  44.8 us (32%)
  Pallas kernels  40 us (28%)
  other arithmetic  4.09 us (3%)
  local copies, waits for them, and re-layouts  3.02 us (2%)
    ppermute x12, waiting for transfers between devices, along(): lax.ppermute(value, 'expert', [(2 * a + x, 2 * b + x) for a, b in pairs f...  20.3 us
    ppermute x11, starting transfers between devices, across(): lax.ppermute(value, 'expert', [(2 * a + x, 2 * a + 1 - x) for a in rows f...  19.4 us
    ppermute x12, starting transfers between devices, along(): lax.ppermute(value, 'expert', [(2 * a + x, 2 * b + x) for a, b in pairs f...  17.8 us
    ppermute x11, waiting for transfers between devices, across(): lax.ppermute(value, 'expert', [(2 * a + x, 2 * a + 1 - x) for a in rows f...  17.4 us
    pallas_call x2, Pallas kernels, route(): pl.pallas_call(functools.partial(route_kernel, first, len(parts), bands,...  17 us
    pallas_call x1, Pallas kernels, back(): pl.pallas_call(functools.partial(back_kernel, pieces, replicas), grid=(ex...  10 us
    pallas_call x2, Pallas kernels, rotate(): pl.pallas_call(functools.partial(rotate_kernel, len(parts), experts_here)...  6.48 us
    all_to_all x1, waiting for transfers between devices, shards(): lax.all_to_all(grad_slots, 'expert', split_axis=0, concat_axis=0, tiled=T...  5.6 us
  transfers between devices with their start and end apart: 30, of which 13 were waited for; matrix products, arithmetic and copies ran while one was open for 4% of the time, Pallas kernels for 20%

profile of v1, /device:TPU:0, one launch (start us, length us, event | category | flops | bytes accessed | tf_op | source)
XLA Modules:
  0.0 141.1 jit_solution(4099628747529421301)
XLA Ops:
  0.6 2.0 %pack.1 = (bf16[128,1152]{1,0:T(8,128)(2,1)}, bf16[128,1024]{1,0:T(8,128)(2,1)}) custom-call(bf16[128,2048]{1,0:T(8,128)(2,1)} %cot_ref.1, bf16[8,128]{1,0:T(8,128)(2,1)} %bitcast.31, s32[8,128]{1,0:T(8,128)} %bitcast.28), custom_call_target="tpu_custom_call" | custom-call | tf_op jit(solution)/shard_map/pack/pallas_call | solution.py:62
  2.6 2.9 %collective-permute-start = (bf16[128,1152]{1,0:T(8,128)(2,1)}, bf16[128,1152]{1,0:T(8,128)(2,1)S(1)}, u32[]{:S(2)}, u32[]{:S(2)}) collective-permute-start(bf16[128,1152]{1,0:T(8,128)(2,1)} %get-tuple-element.52.refs_0_), channel_id=1, source_target_pairs={{0,1},{1,0},{2,3},{3,2},{4,5},{5,4},{6,7},{7,6},{8,9},{9,8},{10,11... | collective-permute-start | bytes 884744 | tf_op jit(solution)/shard_map/ppermute | solution.py:79
  5.6 1.6 %collective-permute-start.1 = (bf16[128,1152]{1,0:T(8,128)(2,1)}, bf16[128,1152]{1,0:T(8,128)(2,1)S(1)}, u32[]{:S(2)}, u32[]{:S(2)}) collective-permute-start(bf16[128,1152]{1,0:T(8,128)(2,1)} %get-tuple-element.52.refs_0_), channel_id=1, source_target_pairs={{0,2},{1,3},{2,0},{3,1},{4,6},{5,7},{6,4},{7,5},{8,10},{9,11},{10,... | collective-permute-start | bytes 884744 | tf_op jit(solution)/shard_map/ppermute | solution.py:75
  7.1 0.7 collective-permute-start.2
  7.8 5.0 %collective-permute-done.refs_6_ = bf16[128,1152]{1,0:T(8,128)(2,1)S(1)} collective-permute-done((bf16[128,1152]{1,0:T(8,128)(2,1)}, bf16[128,1152]{1,0:T(8,128)(2,1)S(1)}, u32[]{:S(2)}, u32[]{:S(2)}) %collective-permute-start) | collective-permute-done | bytes 294944 | tf_op jit(solution)/shard_map/ppermute | solution.py:79
  12.8 1.5 %collective-permute-done.1.refs_1_ = bf16[128,1152]{1,0:T(8,128)(2,1)S(1)} collective-permute-done((bf16[128,1152]{1,0:T(8,128)(2,1)}, bf16[128,1152]{1,0:T(8,128)(2,1)S(1)}, u32[]{:S(2)}, u32[]{:S(2)}) %collective-permute-start.1) | collective-permute-done | bytes 294944 | tf_op jit(solution)/shard_map/ppermute | solution.py:75
  14.7 0.7 collective-permute-start.4
  15.4 1.3 collective-permute-start.5
  16.7 0.7 collective-permute-start.7
  17.4 4.5 %collective-permute-done.3.refs_7_ = bf16[128,1152]{1,0:T(8,128)(2,1)S(1)} collective-permute-done((bf16[128,1152]{1,0:T(8,128)(2,1)S(1)}, bf16[128,1152]{1,0:T(8,128)(2,1)S(1)}, u32[]{:S(2)}, u32[]{:S(2)}) %collective-permute-start.3) | collective-permute-done | bytes 294944 | tf_op jit(solution)/shard_map/ppermute | solution.py:79
  21.9 7.4 %collective-permute-done.5.refs_3_ = bf16[128,1152]{1,0:T(8,128)(2,1)S(1)} collective-permute-done((bf16[128,1152]{1,0:T(8,128)(2,1)S(1)}, bf16[128,1152]{1,0:T(8,128)(2,1)S(1)}, u32[]{:S(2)}, u32[]{:S(2)}) %collective-permute-start.5) | collective-permute-done | bytes 294944 | tf_op jit(solution)/shard_map/ppermute | solution.py:75
  29.3 3.4 %collective-permute-start.8 = (bf16[128,1152]{1,0:T(8,128)(2,1)S(1)}, bf16[128,1152]{1,0:T(8,128)(2,1)S(1)}, u32[]{:S(2)}, u32[]{:S(2)}) collective-permute-start(bf16[128,1152]{1,0:T(8,128)(2,1)S(1)} %collective-permute-done.5.refs_3_), channel_id=1, source_target_pairs={{0,1},{1,0},{6,7},{7,6},{8,9},{9,8},{14,15},{15,14},{16,17},{17,16... | collective-permute-start | bytes 884744 | tf_op jit(solution)/shard_map/ppermute | solution.py:79
  32.6 1.3 collective-permute-start.9
  33.9 0.7 collective-permute-start.6
  34.7 3.2 %collective-permute-done.8.refs_9_ = bf16[128,1152]{1,0:T(8,128)(2,1)S(1)} collective-permute-done((bf16[128,1152]{1,0:T(8,128)(2,1)S(1)}, bf16[128,1152]{1,0:T(8,128)(2,1)S(1)}, u32[]{:S(2)}, u32[]{:S(2)}) %collective-permute-start.8) | collective-permute-done | bytes 294944 | tf_op jit(solution)/shard_map/ppermute | solution.py:79
  37.9 3.4 %collective-permute-done.9.refs_5_ = bf16[128,1152]{1,0:T(8,128)(2,1)S(1)} collective-permute-done((bf16[128,1152]{1,0:T(8,128)(2,1)S(1)}, bf16[128,1152]{1,0:T(8,128)(2,1)S(1)}, u32[]{:S(2)}, u32[]{:S(2)}) %collective-permute-start.9) | collective-permute-done | bytes 294944 | tf_op jit(solution)/shard_map/ppermute | solution.py:75
  41.3 2.4 %collective-permute-start.10 = (bf16[128,1152]{1,0:T(8,128)(2,1)S(1)}, bf16[128,1152]{1,0:T(8,128)(2,1)S(1)}, u32[]{:S(2)}, u32[]{:S(2)}) collective-permute-start(bf16[128,1152]{1,0:T(8,128)(2,1)S(1)} %collective-permute-done.9.refs_5_), channel_id=1, source_target_pairs={{0,1},{1,0},{6,7},{7,6},{8,9},{9,8},{14,15},{15,14},{16,17},{17,16... | collective-permute-start | bytes 884744 | tf_op jit(solution)/shard_map/ppermute | solution.py:79
  43.8 1.4 collective-permute-start.12
  45.2 0.7 stack.51.slots_ref
  45.9 4.5 %collective-permute-done.11.refs_1_ = bf16[128,1024]{1,0:T(8,128)(2,1)S(1)} collective-permute-done((bf16[128,1024]{1,0:T(8,128)(2,1)}, bf16[128,1024]{1,0:T(8,128)(2,1)S(1)}, u32[]{:S(2)}, u32[]{:S(2)}) %collective-permute-start.11) | collective-permute-done | bytes 262176 | tf_op jit(solution)/shard_map/ppermute | solution.py:75
  50.4 1.5 %collective-permute-done.10.refs_11_ = bf16[128,1152]{1,0:T(8,128)(2,1)S(1)} collective-permute-done((bf16[128,1152]{1,0:T(8,128)(2,1)S(1)}, bf16[128,1152]{1,0:T(8,128)(2,1)S(1)}, u32[]{:S(2)}, u32[]{:S(2)}) %collective-permute-start.10) | collective-permute-done | bytes 294944 | tf_op jit(solution)/shard_map/ppermute | solution.py:79
  52.0 0.7 collective-permute-start.14
  52.6 1.3 collective-permute-start.15
  54.0 10.3 %route.2 = (bf16[256,1536]{1,0:T(8,128)(2,1)}, bf16[256,1536]{1,0:T(8,128)(2,1)}, bf16[256,1536]{1,0:T(8,128)(2,1)}, bf16[256,1536]{1,0:T(8,128)(2,1)}, bf16[2,7...) custom-call(s32[12]{0:T(128)} %stack.51.slots_ref, ...), custom_call_target="tpu_custom_call" | custom-call | flops 2818572288 | bytes 6291456 | tf_op jit(solution)/shard_map/route/pallas_call | solution.py:235
  65.0 0.7 collective-permute-start.16
  65.7 1.3 collective-permute-start.19
  67.0 3.8 %collective-permute-start.17 = (bf16[128,1024]{1,0:T(8,128)(2,1)S(1)}, bf16[128,1024]{1,0:T(8,128)(2,1)S(1)}, u32[]{:S(2)}, u32[]{:S(2)}) collective-permute-start(bf16[128,1024]{1,0:T(8,128)(2,1)S(1)} %collective-permute-done.15.refs_3_), channel_id=1, source_target_pairs={{0,1},{1,0},{6,7},{7,6},{8,9},{9,8},{14,15},{15,14},{16,17},{17,16... | collective-permute-start | bytes 786440 | tf_op jit(solution)/shard_map/ppermute | solution.py:79
  70.8 6.3 %collective-permute-start.18 = (bf16[128,1024]{1,0:T(8,128)(2,1)S(1)}, bf16[128,1024]{1,0:T(8,128)(2,1)S(1)}, u32[]{:S(2)}, u32[]{:S(2)}) collective-permute-start(bf16[128,1024]{1,0:T(8,128)(2,1)S(1)} %collective-permute-done.13.refs_6_), channel_id=1, source_target_pairs={{0,2},{1,3},{6,4},{7,5},{8,10},{9,11},{14,12},{15,13},{16,18},{17,... | collective-permute-start | bytes 786440 | tf_op jit(solution)/shard_map/ppermute | solution.py:75
  77.1 1.3 add_convert_fusion.1
  78.5 0.7 collective-permute-start.22
  79.2 3.6 %collective-permute-start.23 = (bf16[128,1024]{1,0:T(8,128)(2,1)S(1)}, bf16[128,1024]{1,0:T(8,128)(2,1)S(1)}, u32[]{:S(2)}, u32[]{:S(2)}) collective-permute-start(bf16[128,1024]{1,0:T(8,128)(2,1)S(1)} %collective-permute-done.11.refs_1_), channel_id=1, source_target_pairs={{0,1},{1,0},{6,7},{7,6},{8,9},{9,8},{14,15},{15,14},{16,17},{17,16... | collective-permute-start | bytes 786440 | tf_op jit(solution)/shard_map/ppermute | solution.py:79
  82.9 1.3 collective-permute-start.24
  84.2 0.6 concatenate.6.slots_ref
  84.9 0.8 fusion.18
  85.6 3.2 %collective-permute-done.23.refs_7_ = bf16[128,1024]{1,0:T(8,128)(2,1)S(1)} collective-permute-done((bf16[128,1024]{1,0:T(8,128)(2,1)S(1)}, bf16[128,1024]{1,0:T(8,128)(2,1)S(1)}, u32[]{:S(2)}, u32[]{:S(2)}) %collective-permute-start.23) | collective-permute-done | bytes 262176 | tf_op jit(solution)/shard_map/ppermute | solution.py:79
  88.8 3.4 %collective-permute-done.24.refs_12_ = bf16[128,1024]{1,0:T(8,128)(2,1)S(1)} collective-permute-done((bf16[128,1024]{1,0:T(8,128)(2,1)S(1)}, bf16[128,1024]{1,0:T(8,128)(2,1)S(1)}, u32[]{:S(2)}, u32[]{:S(2)}) %collective-permute-start.24) | collective-permute-done | bytes 262176 | tf_op jit(solution)/shard_map/ppermute | solution.py:75
  92.3 0.7 copy-done.25
  93.0 6.7 %route.3 = (bf16[256,1536]{1,0:T(8,128)(2,1)}, bf16[256,1536]{1,0:T(8,128)(2,1)}, bf16[2,768,1024]{2,1,0:T(8,128)(2,1)}) custom-call(s32[13]{0:T(128)} %concatenate.6.slots_ref, bf16[128,1024]{1,0:T(8,128)(2,1)} %get-tuple-element.59.refs_0_, bf16[128,1024]{1,0:T(8,128)(2,1)} %copy-done.15, bf16[128,1024]{1,0:T(8,128)(2,1)} %collective-permute-done.12.refs_2_, ...), custom_call_target="tpu_custom_call" | custom-call | flops 2818572288 | bytes 6291456 | tf_op jit(solution)/shard_map/route/pallas_call | solution.py:235
  100.2 1.6 %collective-permute-start.28 = (bf16[256,1536]{1,0:T(8,128)(2,1)S(1)}, bf16[256,1536]{1,0:T(8,128)(2,1)}, u32[]{:S(2)}, u32[]{:S(2)}) collective-permute-start(bf16[256,1536]{1,0:T(8,128)(2,1)S(1)} %add_convert_fusion.1), channel_id=1, source_target_pairs={{0,16},{8,24},{16,0},{24,8},{1,17},{9,25},{17,1},{25,9},{2,18},{10... | collective-permute-start | bytes 2359304 | tf_op jit(solution)/shard_map/ppermute | solution.py:412
  101.8 4.5 %rest.1 = (bf16[256,1536]{1,0:T(8,128)(2,1)}, bf16[256,1536]{1,0:T(8,128)(2,1)}) custom-call(bf16[2,768,1024]{2,1,0:T(8,128)(2,1)} %get-tuple-element.91.refs_1_.routed_ref, bf16[2,768,768]{2,1,0:T(8,128)(2,1)} %get-tuple-element.89.refs_13_.weighted_ref), custom_call_target="tpu_custom_call" | custom-call | flops 1207959552 | bytes 6291456 | tf_op jit(solution)/shard_map/rest/pallas_call | solution.py:265
  107.3 10.0 %back.1 = (bf16[2,8,96,768]{3,2,1,0:T(8,128)(2,1)}, f32[8,2,128]{2,1,0:T(2,128)}) custom-call(bf16[2,768,1024]{2,1,0:T(8,128)(2,1)} %get-tuple-element.75.refs_0_, bf16[2,768,1024]{2,1,0:T(8,128)(2,1)} %get-tuple-element.91.refs_1_.routed_ref, f32[8,8,128]{2,1,0:T(8,128)} %get-tuple-element.90.refs_14_.refs_2_, bf16[2,768,2048]{2,1,0:T(8,128)(2,1)} %refs_3_.1, ...), custom_call_target="tpu_custom_call" | custom-call | flops 4831838208 | bytes 17301504 | tf_op jit(solution)/shard_map/back/pallas_call | solution.py:319
  117.3 4.6 %all-to-all-start = ((f32[8,2,128]{2,1,0:T(2,128)}), f32[8,2,128]{2,1,0:T(2,128)S(1)}, u32[]{:S(2)}, u32[]{:S(2)}) async-start(f32[8,2,128]{2,1,0:T(2,128)} %get-tuple-element.93), calls=%async_computation | async-start | bytes 16384 | tf_op jit(solution)/shard_map/all_to_all | solution.py:467
  121.9 0.9 multiply_convert_fusion.turn_ref
  122.8 5.6 %all-to-all-done = f32[8,2,128]{2,1,0:T(2,128)S(1)} async-done(((f32[8,2,128]{2,1,0:T(2,128)}), f32[8,2,128]{2,1,0:T(2,128)S(1)}, u32[]{:S(2)}, u32[]{:S(2)}) %all-to-all-start) | async-done | bytes 8224 | tf_op jit(solution)/shard_map/all_to_all | solution.py:467
  129.0 3.2 %rotate.2.refs_3_ = f32[512,2,768]{2,1,0:T(2,128)} custom-call(bf16[4,256,256]{2,1,0:T(8,128)(2,1)} %multiply_convert_fusion.turn_ref, bf16[256,1536]{1,0:T(8,128)(2,1)} %get-tuple-element.98.refs_0_, bf16[256,1536]{1,0:T(8,128)(2,1)} %collective-permute-done.21.refs_1_, bf16[256,1536]{1,0:T(8,128)(2,1)} %collective-permute-done.28.refs_2_), custom_call_target="tpu_custom_call" | custom-call | tf_op jit(solution)/shard_map/rotate/pallas_call | solution.py:365
  132.2 4.8 %collective-permute-done.27.refs_2_ = bf16[256,1536]{1,0:T(8,128)(2,1)S(1)} collective-permute-done((bf16[256,1536]{1,0:T(8,128)(2,1)S(1)}, bf16[256,1536]{1,0:T(8,128)(2,1)S(1)}, u32[]{:S(2)}, u32[]{:S(2)}) %collective-permute-start.27) | collective-permute-done | bytes 786464 | tf_op jit(solution)/shard_map/ppermute | solution.py:412
  137.0 0.9 copy-done.1
  137.9 3.2 %rotate.3 = f32[512,2,768]{2,1,0:T(2,128)} custom-call(bf16[4,256,256]{2,1,0:T(8,128)(2,1)} %multiply_convert_fusion.turn_ref, bf16[256,1536]{1,0:T(8,128)(2,1)} %get-tuple-element.94.refs_0_, bf16[256,1536]{1,0:T(8,128)(2,1)} %copy-done, bf16[256,1536]{1,0:T(8,128)(2,1)} %copy-done.1, f32[512,2,768]{2,1,0:T(2,128)} %rotate.2.refs_3_), custom_call_target="tpu_custom_call", output_to_operand_aliasing={{}: (4, {})} | custom-call | tf_op jit(solution)/shard_map/rotate/pallas_call | solution.py:365
  (83 shorter events, 3.3 us)
Async XLA Ops:
  2.6 10.2 %collective-permute-start = (bf16[128,1152]{1,0:T(8,128)(2,1)}, bf16[128,1152]{1,0:T(8,128)(2,1)S(1)}, u32[]{:S(2)}, u32[]{:S(2)}) collective-permute-start(bf16[128,1152]{1,0:T(8,128)(2,1)} %get-tuple-element.52.refs_0_), channel_id=1, source_target_pairs={{0,1},{1,0},{2,3},{3,2},{4,5},{5,4},{6,7},{7,6},{8,9},{9,8},{10,11... | collective-permute-start | bytes 884744 | tf_op jit(solution)/shard_map/ppermute | solution.py:79
  5.6 8.7 %collective-permute-start.1 = (bf16[128,1152]{1,0:T(8,128)(2,1)}, bf16[128,1152]{1,0:T(8,128)(2,1)S(1)}, u32[]{:S(2)}, u32[]{:S(2)}) collective-permute-start(bf16[128,1152]{1,0:T(8,128)(2,1)} %get-tuple-element.52.refs_0_), channel_id=1, source_target_pairs={{0,2},{1,3},{2,0},{3,1},{4,6},{5,7},{6,4},{7,5},{8,10},{9,11},{10,... | collective-permute-start | bytes 884744 | tf_op jit(solution)/shard_map/ppermute | solution.py:75
  7.1 7.1 %collective-permute-start.2 = (bf16[128,1152]{1,0:T(8,128)(2,1)}, bf16[128,1152]{1,0:T(8,128)(2,1)S(1)}, u32[]{:S(2)}, u32[]{:S(2)}) collective-permute-start(bf16[128,1152]{1,0:T(8,128)(2,1)} %get-tuple-element.52.refs_0_), channel_id=1, source_target_pairs={{2,4},{3,5},{4,2},{5,3},{10,12},{11,13},{12,10},{13,11},{18,20},{1... | collective-permute-start | bytes 884744 | tf_op jit(solution)/shard_map/ppermute | solution.py:75
  12.8 41.2 %copy-start.4 = (bf16[128,1152]{1,0:T(8,128)(2,1)}, bf16[128,1152]{1,0:T(8,128)(2,1)S(1)}, u32[]{:S(2)}) copy-start(bf16[128,1152]{1,0:T(8,128)(2,1)S(1)} %collective-permute-done.refs_6_) | copy-start | bytes 884740
  14.2 39.7 %copy-start.5 = (bf16[128,1152]{1,0:T(8,128)(2,1)}, bf16[128,1152]{1,0:T(8,128)(2,1)S(1)}, u32[]{:S(2)}) copy-start(bf16[128,1152]{1,0:T(8,128)(2,1)S(1)} %collective-permute-done.1.refs_1_) | copy-start | bytes 884740
  14.2 39.7 %copy-start.6 = (bf16[128,1152]{1,0:T(8,128)(2,1)}, bf16[128,1152]{1,0:T(8,128)(2,1)S(1)}, u32[]{:S(2)}) copy-start(bf16[128,1152]{1,0:T(8,128)(2,1)S(1)} %collective-permute-done.2.refs_2_) | copy-start | bytes 884740
  14.2 7.6 %collective-permute-start.3 = (bf16[128,1152]{1,0:T(8,128)(2,1)S(1)}, bf16[128,1152]{1,0:T(8,128)(2,1)S(1)}, u32[]{:S(2)}, u32[]{:S(2)}) collective-permute-start(bf16[128,1152]{1,0:T(8,128)(2,1)S(1)} %collective-permute-done.1.refs_1_), channel_id=1, source_target_pairs={{0,1},{1,0},{2,3},{3,2},{4,5},{5,4},{6,7},{7,6},{8,9},{9,8},{10,11... | collective-permute-start | bytes 884744 | tf_op jit(solution)/shard_map/ppermute | solution.py:79
  14.7 7.2 %collective-permute-start.4 = (bf16[128,1152]{1,0:T(8,128)(2,1)S(1)}, bf16[128,1152]{1,0:T(8,128)(2,1)S(1)}, u32[]{:S(2)}, u32[]{:S(2)}) collective-permute-start(bf16[128,1152]{1,0:T(8,128)(2,1)S(1)} %collective-permute-done.1.refs_1_), channel_id=1, source_target_pairs={{2,4},{3,5},{4,2},{5,3},{10,12},{11,13},{12,10},{13,11},{18,20},{1... | collective-permute-start | bytes 884744 | tf_op jit(solution)/shard_map/ppermute | solution.py:75
  15.4 13.9 %collective-permute-start.5 = (bf16[128,1152]{1,0:T(8,128)(2,1)S(1)}, bf16[128,1152]{1,0:T(8,128)(2,1)S(1)}, u32[]{:S(2)}, u32[]{:S(2)}) collective-permute-start(bf16[128,1152]{1,0:T(8,128)(2,1)S(1)} %collective-permute-done.2.refs_2_), channel_id=1, source_target_pairs={{2,0},{3,1},{4,6},{5,7},{10,8},{11,9},{12,14},{13,15},{18,16},{19,... | collective-permute-start | bytes 884744 | tf_op jit(solution)/shard_map/ppermute | solution.py:75
  16.7 18.0 %collective-permute-start.7 = (bf16[128,1152]{1,0:T(8,128)(2,1)S(1)}, bf16[128,1152]{1,0:T(8,128)(2,1)S(1)}, u32[]{:S(2)}, u32[]{:S(2)}) collective-permute-start(bf16[128,1152]{1,0:T(8,128)(2,1)S(1)} %collective-permute-done.2.refs_2_), channel_id=1, source_target_pairs={{2,3},{3,2},{4,5},{5,4},{10,11},{11,10},{12,13},{13,12},{18,19},{1... | collective-permute-start | bytes 884744 | tf_op jit(solution)/shard_map/ppermute | solution.py:79
  21.9 32.1 %copy-start.7 = (bf16[128,1152]{1,0:T(8,128)(2,1)}, bf16[128,1152]{1,0:T(8,128)(2,1)S(1)}, u32[]{:S(2)}) copy-start(bf16[128,1152]{1,0:T(8,128)(2,1)S(1)} %collective-permute-done.3.refs_7_) | copy-start | bytes 884740
  21.9 32.1 %copy-start.8 = (bf16[128,1152]{1,0:T(8,128)(2,1)}, bf16[128,1152]{1,0:T(8,128)(2,1)S(1)}, u32[]{:S(2)}) copy-start(bf16[128,1152]{1,0:T(8,128)(2,1)S(1)} %collective-permute-done.4.refs_4_) | copy-start | bytes 884740
  29.2 24.7 %copy-start.9 = (bf16[128,1152]{1,0:T(8,128)(2,1)}, bf16[128,1152]{1,0:T(8,128)(2,1)S(1)}, u32[]{:S(2)}) copy-start(bf16[128,1152]{1,0:T(8,128)(2,1)S(1)} %collective-permute-done.5.refs_3_) | copy-start | bytes 884740
  29.3 8.6 %collective-permute-start.8 = (bf16[128,1152]{1,0:T(8,128)(2,1)S(1)}, bf16[128,1152]{1,0:T(8,128)(2,1)S(1)}, u32[]{:S(2)}, u32[]{:S(2)}) collective-permute-start(bf16[128,1152]{1,0:T(8,128)(2,1)S(1)} %collective-permute-done.5.refs_3_), channel_id=1, source_target_pairs={{0,1},{1,0},{6,7},{7,6},{8,9},{9,8},{14,15},{15,14},{16,17},{17,16... | collective-permute-start | bytes 884744 | tf_op jit(solution)/shard_map/ppermute | solution.py:79
  32.6 8.6 %collective-permute-start.9 = (bf16[128,1152]{1,0:T(8,128)(2,1)S(1)}, bf16[128,1152]{1,0:T(8,128)(2,1)S(1)}, u32[]{:S(2)}, u32[]{:S(2)}) collective-permute-start(bf16[128,1152]{1,0:T(8,128)(2,1)S(1)} %collective-permute-done.4.refs_4_), channel_id=1, source_target_pairs={{2,0},{3,1},{4,6},{5,7},{10,8},{11,9},{12,14},{13,15},{18,16},{19,... | collective-permute-start | bytes 884744 | tf_op jit(solution)/shard_map/ppermute | solution.py:75
  33.9 16.4 %collective-permute-start.6 = (bf16[128,1152]{1,0:T(8,128)(2,1)S(1)}, bf16[128,1152]{1,0:T(8,128)(2,1)S(1)}, u32[]{:S(2)}, u32[]{:S(2)}) collective-permute-start(bf16[128,1152]{1,0:T(8,128)(2,1)S(1)} %collective-permute-done.4.refs_4_), channel_id=1, source_target_pairs={{2,3},{3,2},{4,5},{5,4},{10,11},{11,10},{12,13},{13,12},{18,19},{1... | collective-permute-start | bytes 884744 | tf_op jit(solution)/shard_map/ppermute | solution.py:79
  34.6 19.3 %copy-start.10 = (bf16[128,1152]{1,0:T(8,128)(2,1)}, bf16[128,1152]{1,0:T(8,128)(2,1)S(1)}, u32[]{:S(2)}) copy-start(bf16[128,1152]{1,0:T(8,128)(2,1)S(1)} %collective-permute-done.7.refs_8_) | copy-start | bytes 884740
  37.9 16.1 %copy-start.11 = (bf16[128,1152]{1,0:T(8,128)(2,1)}, bf16[128,1152]{1,0:T(8,128)(2,1)S(1)}, u32[]{:S(2)}) copy-start(bf16[128,1152]{1,0:T(8,128)(2,1)S(1)} %collective-permute-done.8.refs_9_) | copy-start | bytes 884740
  41.3 12.7 %copy-start.12 = (bf16[128,1152]{1,0:T(8,128)(2,1)}, bf16[128,1152]{1,0:T(8,128)(2,1)S(1)}, u32[]{:S(2)}) copy-start(bf16[128,1152]{1,0:T(8,128)(2,1)S(1)} %collective-permute-done.9.refs_5_) | copy-start | bytes 884740
  41.3 10.6 %collective-permute-start.10 = (bf16[128,1152]{1,0:T(8,128)(2,1)S(1)}, bf16[128,1152]{1,0:T(8,128)(2,1)S(1)}, u32[]{:S(2)}, u32[]{:S(2)}) collective-permute-start(bf16[128,1152]{1,0:T(8,128)(2,1)S(1)} %collective-permute-done.9.refs_5_), channel_id=1, source_target_pairs={{0,1},{1,0},{6,7},{7,6},{8,9},{9,8},{14,15},{15,14},{16,17},{17,16... | collective-permute-start | bytes 884744 | tf_op jit(solution)/shard_map/ppermute | solution.py:79
  43.7 6.6 %collective-permute-start.11 = (bf16[128,1024]{1,0:T(8,128)(2,1)}, bf16[128,1024]{1,0:T(8,128)(2,1)S(1)}, u32[]{:S(2)}, u32[]{:S(2)}) collective-permute-start(bf16[128,1024]{1,0:T(8,128)(2,1)} %get-tuple-element.59.refs_0_), channel_id=1, source_target_pairs={{0,2},{1,3},{2,0},{3,1},{4,6},{5,7},{6,4},{7,5},{8,10},{9,11},{10,... | collective-permute-start | bytes 786440 | tf_op jit(solution)/shard_map/ppermute | solution.py:75
  43.8 6.6 %collective-permute-start.12 = (bf16[128,1024]{1,0:T(8,128)(2,1)}, bf16[128,1024]{1,0:T(8,128)(2,1)}, u32[]{:S(2)}, u32[]{:S(2)}) collective-permute-start(bf16[128,1024]{1,0:T(8,128)(2,1)} %get-tuple-element.59.refs_0_), channel_id=1, source_target_pairs={{2,4},{3,5},{4,2},{5,3},{10,12},{11,13},{12,10},{13,11},{18,20},{1... | collective-permute-start | bytes 786440 | tf_op jit(solution)/shard_map/ppermute | solution.py:75
  50.4 41.9 %copy-start.15 = (bf16[128,1024]{1,0:T(8,128)(2,1)}, bf16[128,1024]{1,0:T(8,128)(2,1)S(1)}, u32[]{:S(2)}) copy-start(bf16[128,1024]{1,0:T(8,128)(2,1)S(1)} %collective-permute-done.11.refs_1_) | copy-start | bytes 786436
  51.9 12.4 %collective-permute-start.13 = (bf16[128,1024]{1,0:T(8,128)(2,1)}, bf16[128,1024]{1,0:T(8,128)(2,1)S(1)}, u32[]{:S(2)}, u32[]{:S(2)}) collective-permute-start(bf16[128,1024]{1,0:T(8,128)(2,1)} %get-tuple-element.59.refs_0_), channel_id=1, source_target_pairs={{0,1},{1,0},{2,3},{3,2},{4,5},{5,4},{6,7},{7,6},{8,9},{9,8},{10,11... | collective-permute-start | bytes 786440 | tf_op jit(solution)/shard_map/ppermute | solution.py:79
  52.0 12.4 %collective-permute-start.14 = (bf16[128,1024]{1,0:T(8,128)(2,1)S(1)}, bf16[128,1024]{1,0:T(8,128)(2,1)S(1)}, u32[]{:S(2)}, u32[]{:S(2)}) collective-permute-start(bf16[128,1024]{1,0:T(8,128)(2,1)S(1)} %collective-permute-done.11.refs_1_), channel_id=1, source_target_pairs={{2,4},{3,5},{4,2},{5,3},{10,12},{11,13},{12,10},{13,11},{18,20},{1... | collective-permute-start | bytes 786440 | tf_op jit(solution)/shard_map/ppermute | solution.py:75
  52.6 11.9 %collective-permute-start.15 = (bf16[128,1024]{1,0:T(8,128)(2,1)}, bf16[128,1024]{1,0:T(8,128)(2,1)S(1)}, u32[]{:S(2)}, u32[]{:S(2)}) collective-permute-start(bf16[128,1024]{1,0:T(8,128)(2,1)} %collective-permute-done.12.refs_2_), channel_id=1, source_target_pairs={{2,0},{3,1},{4,6},{5,7},{10,8},{11,9},{12,14},{13,15},{18,16},{19,... | collective-permute-start | bytes 786440 | tf_op jit(solution)/shard_map/ppermute | solution.py:75
  64.3 14.9 %copy-start.16 = (bf16[128,1024]{1,0:T(8,128)(2,1)}, bf16[128,1024]{1,0:T(8,128)(2,1)S(1)}, u32[]{:S(2)}) copy-start(bf16[128,1024]{1,0:T(8,128)(2,1)S(1)} %collective-permute-done.13.refs_6_) | copy-start | bytes 786436
  64.3 18.5 %copy-start.17 = (bf16[128,1024]{1,0:T(8,128)(2,1)}, bf16[128,1024]{1,0:T(8,128)(2,1)S(1)}, u32[]{:S(2)}) copy-start(bf16[128,1024]{1,0:T(8,128)(2,1)S(1)} %collective-permute-done.14.refs_4_) | copy-start | bytes 786436
  64.5 18.4 %copy-start.18 = (bf16[128,1024]{1,0:T(8,128)(2,1)}, bf16[128,1024]{1,0:T(8,128)(2,1)S(1)}, u32[]{:S(2)}) copy-start(bf16[128,1024]{1,0:T(8,128)(2,1)S(1)} %collective-permute-done.15.refs_3_) | copy-start | bytes 786436
  64.5 6.3 %collective-permute-start.20 = (bf16[256,1536]{1,0:T(8,128)(2,1)}, bf16[256,1536]{1,0:T(8,128)(2,1)S(1)}, u32[]{:S(2)}, u32[]{:S(2)}) collective-permute-start(bf16[256,1536]{1,0:T(8,128)(2,1)} %get-tuple-element.79), channel_id=1, source_target_pairs={{0,8},{8,0},{16,24},{24,16},{1,9},{9,1},{17,25},{25,17},{2,10},{10... | collective-permute-start | bytes 2359304 | tf_op jit(solution)/shard_map/ppermute | solution.py:406
  64.5 18.4 %collective-permute-start.21 = (bf16[256,1536]{1,0:T(8,128)(2,1)}, bf16[256,1536]{1,0:T(8,128)(2,1)}, u32[]{:S(2)}, u32[]{:S(2)}) collective-permute-start(bf16[256,1536]{1,0:T(8,128)(2,1)} %get-tuple-element.81), channel_id=1, source_target_pairs={{0,8},{8,0},{16,24},{24,16},{1,9},{9,1},{17,25},{25,17},{2,10},{10... | collective-permute-start | bytes 2359304 | tf_op jit(solution)/shard_map/ppermute | solution.py:406
  65.0 13.5 %collective-permute-start.16 = (bf16[128,1024]{1,0:T(8,128)(2,1)S(1)}, bf16[128,1024]{1,0:T(8,128)(2,1)S(1)}, u32[]{:S(2)}, u32[]{:S(2)}) collective-permute-start(bf16[128,1024]{1,0:T(8,128)(2,1)S(1)} %collective-permute-done.14.refs_4_), channel_id=1, source_target_pairs={{2,3},{3,2},{4,5},{5,4},{10,11},{11,10},{12,13},{13,12},{18,19},{1... | collective-permute-start | bytes 786440 | tf_op jit(solution)/shard_map/ppermute | solution.py:79
  65.7 17.2 %collective-permute-start.19 = (bf16[128,1024]{1,0:T(8,128)(2,1)S(1)}, bf16[128,1024]{1,0:T(8,128)(2,1)S(1)}, u32[]{:S(2)}, u32[]{:S(2)}) collective-permute-start(bf16[128,1024]{1,0:T(8,128)(2,1)S(1)} %collective-permute-done.14.refs_4_), channel_id=1, source_target_pairs={{2,0},{3,1},{4,6},{5,7},{10,8},{11,9},{12,14},{13,15},{18,16},{19,... | collective-permute-start | bytes 786440 | tf_op jit(solution)/shard_map/ppermute | solution.py:75
  67.0 12.2 %collective-permute-start.17 = (bf16[128,1024]{1,0:T(8,128)(2,1)S(1)}, bf16[128,1024]{1,0:T(8,128)(2,1)S(1)}, u32[]{:S(2)}, u32[]{:S(2)}) collective-permute-start(bf16[128,1024]{1,0:T(8,128)(2,1)S(1)} %collective-permute-done.15.refs_3_), channel_id=1, source_target_pairs={{0,1},{1,0},{6,7},{7,6},{8,9},{9,8},{14,15},{15,14},{16,17},{17,16... | collective-permute-start | bytes 786440 | tf_op jit(solution)/shard_map/ppermute | solution.py:79
  70.8 12.0 %collective-permute-start.18 = (bf16[128,1024]{1,0:T(8,128)(2,1)S(1)}, bf16[128,1024]{1,0:T(8,128)(2,1)S(1)}, u32[]{:S(2)}, u32[]{:S(2)}) collective-permute-start(bf16[128,1024]{1,0:T(8,128)(2,1)S(1)} %collective-permute-done.13.refs_6_), channel_id=1, source_target_pairs={{0,2},{1,3},{6,4},{7,5},{8,10},{9,11},{14,12},{15,13},{16,18},{17,... | collective-permute-start | bytes 786440 | tf_op jit(solution)/shard_map/ppermute | solution.py:75
  78.5 13.8 %copy-start.19 = (bf16[128,1024]{1,0:T(8,128)(2,1)}, bf16[128,1024]{1,0:T(8,128)(2,1)S(1)}, u32[]{:S(2)}) copy-start(bf16[128,1024]{1,0:T(8,128)(2,1)S(1)} %collective-permute-done.16.refs_11_) | copy-start | bytes 786436
  78.5 7.1 %collective-permute-start.22 = (bf16[128,1024]{1,0:T(8,128)(2,1)}, bf16[128,1024]{1,0:T(8,128)(2,1)S(1)}, u32[]{:S(2)}, u32[]{:S(2)}) collective-permute-start(bf16[128,1024]{1,0:T(8,128)(2,1)} %collective-permute-done.12.refs_2_), channel_id=1, source_target_pairs={{2,3},{3,2},{4,5},{5,4},{10,11},{11,10},{12,13},{13,12},{18,19},{1... | collective-permute-start | bytes 786440 | tf_op jit(solution)/shard_map/ppermute | solution.py:79
  79.2 13.1 %copy-start.21 = (bf16[128,1024]{1,0:T(8,128)(2,1)}, bf16[128,1024]{1,0:T(8,128)(2,1)S(1)}, u32[]{:S(2)}) copy-start(bf16[128,1024]{1,0:T(8,128)(2,1)S(1)} %collective-permute-done.17.refs_10_) | copy-start | bytes 786436
  79.2 9.6 %collective-permute-start.23 = (bf16[128,1024]{1,0:T(8,128)(2,1)S(1)}, bf16[128,1024]{1,0:T(8,128)(2,1)S(1)}, u32[]{:S(2)}, u32[]{:S(2)}) collective-permute-start(bf16[128,1024]{1,0:T(8,128)(2,1)S(1)} %collective-permute-done.11.refs_1_), channel_id=1, source_target_pairs={{0,1},{1,0},{6,7},{7,6},{8,9},{9,8},{14,15},{15,14},{16,17},{17,16... | collective-permute-start | bytes 786440 | tf_op jit(solution)/shard_map/ppermute | solution.py:79
  82.9 9.4 %copy-start.22 = (bf16[128,1024]{1,0:T(8,128)(2,1)}, bf16[128,1024]{1,0:T(8,128)(2,1)S(1)}, u32[]{:S(2)}) copy-start(bf16[128,1024]{1,0:T(8,128)(2,1)S(1)} %collective-permute-done.18.refs_8_) | copy-start | bytes 786436
  82.9 9.4 %copy-start.20 = (bf16[128,1024]{1,0:T(8,128)(2,1)}, bf16[128,1024]{1,0:T(8,128)(2,1)S(1)}, u32[]{:S(2)}) copy-start(bf16[128,1024]{1,0:T(8,128)(2,1)S(1)} %collective-permute-done.19.refs_5_) | copy-start | bytes 786436
  82.9 9.3 %collective-permute-start.24 = (bf16[128,1024]{1,0:T(8,128)(2,1)S(1)}, bf16[128,1024]{1,0:T(8,128)(2,1)S(1)}, u32[]{:S(2)}, u32[]{:S(2)}) collective-permute-start(bf16[128,1024]{1,0:T(8,128)(2,1)S(1)} %collective-permute-done.16.refs_11_), channel_id=1, source_target_pairs={{2,0},{3,1},{4,6},{5,7},{10,8},{11,9},{12,14},{13,15},{18,16},{19,... | collective-permute-start | bytes 786440 | tf_op jit(solution)/shard_map/ppermute | solution.py:75
  99.8 6.7 %collective-permute-start.26 = (bf16[256,1536]{1,0:T(8,128)(2,1)}, bf16[256,1536]{1,0:T(8,128)(2,1)S(1)}, u32[]{:S(2)}, u32[]{:S(2)}) collective-permute-start(bf16[256,1536]{1,0:T(8,128)(2,1)} %get-tuple-element.96), channel_id=1, source_target_pairs={{0,8},{8,0},{16,24},{24,16},{1,9},{9,1},{17,25},{25,17},{2,10},{10... | collective-permute-start | bytes 2359304 | tf_op jit(solution)/shard_map/ppermute | solution.py:406
  100.2 28.8 %collective-permute-start.28 = (bf16[256,1536]{1,0:T(8,128)(2,1)S(1)}, bf16[256,1536]{1,0:T(8,128)(2,1)}, u32[]{:S(2)}, u32[]{:S(2)}) collective-permute-start(bf16[256,1536]{1,0:T(8,128)(2,1)S(1)} %add_convert_fusion.1), channel_id=1, source_target_pairs={{0,16},{8,24},{16,0},{24,8},{1,17},{9,25},{17,1},{25,9},{2,18},{10... | collective-permute-start | bytes 2359304 | tf_op jit(solution)/shard_map/ppermute | solution.py:412
  106.3 25.9 %collective-permute-start.25 = (bf16[256,1536]{1,0:T(8,128)(2,1)}, bf16[256,1536]{1,0:T(8,128)(2,1)S(1)}, u32[]{:S(2)}, u32[]{:S(2)}) collective-permute-start(bf16[256,1536]{1,0:T(8,128)(2,1)} %get-tuple-element.95), channel_id=1, source_target_pairs={{0,8},{8,0},{16,24},{24,16},{1,9},{9,1},{17,25},{25,17},{2,10},{10... | collective-permute-start | bytes 2359304 | tf_op jit(solution)/shard_map/ppermute | solution.py:406
  106.7 21.7 %copy-start.3 = (s32[128,8]{0,1:T(8,128)S(1)}, s32[128,8]{0,1:T(8,128)}, u32[]{:S(2)}) copy-start(s32[128,8]{0,1:T(8,128)} %param.8) | copy-start | bytes 12292
  106.7 30.3 %collective-permute-start.27 = (bf16[256,1536]{1,0:T(8,128)(2,1)S(1)}, bf16[256,1536]{1,0:T(8,128)(2,1)S(1)}, u32[]{:S(2)}, u32[]{:S(2)}) collective-permute-start(bf16[256,1536]{1,0:T(8,128)(2,1)S(1)} %add_convert_fusion), channel_id=1, source_target_pairs={{0,16},{8,24},{16,0},{24,8},{1,17},{9,25},{17,1},{25,9},{2,18},{10... | collective-permute-start | bytes 2359304 | tf_op jit(solution)/shard_map/ppermute | solution.py:412
  117.3 11.1 %all-to-all-start = ((f32[8,2,128]{2,1,0:T(2,128)}), f32[8,2,128]{2,1,0:T(2,128)S(1)}, u32[]{:S(2)}, u32[]{:S(2)}) async-start(f32[8,2,128]{2,1,0:T(2,128)} %get-tuple-element.93), calls=%async_computation | async-start | bytes 16384 | tf_op jit(solution)/shard_map/all_to_all | solution.py:467
  (8 other events, 27.0 us)

commit v2 on v1

--- a/solution.py
+++ b/solution.py
@@ -67,16 +67,16 @@
     )(cotangent, gate_prob.T, routes.T)
 
 
-EDGE, MIDDLE = ((0, 1), (1, 0), (2, 3), (3, 2)), ((1, 2), (2, 1))
-OUTWARD, INWARD = ((1, 0), (2, 3)), ((0, 1), (3, 2))
-
-
-def along(value, pairs):
+LINES = 4
+
+
+def along(value, by):
+    pairs = [(line, (line + by) % LINES) for line in range(LINES)]
     return lax.ppermute(value, "expert", [(2 * a + x, 2 * b + x) for a, b in pairs for x in (0, 1)])
 
 
-def across(value, rows):
-    return lax.ppermute(value, "expert", [(2 * a + x, 2 * a + 1 - x) for a in rows for x in (0, 1)])
+def across(value):
+    return lax.ppermute(value, "expert", [(i, i ^ 1) for i in range(2 * LINES)])
 
 
 def fence(*values):
@@ -86,15 +86,8 @@
 def line_slots():
     place = lax.axis_index("expert")
     line, side = place // 2, place % 2
-    middle = (line == 1) | (line == 2)
-    near = line ^ 1
-    far = jnp.where(middle, 3 - line, 3 - near)
-    last = far ^ 1
-    lines = [line, near, far, far, last, last]
-    valid = [True, True, middle, ~middle, middle, ~middle]
-    same = [jnp.where(ok, 2 * at + side, -1) for at, ok in zip(lines, valid)]
-    other = [jnp.where(ok, 2 * at + 1 - side, -1) for at, ok in zip(lines, valid)]
-    return jnp.stack(same + other).astype(jnp.int32)
+    lines = [line, (line + LINES - 1) % LINES, (line + 1) % LINES, (line + 2) % LINES]
+    return jnp.stack([2 * at + side for at in lines] + [2 * at + 1 - side for at in lines]).astype(jnp.int32)
 
 
 def load_parts(slots_ref, refs, tokens, dst_ref, sem):
@@ -245,55 +238,24 @@
             pltpu.SemaphoreType.DMA,
         ],
         compiler_params=params(),
-        cost_estimate=pl.CostEstimate(
-            flops=2 * slot_rows * experts_here * columns * (tokens + units),
-            bytes_accessed=4 * slot_rows * experts_here * columns,
-            transcendentals=0,
-        ),
         name="route",
     )(slots, *parts, *operands)
 
 
-def rest_kernel(bands, width, groups, routed_ref, weighted_ref, *outs):
-    grad_bands(routed_ref.at[0], weighted_ref, outs, bands, width, groups)
-
-
-def rest(routed, weighted, bands, width, groups):
-    experts_here, slot_rows, columns = routed.shape
-    units = weighted.shape[2]
-    band_specs, band_shapes = band_outputs(bands, width, experts_here, units)
-    return pl.pallas_call(
-        functools.partial(rest_kernel, bands, width, groups),
-        grid=(experts_here,),
-        in_specs=[
-            pl.BlockSpec((1, slot_rows, columns), lambda e: (e, 0, 0)),
-            pl.BlockSpec((1, slot_rows, units), lambda e: (e, 0, 0)),
-        ],
-        out_specs=band_specs,
-        out_shape=band_shapes,
-        compiler_params=params(),
-        cost_estimate=pl.CostEstimate(
-            flops=slot_rows * experts_here * columns * units,
-            bytes_accessed=4 * slot_rows * experts_here * columns,
-            transcendentals=0,
-        ),
-        name="rest",
-    )(routed, weighted)
-
-
-def back_kernel(pieces, replicas, *refs):
-    routed, refs = refs[: len(pieces)], refs[len(pieces) :]
-    table_ref, weight_ref, hidden_ref, grad_ref, prob_ref, held = refs
+def back_kernel(replicas, last, *refs):
+    routed_ref, weight_refs, refs = refs[0], refs[1 : 1 + replicas], refs[1 + replicas :]
+    weight = jnp.concatenate([ref[0] for ref in weight_refs], axis=1)
+    made = dot(routed_ref[0], weight, ((1,), (1,)))
+    if not last:
+        refs[0][0] = made.astype(BF16)
+        return
+    before_ref, table_ref, hidden_ref, grad_ref, prob_ref, held = refs
     expert = pl.program_id(0)
     experts_here = pl.num_programs(0)
     _, sources, cap, units = hidden_ref.shape
     tokens = table_ref.shape[2]
     cap_rows = held.shape[0] // sources
-    columns = []
-    for q in range(replicas):
-        for ref, (_, width) in zip(routed, pieces):
-            columns.append(ref[0, :, q * width : (q + 1) * width])
-    held[...] = dot(jnp.concatenate(columns, axis=1), weight_ref[0], ((1,), (1,)))
+    held[...] = made + before_ref[0].astype(F32)
 
     def finish(s, carry):
         mine = held[pl.ds(pl.multiple_of(s * cap_rows, cap_rows), cap), :]
@@ -311,37 +273,41 @@
     lax.fori_loop(0, sources, finish, 0, unroll=sources <= 8)
 
 
-def back(routed, table, weight, hidden, pieces, replicas):
-    experts_here, sources, cap, units = hidden.shape
-    features = weight.shape[2]
-    tokens = table.shape[2]
-    slot_rows = routed[0].shape[1]
-    return pl.pallas_call(
-        functools.partial(back_kernel, pieces, replicas),
-        grid=(experts_here,),
-        in_specs=[pl.BlockSpec((1,) + part.shape[1:], lambda e: (e, 0, 0)) for part in routed]
-        + [
-            pl.BlockSpec(table.shape, lambda e: (0, 0, 0)),
-            pl.BlockSpec((1, units, features), lambda e: (e, 0, 0)),
-            pl.BlockSpec((1, sources, cap, units), lambda e: (e, 0, 0, 0)),
-        ],
-        out_specs=[
-            pl.BlockSpec((1, sources, cap, units), lambda e: (e, 0, 0, 0)),
-            pl.BlockSpec((sources, experts_here, tokens), lambda e: (0, 0, 0)),
-        ],
-        out_shape=[
+def back(routed, weight, start, replicas, before=None, table=None, hidden=None):
+    experts_here, slot_rows, columns = routed.shape
+    units, features = weight.shape[1:]
+    width, rows_own = columns // replicas, features // replicas
+    last = before is not None
+    product = pl.BlockSpec((1, slot_rows, units), lambda e: (e, 0, 0))
+
+    def share(q):
+        return pl.BlockSpec((1, units, width), lambda e: (e, 0, (q * rows_own + start) // width))
+
+    operands = [routed] + [weight] * replicas
+    in_specs = [pl.BlockSpec((1, slot_rows, columns), lambda e: (e, 0, 0))] + [share(q) for q in range(replicas)]
+    if last:
+        sources, cap = hidden.shape[1:3]
+        tokens = table.shape[2]
+        saved = pl.BlockSpec((1, sources, cap, units), lambda e: (e, 0, 0, 0))
+        operands += [before, table, hidden]
+        in_specs += [product, pl.BlockSpec(table.shape, lambda e: (0, 0, 0)), saved]
+        out_specs = [saved, pl.BlockSpec((sources, experts_here, tokens), lambda e: (0, 0, 0))]
+        out_shape = [
             jax.ShapeDtypeStruct(hidden.shape, BF16),
             jax.ShapeDtypeStruct((sources, experts_here, tokens), F32),
-        ],
-        scratch_shapes=[pltpu.VMEM((slot_rows, units), F32)],
+        ]
+    else:
+        out_specs, out_shape = product, jax.ShapeDtypeStruct((experts_here, slot_rows, units), BF16)
+    return pl.pallas_call(
+        functools.partial(back_kernel, replicas, last),
+        grid=(experts_here,),
+        in_specs=in_specs,
+        out_specs=out_specs,
+        out_shape=out_shape,
+        scratch_shapes=[pltpu.VMEM((slot_rows, units), F32)] if last else [],
         compiler_params=params(),
-        cost_estimate=pl.CostEstimate(
-            flops=2 * experts_here * slot_rows * features * units,
-            bytes_accessed=2 * (weight.size + 2 * hidden.size + experts_here * slot_rows * features),
-            transcendentals=0,
-        ),
         name="back",
-    )(*routed, table, weight, hidden)
+    )(*operands)
 
 
 def rotate_kernel(count, experts_here, turn_ref, *refs):
@@ -415,62 +381,52 @@
     def add(a, b):
         return (a.astype(F32) + b.astype(F32)).astype(BF16)
 
+    bands = away_bands + here_bands
+
     def route_first(parts, slots):
-        return route(parts, slots, width, away_bands + here_bands, groups, tokens, hidden=saved)
-
-    if sources == 8:
+        return route(parts, slots, width, bands, groups, tokens, hidden=saved)
+
+    if sources == 2 * LINES:
         a, b = sent
         slots = line_slots()
-        a_x0, a_s1, a_s2 = fence(across(a, range(4)), along(a, EDGE), along(a, MIDDLE))
-        a_x1, a_s3, a_s4 = fence(across(a_s1, range(4)), along(a_s1, MIDDLE), along(a_s2, OUTWARD))
-        a_x2, a_x4, a_s5 = fence(across(a_s2, (1, 2)), across(a_s4, (0, 3)), along(a_s3, OUTWARD))
-        a_x3, a_x5, b, b_s1, b_s2 = fence(
-            across(a_s3, (1, 2)), across(a_s5, (0, 3)), b, along(b, EDGE), along(b, MIDDLE)
-        )
-        a_parts = [a, a_s1, a_s2, a_s4, a_s3, a_s5, a_x0, a_x1, a_x2, a_x4, a_x3, a_x5]
-        made = route_first(a_parts, slots)
-        b_x0, b_s3, b_s4, *made = fence(across(b, range(4)), along(b_s1, MIDDLE), along(b_s2, OUTWARD), *made)
+        a_x, b_x, a_next, a_prev, a, b = fence(across(a), across(b), along(a, 1), along(a, -1), a, b)
+        a_opp, a_xnext, a_xprev, b = fence(along(a, 2), across(a_next), across(a_prev), b)
+        a_xopp, b_next, b_prev, b = fence(across(a_opp), along(b, 1), along(b, -1), b)
+        b_opp, b_xnext, b_xprev = along(b, 2), across(b_next), across(b_prev)
+        made = route_first([a, a_next, a_prev, a_opp, a_x, a_xnext, a_xprev, a_xopp], slots)
+        b_opp, b_xnext, b_xprev, *made = fence(b_opp, b_xnext, b_xprev, *made)
+        b_xopp = across(b_opp)
         away_send, away_keep, here_send, here_keep, routed_a, weighted, table = made
-        away_got, here_got = swap(away_send), swap(here_send)
-        away_sum = add(away_got, away_keep)
-        b_x3, b_x4, b_w, b_s5, away_sum, here_got = fence(
-            across(b_s3, (1, 2)), across(b_s4, (0, 3)), along(b_x0, INWARD), along(b_s3, OUTWARD), away_sum, here_got
-        )
-        final_a = [here_keep, here_got] + to_chips(away_sum)
-        b_x2, b_x1, b_w5 = fence(across(b_s2, (1, 2)), across(b_s1, (0, 3)), along(b_x3, OUTWARD))
-        b_parts = [b, b_s1, b_s2, b_s4, b_s3, b_s5, b_x0, b_x1, b_w, b_x2, b_x4, b_x3, b_w5]
-        middle = (slots[2] >= 0)
-        b_slots = jnp.concatenate(
-            [
-                slots[:7],
-                jnp.where(middle, -1, slots[7:8]),
-                jnp.where(middle, slots[7:8], -1),
-                slots[8:],
-            ]
-        )
+        away_sum = add(swap(away_send), away_keep)
+        here_got = swap(here_send)
+        a_arrived = to_chips(away_sum)
+        product = back(routed_a, down_weight, 0, replicas)
+        b_xopp, here_got, product = fence(b_xopp, here_got, product)
+        b_parts = [b, b_next, b_prev, b_opp, b_x, b_xnext, b_xprev, b_xopp]
+        b_slots = slots
     else:
         a, b = [lax.all_gather(part, "expert", axis=0, tiled=True) for part in sent]
         slots = b_slots = jnp.zeros((1,), jnp.int32)
         a_parts, b_parts = [a], [b]
         made = route_first(a_parts, slots)
         away_send, away_keep, here_send, here_keep, routed_a, weighted, table = made
-        final_a = [here_keep, swap(here_send)] + to_chips(add(swap(away_send), away_keep))
-
-    away_send, away_keep, routed_b = route(
-        b_parts, b_slots, width, away_bands, groups, tokens, weighted=weighted, table=table, cap=cap
-    )
-    arrived = to_chips(add(swap(away_send), away_keep))
-    here_send, here_keep = rest(routed_b, weighted, here_bands, width, groups)
-    final_b = [here_keep, swap(here_send)] + arrived
-
-    grad_hidden, grad_slots = back([routed_a, routed_b], table, down_weight, saved, pieces, replicas)
+        here_got = swap(here_send)
+        a_arrived = to_chips(add(swap(away_send), away_keep))
+        product = back(routed_a, down_weight, 0, replicas)
+
+    made = route(b_parts, b_slots, width, bands, groups, tokens, weighted=weighted, table=table, cap=cap)
+    made, a_arrived = fence(made, a_arrived)
+    away_send, away_keep, here_send, here_keep_b, routed_b = made
+    b_arrived = to_chips(add(swap(away_send), away_keep))
+    here_got_b = swap(here_send)
+    grad_hidden, grad_slots = back(routed_b, down_weight, width, replicas, product, table, saved)
     returned = lax.all_to_all(grad_slots, "expert", split_axis=0, concat_axis=0, tiled=True)
+    out = rotate([here_keep, here_got] + a_arrived, turns, 0, rows_own, experts_here, None)
+    out, returned, here_got_b, *b_arrived = fence(out, returned, here_got_b, *b_arrived)
     of_token = returned.reshape(-1, 1, tokens)
     named = routes.T[None] == jnp.arange(of_token.shape[0], dtype=jnp.int32)[:, None, None]
     grad_prob = jnp.sum(jnp.where(named, of_token, 0.0), axis=0).T
-
-    out = rotate(final_a, turns, 0, rows_own, experts_here, None)
-    out = rotate(final_b, turns, width // BLOCK, rows_own, experts_here, out)
+    out = rotate([here_keep_b, here_got_b] + b_arrived, turns, width // BLOCK, rows_own, experts_here, out)
     return (grad_hidden[None], grad_prob, out)
 
 

time: 142 us -> 121 us (0.85)
  starting transfers between devices: 44.8 us -> 29.3 us
  waiting for transfers between devices: 48.1 us -> 40.3 us
    ppermute x11 -> x8, starting transfers between devices: 19.4 us -> 9.42 us  [across(): return lax.ppermute(value, 'expert', [(i, i ^ 1) for i in range(2 * LINES)])]
    ppermute x11 -> x8, waiting for transfers between devices: 17.4 us -> 9.52 us  [across(): return lax.ppermute(value, 'expert', [(i, i ^ 1) for i in range(2 * LINES)])]
    ppermute x12 -> x6, starting transfers between devices: 17.8 us -> 11.5 us  [along(): lax.ppermute(value, 'expert', [(2 * a + x, 2 * b + x) for a, b in pairs f...]
    ppermute x12 -> x6, waiting for transfers between devices: 20.3 us -> 24.4 us  [along(): lax.ppermute(value, 'expert', [(2 * a + x, 2 * b + x) for a, b in pairs f...]
    ppermute x2, waiting for transfers between devices: 4.79 us -> 0.81 us  [to_chips(): moved.append(lax.ppermute(value[(k - 1) * width:k * width], 'dp', pairs))]
    all_to_all x1, waiting for transfers between devices: 5.6 us -> 2.36 us  [shards(): lax.all_to_all(grad_slots, 'expert', split_axis=0, concat_axis=0, tiled=T...]
    ppermute x4, waiting for transfers between devices: 0.01 us -> 3.21 us  [swap(): return lax.ppermute(value, 'dp', [(i, i ^ 1) for i in range(replicas)])]
    pallas_call x2, Pallas kernels: 17 us -> 18.7 us  [route(): pl.pallas_call(functools.partial(route_kernel, first, len(parts), bands,...]
  transfers between devices with their start and end apart: 30 -> 21, of which waited for: 13 -> 10; matrix products, arithmetic and copies ran while one was open for 4% -> 4% of each run, Pallas kernels for 20% -> 30%
where the time goes in v2:
time: 121 us; the launch traced here: 120 us
  Pallas kernels  40.9 us (34%)
  waiting for transfers between devices  40.3 us (33%)
  starting transfers between devices  29.3 us (24%)
  other arithmetic  5.29 us (4%)
  local copies, waits for them, and re-layouts  3.59 us (3%)
    ppermute x6, waiting for transfers between devices, along(): lax.ppermute(value, 'expert', [(2 * a + x, 2 * b + x) for a, b in pairs f...  24.4 us
    pallas_call x2, Pallas kernels, route(): pl.pallas_call(functools.partial(route_kernel, first, len(parts), bands,...  18.7 us
    pallas_call x2, Pallas kernels, back(): pl.pallas_call(functools.partial(back_kernel, replicas, last), grid=(expe...  13.8 us
    ppermute x6, starting transfers between devices, along(): lax.ppermute(value, 'expert', [(2 * a + x, 2 * b + x) for a, b in pairs f...  11.5 us
    ppermute x8, waiting for transfers between devices, across(): return lax.ppermute(value, 'expert', [(i, i ^ 1) for i in range(2 * LINES)])  9.52 us
    ppermute x8, starting transfers between devices, across(): return lax.ppermute(value, 'expert', [(i, i ^ 1) for i in range(2 * LINES)])  9.42 us
    pallas_call x2, Pallas kernels, rotate(): pl.pallas_call(functools.partial(rotate_kernel, len(parts), experts_here)...  6.48 us
    all_to_all x1, starting transfers between devices, shards(): lax.all_to_all(grad_slots, 'expert', split_axis=0, concat_axis=0, tiled=T...  4.2 us
  transfers between devices with their start and end apart: 21, of which 10 were waited for; matrix products, arithmetic and copies ran while one was open for 4% of the time, Pallas kernels for 30%

profile of v2, /device:TPU:0, one launch (start us, length us, event | category | flops | bytes accessed | tf_op | source)
XLA Modules:
  0.0 120.2 jit_solution(6195694602267329072)
XLA Ops:
  0.6 2.0 %pack.1 = (bf16[128,1152]{1,0:T(8,128)(2,1)}, bf16[128,1024]{1,0:T(8,128)(2,1)}) custom-call(bf16[128,2048]{1,0:T(8,128)(2,1)} %cot_ref.1, bf16[8,128]{1,0:T(8,128)(2,1)} %bitcast.28, s32[8,128]{1,0:T(8,128)} %bitcast.25), custom_call_target="tpu_custom_call" | custom-call | tf_op jit(solution)/shard_map/pack/pallas_call | solution.py:62
  2.6 2.9 %collective-permute-start = (bf16[128,1152]{1,0:T(8,128)(2,1)}, bf16[128,1152]{1,0:T(8,128)(2,1)S(1)}, u32[]{:S(2)}, u32[]{:S(2)}) collective-permute-start(bf16[128,1152]{1,0:T(8,128)(2,1)} %get-tuple-element.58.refs_0_), channel_id=1, source_target_pairs={{0,1},{1,0},{2,3},{3,2},{4,5},{5,4},{6,7},{7,6},{8,9},{9,8},{10,11... | collective-permute-start | bytes 884744 | tf_op jit(solution)/shard_map/ppermute | solution.py:79
  5.6 1.6 %collective-permute-start.2 = (bf16[128,1152]{1,0:T(8,128)(2,1)}, bf16[128,1152]{1,0:T(8,128)(2,1)S(1)}, u32[]{:S(2)}, u32[]{:S(2)}) collective-permute-start(bf16[128,1152]{1,0:T(8,128)(2,1)} %get-tuple-element.58.refs_0_), channel_id=1, source_target_pairs={{0,2},{1,3},{2,4},{3,5},{4,6},{5,7},{6,0},{7,1},{8,10},{9,11},{10,... | collective-permute-start | bytes 884744 | tf_op jit(solution)/shard_map/ppermute | solution.py:75
  7.1 2.2 %collective-permute-start.3 = (bf16[128,1152]{1,0:T(8,128)(2,1)}, bf16[128,1152]{1,0:T(8,128)(2,1)S(1)}, u32[]{:S(2)}, u32[]{:S(2)}) collective-permute-start(bf16[128,1152]{1,0:T(8,128)(2,1)} %get-tuple-element.58.refs_0_), channel_id=1, source_target_pairs={{0,6},{1,7},{2,0},{3,1},{4,2},{5,3},{6,4},{7,5},{8,14},{9,15},{10,... | collective-permute-start | bytes 884744 | tf_op jit(solution)/shard_map/ppermute | solution.py:75
  9.4 0.3 collective-permute-start.1
  9.7 8.7 %collective-permute-done.1.refs_4_ = bf16[128,1024]{1,0:T(8,128)(2,1)S(1)} collective-permute-done((bf16[128,1024]{1,0:T(8,128)(2,1)}, bf16[128,1024]{1,0:T(8,128)(2,1)S(1)}, u32[]{:S(2)}, u32[]{:S(2)}) %collective-permute-start.1) | collective-permute-done | bytes 262176 | tf_op jit(solution)/shard_map/ppermute | solution.py:79
  18.4 3.4 %collective-permute-done.3.refs_2_ = bf16[128,1152]{1,0:T(8,128)(2,1)S(1)} collective-permute-done((bf16[128,1152]{1,0:T(8,128)(2,1)}, bf16[128,1152]{1,0:T(8,128)(2,1)S(1)}, u32[]{:S(2)}, u32[]{:S(2)}) %collective-permute-start.3) | collective-permute-done | bytes 294944 | tf_op jit(solution)/shard_map/ppermute | solution.py:75
  21.9 1.4 %collective-permute-start.4 = (bf16[128,1152]{1,0:T(8,128)(2,1)}, bf16[128,1152]{1,0:T(8,128)(2,1)S(1)}, u32[]{:S(2)}, u32[]{:S(2)}) collective-permute-start(bf16[128,1152]{1,0:T(8,128)(2,1)} %get-tuple-element.58.refs_0_), channel_id=1, source_target_pairs={{0,4},{1,5},{2,6},{3,7},{4,0},{5,1},{6,2},{7,3},{8,12},{9,13},{10,... | collective-permute-start | bytes 884744 | tf_op jit(solution)/shard_map/ppermute | solution.py:75
  23.2 0.5 collective-permute-start.5
  23.8 1.5 %collective-permute-start.6 = (bf16[128,1152]{1,0:T(8,128)(2,1)S(1)}, bf16[128,1152]{1,0:T(8,128)(2,1)S(1)}, u32[]{:S(2)}, u32[]{:S(2)}) collective-permute-start(bf16[128,1152]{1,0:T(8,128)(2,1)S(1)} %collective-permute-done.3.refs_2_), channel_id=1, source_target_pairs={{0,1},{1,0},{2,3},{3,2},{4,5},{5,4},{6,7},{7,6},{8,9},{9,8},{10,11... | collective-permute-start | bytes 884744 | tf_op jit(solution)/shard_map/ppermute | solution.py:79
  25.2 12.3 %collective-permute-done.4.refs_3_ = bf16[128,1152]{1,0:T(8,128)(2,1)S(1)} collective-permute-done((bf16[128,1152]{1,0:T(8,128)(2,1)}, bf16[128,1152]{1,0:T(8,128)(2,1)S(1)}, u32[]{:S(2)}, u32[]{:S(2)}) %collective-permute-start.4) | collective-permute-done | bytes 294944 | tf_op jit(solution)/shard_map/ppermute | solution.py:75
  37.6 0.6 collective-permute-start.7
  38.2 0.6 collective-permute-start.8
  38.8 3.2 %collective-permute-start.9 = (bf16[128,1024]{1,0:T(8,128)(2,1)}, bf16[128,1024]{1,0:T(8,128)(2,1)S(1)}, u32[]{:S(2)}, u32[]{:S(2)}) collective-permute-start(bf16[128,1024]{1,0:T(8,128)(2,1)} %get-tuple-element.64.refs_0_), channel_id=1, source_target_pairs={{0,6},{1,7},{2,0},{3,1},{4,2},{5,3},{6,4},{7,5},{8,14},{9,15},{10,... | collective-permute-start | bytes 786440 | tf_op jit(solution)/shard_map/ppermute | solution.py:75
  42.0 7.4 %collective-permute-done.8.refs_1_ = bf16[128,1024]{1,0:T(8,128)(2,1)S(1)} collective-permute-done((bf16[128,1024]{1,0:T(8,128)(2,1)}, bf16[128,1024]{1,0:T(8,128)(2,1)S(1)}, u32[]{:S(2)}, u32[]{:S(2)}) %collective-permute-start.8) | collective-permute-done | bytes 262176 | tf_op jit(solution)/shard_map/ppermute | solution.py:75
  49.4 1.2 collective-permute-done.9.refs_2_
  50.6 2.5 %collective-permute-start.10 = (bf16[128,1024]{1,0:T(8,128)(2,1)}, bf16[128,1024]{1,0:T(8,128)(2,1)S(1)}, u32[]{:S(2)}, u32[]{:S(2)}) collective-permute-start(bf16[128,1024]{1,0:T(8,128)(2,1)} %get-tuple-element.64.refs_0_), channel_id=1, source_target_pairs={{0,4},{1,5},{2,6},{3,7},{4,0},{5,1},{6,2},{7,3},{8,12},{9,13},{10,... | collective-permute-start | bytes 786440 | tf_op jit(solution)/shard_map/ppermute | solution.py:75
  53.1 1.5 %collective-permute-start.11 = (bf16[128,1024]{1,0:T(8,128)(2,1)S(1)}, bf16[128,1024]{1,0:T(8,128)(2,1)S(1)}, u32[]{:S(2)}, u32[]{:S(2)}) collective-permute-start(bf16[128,1024]{1,0:T(8,128)(2,1)S(1)} %collective-permute-done.8.refs_1_), channel_id=1, source_target_pairs={{0,1},{1,0},{2,3},{3,2},{4,5},{5,4},{6,7},{7,6},{8,9},{9,8},{10,11... | collective-permute-start | bytes 786440 | tf_op jit(solution)/shard_map/ppermute | solution.py:79
  54.6 0.5 collective-permute-start.12
  55.1 0.6 stack.35.slots_ref
  55.8 10.2 %route.2 = (bf16[256,1536]{1,0:T(8,128)(2,1)}, bf16[256,1536]{1,0:T(8,128)(2,1)}, bf16[256,1536]{1,0:T(8,128)(2,1)}, bf16[256,1536]{1,0:T(8,128)(2,1)}, bf16[2,7...) custom-call(s32[8]{0:T(128)} %stack.35.slots_ref, ...), custom_call_target="tpu_custom_call" | custom-call | tf_op jit(solution)/shard_map/route/pallas_call | solution.py:228
  66.1 0.7 copy-done.14
  66.9 0.5 collective-permute-start.14
  67.4 2.0 %collective-permute-done.15 = bf16[256,1536]{1,0:T(8,128)(2,1)S(1)} collective-permute-done((bf16[256,1536]{1,0:T(8,128)(2,1)}, bf16[256,1536]{1,0:T(8,128)(2,1)S(1)}, u32[]{:S(2)}, u32[]{:S(2)}) %collective-permute-start.15) | collective-permute-done | bytes 786464 | tf_op jit(solution)/shard_map/ppermute | solution.py:372
  69.4 1.3 %add_convert_fusion.1 = bf16[256,1536]{1,0:T(8,128)(2,1)S(1)} fusion(bf16[256,1536]{1,0:T(8,128)(2,1)} %get-tuple-element.93, bf16[256,1536]{1,0:T(8,128)(2,1)S(1)} %collective-permute-done.15), kind=kLoop, calls=%fused_computation.1 | loop fusion | flops 1572864 | bytes 2359296 | tf_op jit(solution)/shard_map/convert_element_type | solution.py:382
  70.7 1.6 %collective-permute-start.16 = (bf16[256,1536]{1,0:T(8,128)(2,1)S(1)}, bf16[256,1536]{1,0:T(8,128)(2,1)S(1)}, u32[]{:S(2)}, u32[]{:S(2)}) collective-permute-start(bf16[256,1536]{1,0:T(8,128)(2,1)S(1)} %add_convert_fusion.1), channel_id=1, source_target_pairs={{0,16},{8,24},{16,0},{24,8},{1,17},{9,25},{17,1},{25,9},{2,18},{10... | collective-permute-start | bytes 2359304 | tf_op jit(solution)/shard_map/ppermute | solution.py:378
  72.3 1.5 %collective-permute-start.13 = (bf16[128,1024]{1,0:T(8,128)(2,1)S(1)}, bf16[128,1024]{1,0:T(8,128)(2,1)S(1)}, u32[]{:S(2)}, u32[]{:S(2)}) collective-permute-start(bf16[128,1024]{1,0:T(8,128)(2,1)S(1)} %copy-done.15), channel_id=1, source_target_pairs={{0,1},{1,0},{2,3},{3,2},{4,5},{5,4},{6,7},{7,6},{8,9},{9,8},{10,11... | collective-permute-start | bytes 786440 | tf_op jit(solution)/shard_map/ppermute | solution.py:79
  73.8 5.7 %back.2.refs_5_ = bf16[2,768,768]{2,1,0:T(8,128)(2,1)} custom-call(bf16[2,768,1024]{2,1,0:T(8,128)(2,1)} %get-tuple-element.83.refs_0_, bf16[2,768,2048]{2,1,0:T(8,128)(2,1)} %refs_4_.3, bf16[2,768,2048]{2,1,0:T(8,128)(2,1)} %refs_4_.3, bf16[2,768,2048]{2,1,0:T(8,128)(2,1)} %refs_4_.3, bf16[2,768,2048]{2,1,0:T(8,128)(2,1)} %refs_4_.3), custom_call_target="tpu_custom_call" | custom-call | tf_op jit(solution)/shard_map/back/pallas_call | solution.py:301
  79.5 0.8 collective-permute-done.13.refs_7_
  80.4 0.7 copy-done.17
  81.1 8.4 %route.3 = (bf16[256,1536]{1,0:T(8,128)(2,1)}, bf16[256,1536]{1,0:T(8,128)(2,1)}, bf16[256,1536]{1,0:T(8,128)(2,1)}, bf16[256,1536]{1,0:T(8,128)(2,1)}, bf16[2,768,1024]{2,1,0:T(8,128)(2,1)}) custom-call(s32[8]{0:T(128)} %stack.35.slots_ref, bf16[128,1024]{1,0:T(8,128)(2,1)} %get-tuple-element.64.refs_0_, bf16[128,1024]{1,0:T(8,128)(2,1)} %copy-done.12, ...), custom_call_target="tpu_custom_call" | custom-call | tf_op jit(solution)/shard_map/route/pallas_call | solution.py:228
  89.5 0.8 collective-permute-done.16.refs_2_
  90.3 0.9 copy-done.3
  91.3 0.8 fusion.18
  92.0 0.5 collective-permute-start.17
  92.5 1.2 %collective-permute-done.18 = bf16[256,1536]{1,0:T(8,128)(2,1)S(1)} collective-permute-done((bf16[256,1536]{1,0:T(8,128)(2,1)}, bf16[256,1536]{1,0:T(8,128)(2,1)S(1)}, u32[]{:S(2)}, u32[]{:S(2)}) %collective-permute-start.18) | collective-permute-done | bytes 786464 | tf_op jit(solution)/shard_map/ppermute | solution.py:372
  93.8 1.3 %add_convert_fusion = bf16[256,1536]{1,0:T(8,128)(2,1)S(1)} fusion(bf16[256,1536]{1,0:T(8,128)(2,1)} %get-tuple-element.103, bf16[256,1536]{1,0:T(8,128)(2,1)S(1)} %collective-permute-done.18), kind=kLoop, calls=%fused_computation | loop fusion | flops 1572864 | bytes 2359296 | tf_op jit(solution)/shard_map/convert_element_type | solution.py:382
  95.1 1.6 %collective-permute-start.19 = (bf16[256,1536]{1,0:T(8,128)(2,1)S(1)}, bf16[256,1536]{1,0:T(8,128)(2,1)S(1)}, u32[]{:S(2)}, u32[]{:S(2)}) collective-permute-start(bf16[256,1536]{1,0:T(8,128)(2,1)S(1)} %add_convert_fusion), channel_id=1, source_target_pairs={{0,16},{8,24},{16,0},{24,8},{1,17},{9,25},{17,1},{25,9},{2,18},{10... | collective-permute-start | bytes 2359304 | tf_op jit(solution)/shard_map/ppermute | solution.py:378
  96.7 0.3 fusion.10
  97.0 8.0 %back.3 = (bf16[2,8,96,768]{3,2,1,0:T(8,128)(2,1)}, f32[8,2,128]{2,1,0:T(2,128)}) custom-call(bf16[2,768,1024]{2,1,0:T(8,128)(2,1)} %get-tuple-element.94.refs_0_, bf16[2,768,2048]{2,1,0:T(8,128)(2,1)} %refs_4_.3, bf16[2,768,2048]{2,1,0:T(8,128)(2,1)} %refs_4_.3, bf16[2,768,2048]{2,1,0:T(8,128)(2,1)} %refs_4_.3, bf16[2,768,2048]{2,1,0:T(8,128)(2,1)} %refs_4_.3, ...), custom_call_target="tpu_custom_call" | custom-call | tf_op jit(solution)/shard_map/back/pallas_call | solution.py:301
  105.1 4.2 %all-to-all-start = ((f32[8,2,128]{2,1,0:T(2,128)}), f32[8,2,128]{2,1,0:T(2,128)S(1)}, u32[]{:S(2)}, u32[]{:S(2)}) async-start(f32[8,2,128]{2,1,0:T(2,128)} %get-tuple-element.100), calls=%async_computation | async-start | bytes 16384 | tf_op jit(solution)/shard_map/all_to_all | solution.py:423
  109.3 0.9 multiply_convert_fusion.turn_ref
  110.2 3.2 %rotate.2.refs_3_ = f32[512,2,768]{2,1,0:T(2,128)} custom-call(bf16[4,256,256]{2,1,0:T(8,128)(2,1)} %multiply_convert_fusion.turn_ref, bf16[256,1536]{1,0:T(8,128)(2,1)} %get-tuple-element.97.refs_0_, bf16[256,1536]{1,0:T(8,128)(2,1)} %copy-done.2, bf16[256,1536]{1,0:T(8,128)(2,1)} %copy-done.3), custom_call_target="tpu_custom_call" | custom-call | tf_op jit(solution)/shard_map/rotate/pallas_call | solution.py:331
  113.4 2.4 %all-to-all-done = f32[8,2,128]{2,1,0:T(2,128)S(1)} async-done(((f32[8,2,128]{2,1,0:T(2,128)}), f32[8,2,128]{2,1,0:T(2,128)S(1)}, u32[]{:S(2)}, u32[]{:S(2)}) %all-to-all-start) | async-done | bytes 8224 | tf_op jit(solution)/shard_map/all_to_all | solution.py:423
  115.8 0.7 select_reduce_fusion
  116.5 0.2 copy-done
  116.7 0.3 copy-done.1
  116.9 3.2 %rotate.3 = f32[512,2,768]{2,1,0:T(2,128)} custom-call(bf16[4,256,256]{2,1,0:T(8,128)(2,1)} %multiply_convert_fusion.turn_ref, bf16[256,1536]{1,0:T(8,128)(2,1)} %get-tuple-element.105.refs_0_, bf16[256,1536]{1,0:T(8,128)(2,1)} %copy-done, bf16[256,1536]{1,0:T(8,128)(2,1)} %copy-done.1, f32[512,2,768]{2,1,0:T(2,128)} %rotate.2.refs_3_), custom_call_target="tpu_custom_call", output_to_operand_aliasing={{}: (4, {})} | custom-call | tf_op jit(solution)/shard_map/rotate/pallas_call | solution.py:331
  (50 shorter events, 0.2 us)
Async XLA Ops:
  2.6 15.8 %collective-permute-start = (bf16[128,1152]{1,0:T(8,128)(2,1)}, bf16[128,1152]{1,0:T(8,128)(2,1)S(1)}, u32[]{:S(2)}, u32[]{:S(2)}) collective-permute-start(bf16[128,1152]{1,0:T(8,128)(2,1)} %get-tuple-element.58.refs_0_), channel_id=1, source_target_pairs={{0,1},{1,0},{2,3},{3,2},{4,5},{5,4},{6,7},{7,6},{8,9},{9,8},{10,11... | collective-permute-start | bytes 884744 | tf_op jit(solution)/shard_map/ppermute | solution.py:79
  5.6 12.8 %collective-permute-start.2 = (bf16[128,1152]{1,0:T(8,128)(2,1)}, bf16[128,1152]{1,0:T(8,128)(2,1)S(1)}, u32[]{:S(2)}, u32[]{:S(2)}) collective-permute-start(bf16[128,1152]{1,0:T(8,128)(2,1)} %get-tuple-element.58.refs_0_), channel_id=1, source_target_pairs={{0,2},{1,3},{2,4},{3,5},{4,6},{5,7},{6,0},{7,1},{8,10},{9,11},{10,... | collective-permute-start | bytes 884744 | tf_op jit(solution)/shard_map/ppermute | solution.py:75
  7.1 14.7 %collective-permute-start.3 = (bf16[128,1152]{1,0:T(8,128)(2,1)}, bf16[128,1152]{1,0:T(8,128)(2,1)S(1)}, u32[]{:S(2)}, u32[]{:S(2)}) collective-permute-start(bf16[128,1152]{1,0:T(8,128)(2,1)} %get-tuple-element.58.refs_0_), channel_id=1, source_target_pairs={{0,6},{1,7},{2,0},{3,1},{4,2},{5,3},{6,4},{7,5},{8,14},{9,15},{10,... | collective-permute-start | bytes 884744 | tf_op jit(solution)/shard_map/ppermute | solution.py:75
  9.4 9.0 %collective-permute-start.1 = (bf16[128,1024]{1,0:T(8,128)(2,1)}, bf16[128,1024]{1,0:T(8,128)(2,1)S(1)}, u32[]{:S(2)}, u32[]{:S(2)}) collective-permute-start(bf16[128,1024]{1,0:T(8,128)(2,1)} %get-tuple-element.64.refs_0_), channel_id=1, source_target_pairs={{0,1},{1,0},{2,3},{3,2},{4,5},{5,4},{6,7},{7,6},{8,9},{9,8},{10,11... | collective-permute-start | bytes 786440 | tf_op jit(solution)/shard_map/ppermute | solution.py:79
  18.4 61.1 %copy-start.11 = (bf16[128,1024]{1,0:T(8,128)(2,1)}, bf16[128,1024]{1,0:T(8,128)(2,1)S(1)}, u32[]{:S(2)}) copy-start(bf16[128,1024]{1,0:T(8,128)(2,1)S(1)} %collective-permute-done.1.refs_4_) | copy-start | bytes 786436
  18.4 37.3 %copy-start.4 = (bf16[128,1152]{1,0:T(8,128)(2,1)}, bf16[128,1152]{1,0:T(8,128)(2,1)S(1)}, u32[]{:S(2)}) copy-start(bf16[128,1152]{1,0:T(8,128)(2,1)S(1)} %collective-permute-done.refs_4_) | copy-start | bytes 884740
  18.4 37.3 %copy-start.5 = (bf16[128,1152]{1,0:T(8,128)(2,1)}, bf16[128,1152]{1,0:T(8,128)(2,1)S(1)}, u32[]{:S(2)}) copy-start(bf16[128,1152]{1,0:T(8,128)(2,1)S(1)} %collective-permute-done.2.refs_1_) | copy-start | bytes 884740
  21.9 33.9 %copy-start.6 = (bf16[128,1152]{1,0:T(8,128)(2,1)}, bf16[128,1152]{1,0:T(8,128)(2,1)S(1)}, u32[]{:S(2)}) copy-start(bf16[128,1152]{1,0:T(8,128)(2,1)S(1)} %collective-permute-done.3.refs_2_) | copy-start | bytes 884740
  21.9 15.7 %collective-permute-start.4 = (bf16[128,1152]{1,0:T(8,128)(2,1)}, bf16[128,1152]{1,0:T(8,128)(2,1)S(1)}, u32[]{:S(2)}, u32[]{:S(2)}) collective-permute-start(bf16[128,1152]{1,0:T(8,128)(2,1)} %get-tuple-element.58.refs_0_), channel_id=1, source_target_pairs={{0,4},{1,5},{2,6},{3,7},{4,0},{5,1},{6,2},{7,3},{8,12},{9,13},{10,... | collective-permute-start | bytes 884744 | tf_op jit(solution)/shard_map/ppermute | solution.py:75
  23.2 14.3 %collective-permute-start.5 = (bf16[128,1152]{1,0:T(8,128)(2,1)S(1)}, bf16[128,1152]{1,0:T(8,128)(2,1)S(1)}, u32[]{:S(2)}, u32[]{:S(2)}) collective-permute-start(bf16[128,1152]{1,0:T(8,128)(2,1)S(1)} %collective-permute-done.2.refs_1_), channel_id=1, source_target_pairs={{0,1},{1,0},{2,3},{3,2},{4,5},{5,4},{6,7},{7,6},{8,9},{9,8},{10,11... | collective-permute-start | bytes 884744 | tf_op jit(solution)/shard_map/ppermute | solution.py:79
  23.8 13.8 %collective-permute-start.6 = (bf16[128,1152]{1,0:T(8,128)(2,1)S(1)}, bf16[128,1152]{1,0:T(8,128)(2,1)S(1)}, u32[]{:S(2)}, u32[]{:S(2)}) collective-permute-start(bf16[128,1152]{1,0:T(8,128)(2,1)S(1)} %collective-permute-done.3.refs_2_), channel_id=1, source_target_pairs={{0,1},{1,0},{2,3},{3,2},{4,5},{5,4},{6,7},{7,6},{8,9},{9,8},{10,11... | collective-permute-start | bytes 884744 | tf_op jit(solution)/shard_map/ppermute | solution.py:79
  37.5 18.2 %copy-start.7 = (bf16[128,1152]{1,0:T(8,128)(2,1)}, bf16[128,1152]{1,0:T(8,128)(2,1)S(1)}, u32[]{:S(2)}) copy-start(bf16[128,1152]{1,0:T(8,128)(2,1)S(1)} %collective-permute-done.4.refs_3_) | copy-start | bytes 884740
  37.6 18.2 %copy-start.8 = (bf16[128,1152]{1,0:T(8,128)(2,1)}, bf16[128,1152]{1,0:T(8,128)(2,1)S(1)}, u32[]{:S(2)}) copy-start(bf16[128,1152]{1,0:T(8,128)(2,1)S(1)} %collective-permute-done.5.refs_5_) | copy-start | bytes 884740
  37.6 18.2 %copy-start.9 = (bf16[128,1152]{1,0:T(8,128)(2,1)}, bf16[128,1152]{1,0:T(8,128)(2,1)S(1)}, u32[]{:S(2)}) copy-start(bf16[128,1152]{1,0:T(8,128)(2,1)S(1)} %collective-permute-done.6.refs_6_) | copy-start | bytes 884740
  37.6 13.0 %collective-permute-start.7 = (bf16[128,1152]{1,0:T(8,128)(2,1)S(1)}, bf16[128,1152]{1,0:T(8,128)(2,1)S(1)}, u32[]{:S(2)}, u32[]{:S(2)}) collective-permute-start(bf16[128,1152]{1,0:T(8,128)(2,1)S(1)} %collective-permute-done.4.refs_3_), channel_id=1, source_target_pairs={{0,1},{1,0},{2,3},{3,2},{4,5},{5,4},{6,7},{7,6},{8,9},{9,8},{10,11... | collective-permute-start | bytes 884744 | tf_op jit(solution)/shard_map/ppermute | solution.py:79
  38.2 11.3 %collective-permute-start.8 = (bf16[128,1024]{1,0:T(8,128)(2,1)}, bf16[128,1024]{1,0:T(8,128)(2,1)S(1)}, u32[]{:S(2)}, u32[]{:S(2)}) collective-permute-start(bf16[128,1024]{1,0:T(8,128)(2,1)} %get-tuple-element.64.refs_0_), channel_id=1, source_target_pairs={{0,2},{1,3},{2,4},{3,5},{4,6},{5,7},{6,0},{7,1},{8,10},{9,11},{10,... | collective-permute-start | bytes 786440 | tf_op jit(solution)/shard_map/ppermute | solution.py:75
  38.8 11.8 %collective-permute-start.9 = (bf16[128,1024]{1,0:T(8,128)(2,1)}, bf16[128,1024]{1,0:T(8,128)(2,1)S(1)}, u32[]{:S(2)}, u32[]{:S(2)}) collective-permute-start(bf16[128,1024]{1,0:T(8,128)(2,1)} %get-tuple-element.64.refs_0_), channel_id=1, source_target_pairs={{0,6},{1,7},{2,0},{3,1},{4,2},{5,3},{6,4},{7,5},{8,14},{9,15},{10,... | collective-permute-start | bytes 786440 | tf_op jit(solution)/shard_map/ppermute | solution.py:75
  49.4 30.1 %copy-start.12 = (bf16[128,1024]{1,0:T(8,128)(2,1)}, bf16[128,1024]{1,0:T(8,128)(2,1)S(1)}, u32[]{:S(2)}) copy-start(bf16[128,1024]{1,0:T(8,128)(2,1)S(1)} %collective-permute-done.8.refs_1_) | copy-start | bytes 786436
  50.6 15.5 %copy-start.13 = (bf16[128,1024]{1,0:T(8,128)(2,1)}, bf16[128,1024]{1,0:T(8,128)(2,1)S(1)}, u32[]{:S(2)}) copy-start(bf16[128,1024]{1,0:T(8,128)(2,1)S(1)} %collective-permute-done.9.refs_2_) | copy-start | bytes 786436
  50.6 5.2 %copy-start.10 = (bf16[128,1152]{1,0:T(8,128)(2,1)}, bf16[128,1152]{1,0:T(8,128)(2,1)S(1)}, u32[]{:S(2)}) copy-start(bf16[128,1152]{1,0:T(8,128)(2,1)S(1)} %collective-permute-done.7.refs_7_) | copy-start | bytes 884740
  50.6 15.4 %collective-permute-start.10 = (bf16[128,1024]{1,0:T(8,128)(2,1)}, bf16[128,1024]{1,0:T(8,128)(2,1)S(1)}, u32[]{:S(2)}, u32[]{:S(2)}) collective-permute-start(bf16[128,1024]{1,0:T(8,128)(2,1)} %get-tuple-element.64.refs_0_), channel_id=1, source_target_pairs={{0,4},{1,5},{2,6},{3,7},{4,0},{5,1},{6,2},{7,3},{8,12},{9,13},{10,... | collective-permute-start | bytes 786440 | tf_op jit(solution)/shard_map/ppermute | solution.py:75
  53.1 13.0 %collective-permute-start.11 = (bf16[128,1024]{1,0:T(8,128)(2,1)S(1)}, bf16[128,1024]{1,0:T(8,128)(2,1)S(1)}, u32[]{:S(2)}, u32[]{:S(2)}) collective-permute-start(bf16[128,1024]{1,0:T(8,128)(2,1)S(1)} %collective-permute-done.8.refs_1_), channel_id=1, source_target_pairs={{0,1},{1,0},{2,3},{3,2},{4,5},{5,4},{6,7},{7,6},{8,9},{9,8},{10,11... | collective-permute-start | bytes 786440 | tf_op jit(solution)/shard_map/ppermute | solution.py:79
  54.6 11.5 %collective-permute-start.12 = (bf16[128,1024]{1,0:T(8,128)(2,1)S(1)}, bf16[128,1024]{1,0:T(8,128)(2,1)}, u32[]{:S(2)}, u32[]{:S(2)}) collective-permute-start(bf16[128,1024]{1,0:T(8,128)(2,1)S(1)} %collective-permute-done.9.refs_2_), channel_id=1, source_target_pairs={{0,1},{1,0},{2,3},{3,2},{4,5},{5,4},{6,7},{7,6},{8,9},{9,8},{10,11... | collective-permute-start | bytes 786440 | tf_op jit(solution)/shard_map/ppermute | solution.py:79
  66.0 0.7 copy-start.14
  66.0 0.8 copy-start.16
  66.9 2.5 %collective-permute-start.15 = (bf16[256,1536]{1,0:T(8,128)(2,1)}, bf16[256,1536]{1,0:T(8,128)(2,1)S(1)}, u32[]{:S(2)}, u32[]{:S(2)}) collective-permute-start(bf16[256,1536]{1,0:T(8,128)(2,1)} %get-tuple-element.92), channel_id=1, source_target_pairs={{0,8},{8,0},{16,24},{24,16},{1,9},{9,1},{17,25},{25,17},{2,10},{10... | collective-permute-start | bytes 2359304 | tf_op jit(solution)/shard_map/ppermute | solution.py:372
  66.9 5.4 %copy-start.15 = (bf16[128,1024]{1,0:T(8,128)(2,1)S(1)}, bf16[128,1024]{1,0:T(8,128)(2,1)}, u32[]{:S(2)}) copy-start(bf16[128,1024]{1,0:T(8,128)(2,1)} %copy-done.14) | copy-start | bytes 786436
  66.9 13.5 %collective-permute-start.14 = (bf16[256,1536]{1,0:T(8,128)(2,1)}, bf16[256,1536]{1,0:T(8,128)(2,1)S(1)}, u32[]{:S(2)}, u32[]{:S(2)}) collective-permute-start(bf16[256,1536]{1,0:T(8,128)(2,1)} %get-tuple-element.82), channel_id=1, source_target_pairs={{0,8},{8,0},{16,24},{24,16},{1,9},{9,1},{17,25},{25,17},{2,10},{10... | collective-permute-start | bytes 2359304 | tf_op jit(solution)/shard_map/ppermute | solution.py:372
  70.7 19.6 %collective-permute-start.16 = (bf16[256,1536]{1,0:T(8,128)(2,1)S(1)}, bf16[256,1536]{1,0:T(8,128)(2,1)S(1)}, u32[]{:S(2)}, u32[]{:S(2)}) collective-permute-start(bf16[256,1536]{1,0:T(8,128)(2,1)S(1)} %add_convert_fusion.1), channel_id=1, source_target_pairs={{0,16},{8,24},{16,0},{24,8},{1,17},{9,25},{17,1},{25,9},{2,18},{10... | collective-permute-start | bytes 2359304 | tf_op jit(solution)/shard_map/ppermute | solution.py:378
  72.3 8.1 %collective-permute-start.13 = (bf16[128,1024]{1,0:T(8,128)(2,1)S(1)}, bf16[128,1024]{1,0:T(8,128)(2,1)S(1)}, u32[]{:S(2)}, u32[]{:S(2)}) collective-permute-start(bf16[128,1024]{1,0:T(8,128)(2,1)S(1)} %copy-done.15), channel_id=1, source_target_pairs={{0,1},{1,0},{2,3},{3,2},{4,5},{5,4},{6,7},{7,6},{8,9},{9,8},{10,11... | collective-permute-start | bytes 786440 | tf_op jit(solution)/shard_map/ppermute | solution.py:79
  80.4 0.7 copy-start.17
  81.1 14.0 %copy-start.2 = (bf16[256,1536]{1,0:T(8,128)(2,1)}, bf16[256,1536]{1,0:T(8,128)(2,1)S(1)}, u32[]{:S(2)}) copy-start(bf16[256,1536]{1,0:T(8,128)(2,1)S(1)} %collective-permute-done.14.refs_1_) | copy-start | bytes 2359300
  90.3 0.9 copy-start.3
  91.3 2.5 %collective-permute-start.18 = (bf16[256,1536]{1,0:T(8,128)(2,1)}, bf16[256,1536]{1,0:T(8,128)(2,1)S(1)}, u32[]{:S(2)}, u32[]{:S(2)}) collective-permute-start(bf16[256,1536]{1,0:T(8,128)(2,1)} %get-tuple-element.102), channel_id=1, source_target_pairs={{0,8},{8,0},{16,24},{24,16},{1,9},{9,1},{17,25},{25,17},{2,10},{10... | collective-permute-start | bytes 2359304 | tf_op jit(solution)/shard_map/ppermute | solution.py:372
  92.0 23.7 %collective-permute-start.17 = (bf16[256,1536]{1,0:T(8,128)(2,1)}, bf16[256,1536]{1,0:T(8,128)(2,1)S(1)}, u32[]{:S(2)}, u32[]{:S(2)}) collective-permute-start(bf16[256,1536]{1,0:T(8,128)(2,1)} %get-tuple-element.101), channel_id=1, source_target_pairs={{0,8},{8,0},{16,24},{24,16},{1,9},{9,1},{17,25},{25,17},{2,10},{10... | collective-permute-start | bytes 2359304 | tf_op jit(solution)/shard_map/ppermute | solution.py:372
  95.1 20.7 %collective-permute-start.19 = (bf16[256,1536]{1,0:T(8,128)(2,1)S(1)}, bf16[256,1536]{1,0:T(8,128)(2,1)S(1)}, u32[]{:S(2)}, u32[]{:S(2)}) collective-permute-start(bf16[256,1536]{1,0:T(8,128)(2,1)S(1)} %add_convert_fusion), channel_id=1, source_target_pairs={{0,16},{8,24},{16,0},{24,8},{1,17},{9,25},{17,1},{25,9},{2,18},{10... | collective-permute-start | bytes 2359304 | tf_op jit(solution)/shard_map/ppermute | solution.py:378
  105.1 10.7 %all-to-all-start = ((f32[8,2,128]{2,1,0:T(2,128)}), f32[8,2,128]{2,1,0:T(2,128)S(1)}, u32[]{:S(2)}, u32[]{:S(2)}) async-start(f32[8,2,128]{2,1,0:T(2,128)} %get-tuple-element.100), calls=%async_computation | async-start | bytes 16384 | tf_op jit(solution)/shard_map/all_to_all | solution.py:423
  110.2 5.6 %copy-start.18 = (s32[128,8]{0,1:T(8,128)S(1)}, s32[128,8]{0,1:T(8,128)}, u32[]{:S(2)}) copy-start(s32[128,8]{0,1:T(8,128)} %param.8) | copy-start | bytes 12292
  115.8 0.9 copy-start
  115.8 1.2 copy-start.1

commit v3 on v2

v3 whole, which is shorter than its diff:
```python
import functools
import math

import jax
import jax.numpy as jnp
from jax import lax
from jax.experimental import pallas as pl
from jax.experimental.pallas import tpu as pltpu
from jax.sharding import PartitionSpec as P

BLOCK = 128
LANES = 128
CORES = 2
NO_SLOT = 512.0
VMEM = 56 * 1024 * 1024
F32 = jnp.float32
BF16 = jnp.bfloat16


ANY = pl.BlockSpec(memory_space=pl.ANY)
HBM = pl.BlockSpec(memory_space=pltpu.HBM)
SMEM = pl.BlockSpec(memory_space=pltpu.SMEM)


def params(limit=VMEM):
    return pltpu.CompilerParams(vmem_limit_bytes=limit)


def dot(a, b, contract=((1,), (0,))):
    return lax.dot_general(a, b, (contract, ((), ())), preferred_element_type=F32)


def iota(shape, axis):
    return lax.broadcasted_iota(jnp.int32, shape, axis)


def pack_kernel(pieces, replicas, cot_ref, gate_ref, route_ref, *out_refs):
    rows_own = cot_ref.shape[1] // replicas
    for out_ref, (start, width) in zip(out_refs, pieces):
        for q in range(replicas):
            at = q * rows_own + start
            out_ref[:, q * width : (q + 1) * width] = cot_ref[:, at : at + width]
    tokens = cot_ref.shape[0]
    line = iota((LANES, tokens), 0)
    half = LANES // 2
    gate = jnp.zeros((LANES, tokens), F32)
    hit = jnp.zeros((LANES, tokens), F32)
    for k in range(route_ref.shape[0]):
        named = route_ref[k : k + 1, :]
        gate = gate + jnp.where(named == line, gate_ref[k : k + 1, :].astype(F32), 0.0)
        hit = hit + jnp.where(named == line - half, 1.0, 0.0)
    earlier = (iota((tokens, tokens), 0) < iota((tokens, tokens), 1)).astype(F32).astype(BF16)
    rank = dot(hit.astype(BF16), earlier)
    table = jnp.where(line < half, gate, jnp.where(hit > 0, rank, NO_SLOT))
    first = out_refs[0]
    first[:, first.shape[1] - tokens :] = table.astype(BF16)


def pack(cotangent, gate_prob, routes, pieces, replicas):
    tokens = cotangent.shape[0]
    widths = [replicas * width for _, width in pieces]
    widths[0] += tokens
    return pl.pallas_call(
        functools.partial(pack_kernel, pieces, replicas),
        out_shape=[jax.ShapeDtypeStruct((tokens, width), BF16) for width in widths],
        compiler_params=params(),
        name="pack",
    )(cotangent, gate_prob.T, routes.T)


LINES = 4


def along(value, by):
    pairs = [(line, (line + by) % LINES) for line in range(LINES)]
    return lax.ppermute(value, "expert", [(2 * a + x, 2 * b + x) for a, b in pairs for x in (0, 1)])


def across(value):
    return lax.ppermute(value, "expert", [(i, i ^ 1) for i in range(2 * LINES)])


def fence(*values):
    return lax.optimization_barrier(values)


def line_slots():
    place = lax.axis_index("expert")
    line, side = place // 2, place % 2
    before, behind, facing = (line + LINES - 1) % LINES, (line + 1) % LINES, (line + 2) % LINES
    near = [2 * line + side, 2 * line + 1 - side, 2 * before + side, 2 * behind + side]
    far = [2 * facing + side, 2 * before + 1 - side, 2 * behind + 1 - side]
    farthest = [2 * facing + 1 - side]
    return jnp.stack(near + far + farthest).astype(jnp.int32)


def hits(table, expert, experts_here, cap_rows):
    line = iota(table.shape, 0)
    rank = jnp.sum(jnp.where(line == experts_here + expert, table, 0.0), axis=0, keepdims=True)
    prob = jnp.sum(jnp.where(line == expert, table, 0.0), axis=0, keepdims=True)
    return iota((cap_rows, table.shape[1]), 0).astype(F32) == rank, prob


def fill_slots(rows, routed, tables, sources):
    experts_here, slot_rows, columns = routed.shape
    cap_rows = slot_rows // sources
    tokens = rows.shape[0] // sources

    def fill(first, table_ref, s):
        table = table_ref[s]
        picked = [hits(table, e, experts_here, cap_rows)[0].astype(F32).astype(BF16) for e in range(experts_here)]
        at = pl.multiple_of((first + s) * tokens, tokens)
        got = dot(jnp.concatenate(picked, axis=0), rows[pl.ds(at, tokens), :columns]).astype(BF16)
        to = pl.multiple_of((first + s) * cap_rows, cap_rows)
        for e in range(experts_here):
            routed[e, pl.ds(to, cap_rows), :] = got[e * cap_rows : (e + 1) * cap_rows, :]

    first = 0
    for table_ref in tables:
        each(table_ref.shape[0], functools.partial(fill, first, table_ref))
        first += table_ref.shape[0]


def each(count, body):
    def step(s, carry):
        body(s)
        return carry

    lax.fori_loop(0, count, step, 0, unroll=count <= 8)


def part_copies(parts, rows, sem):
    size = rows.shape[0] // len(parts)
    return [
        pltpu.make_async_copy(part, rows.at[pl.ds(i * size, size), :], sem.at[i]) for i, part in enumerate(parts)
    ]


def whole(part):
    return pl.BlockSpec((1,) + part.shape[1:], lambda e, *_: (e, 0, 0))


def weight_share(weight, columns, replicas, start):
    units, features = weight.shape[1:]
    width, rows_own = columns // replicas, features // replicas

    def share(q):
        return pl.BlockSpec((1, units, width), lambda e: (e, 0, (q * rows_own + start) // width))

    return [share(q) for q in range(replicas)]


def joined(refs):
    return jnp.concatenate([ref[0] for ref in refs], axis=1)


def visit_kernel(parts_here, shares, begin, slots_ref, *refs):
    parts, refs = refs[:parts_here], refs[parts_here:]
    weight_refs, refs = refs[:shares], refs[shares:]
    hidden_hbm, routed_ref, weighted_ref, table_ref = refs[:4]
    product_ref = refs[4] if shares else None
    rows, routed, saved, part_sem, saved_sem = refs[-5:]
    expert = pl.program_id(0)
    experts_here, slot_rows, columns = routed.shape
    _, count, cap, units = saved.shape
    tokens = table_ref.shape[2]
    cap_rows = slot_rows // count

    def saved_copies(s):
        return pltpu.make_async_copy(hidden_hbm.at[:, slots_ref[begin + s]], saved.at[:, s], saved_sem.at[s])

    @pl.when(expert == 0)
    def _():
        for copy in part_copies(parts, rows, part_sem):
            copy.start()
        each(count, lambda s: saved_copies(s).start())
        for copy in part_copies(parts, rows, part_sem):
            copy.wait()
        base = lax.axis_index("expert") * experts_here
        row, lane = iota((8, LANES), 0), iota((8, LANES), 1)
        wanted = base + jnp.where(row < experts_here, row, row - experts_here + LANES // 2)
        chosen = ((lane == wanted) & (row < 2 * experts_here)).astype(F32).astype(BF16)

        def look_up(s):
            at = pl.multiple_of(s * tokens, tokens)
            table_ref[s] = dot(chosen, rows[pl.ds(at, tokens), columns : columns + tokens])

        each(count, look_up)
        fill_slots(rows, routed, [table_ref], count)
        each(count, lambda s: saved_copies(s).wait())

    routed_ref[0] = routed[expert]
    if shares:
        product_ref[0] = dot(routed[expert], joined(weight_refs), ((1,), (1,))).astype(BF16)

    def weigh(s):
        hit, prob = hits(table_ref[s], expert, experts_here, cap)
        of_slot = jnp.sum(jnp.where(hit, prob, 0.0), axis=1, keepdims=True)
        scaled = of_slot * saved[expert, s].astype(F32)
        if cap_rows > cap:
            scaled = jnp.concatenate([scaled, jnp.zeros((cap_rows - cap, units), F32)], axis=0)
        weighted_ref[0, pl.ds(pl.multiple_of(s * cap_rows, cap_rows), cap_rows), :] = scaled.astype(BF16)

    each(count, weigh)


def visit(parts, slots, begin, weight, hidden, replicas, tokens, with_product=True):
    experts_here, _, cap, units = hidden.shape
    cap_rows = -(-cap // 16) * 16
    count = sum(part.shape[0] for part in parts) // tokens
    slot_rows = count * cap_rows
    columns = parts[0].shape[1] - tokens
    shares = weight_share(weight, columns, replicas, 0) if with_product else []
    product = jax.ShapeDtypeStruct((experts_here, slot_rows, units), BF16)
    routed = jax.ShapeDtypeStruct((experts_here, slot_rows, columns), BF16)
    table = jax.ShapeDtypeStruct((count, 8, tokens), F32)
    return pl.pallas_call(
        functools.partial(visit_kernel, len(parts), len(shares), begin),
        grid=(experts_here,),
        in_specs=[SMEM] + [HBM] * len(parts) + shares + [HBM],
        out_specs=[whole(routed), whole(product), pl.BlockSpec(table.shape, lambda e: (0, 0, 0))]
        + [whole(product)] * with_product,
        out_shape=[routed, product, table] + [product] * with_product,
        scratch_shapes=[
            pltpu.VMEM((count * tokens, parts[0].shape[1]), BF16),
            pltpu.VMEM((experts_here, slot_rows, columns), BF16),
            pltpu.VMEM((experts_here, count, cap, units), BF16),
            pltpu.SemaphoreType.DMA((len(parts),)),
            pltpu.SemaphoreType.DMA((count,)),
        ],
        compiler_params=params(),
        name="visit",
    )(slots, *parts, *[weight] * len(shares), hidden)


def owners(replicas):
    place = lax.axis_index("dp")
    groups = replicas // CORES
    chip, core = place // CORES, place % CORES
    away = [(chip + j + 1) % groups * CORES for j in range(groups)]
    return jnp.stack([at + 1 - core for at in away] + [at + core for at in away]).astype(jnp.int32)


def store_bands(taken, weighted_refs, outs):
    weighted = jnp.concatenate([ref[0] for ref in weighted_refs], axis=0)
    made = dot(taken, weighted, ((0,), (0,))).astype(BF16)
    at = 0
    for out_ref in outs:
        out_ref[...] = made[at : at + out_ref.shape[0], :]
        at += out_ref.shape[0]


def band_outputs(bands, width, experts_here, units):
    rows = [len(band) * width for band in bands]
    rows = [rows[0] // 2, rows[0] // 2] + rows[1:]
    specs = [pl.BlockSpec((size, units), lambda e, *_: (0, e)) for size in rows]
    shapes = [jax.ShapeDtypeStruct((size, experts_here * units), BF16) for size in rows]
    return specs, shapes


def bands_kernel(total, groups_here, weighted_here, owners_ref, *refs):
    taken = [
        jnp.concatenate([ref[0] for ref in refs[j * groups_here : (j + 1) * groups_here]], axis=0)
        for j in range(total)
    ]
    refs = refs[total * groups_here :]
    store_bands(jnp.concatenate(taken, axis=1), refs[:weighted_here], refs[weighted_here:])


def grad_bands(routed, weighted, owned, bands):
    experts_here, _, units = weighted[0].shape
    width = routed[0].shape[2] // owned.shape[0]
    wanted = [j for band in bands for j in band]
    out_specs, out_shape = band_outputs(bands, width, experts_here, units)

    def share(part, j):
        return pl.BlockSpec((1, part.shape[1], width), lambda e, owned: (e, 0, owned[j]))

    return pl.pallas_call(
        functools.partial(bands_kernel, len(wanted), len(routed), len(weighted)),
        grid_spec=pltpu.PrefetchScalarGridSpec(
            num_scalar_prefetch=1,
            grid=(experts_here,),
            in_specs=[share(part, j) for j in wanted for part in routed] + [whole(part) for part in weighted],
            out_specs=out_specs,
        ),
        out_shape=out_shape,
        compiler_params=params(),
        name="bands",
    )(owned, *[part for _ in wanted for part in routed], *weighted)


def route_kernel(parts_here, groups_here, wanted, width, owners_ref, *refs):
    parts, refs = refs[:parts_here], refs[parts_here:]
    tables, refs = refs[:groups_here], refs[groups_here:]
    weighted, refs = refs[:groups_here], refs[groups_here:]
    outs, (routed_hbm, rows, routed, part_sem, out_sem) = refs[:-5], refs[-5:]
    expert = pl.program_id(0)
    keep = pltpu.make_async_copy(routed, routed_hbm, out_sem)

    @pl.when(expert == 0)
    def _():
        for copy in part_copies(parts, rows, part_sem):
            copy.start()
        for copy in part_copies(parts, rows, part_sem):
            copy.wait()
        fill_slots(rows, routed, tables, sum(table.shape[0] for table in tables))
        keep.start()

    taken = [routed[expert, :, pl.ds(pl.multiple_of(owners_ref[j] * width, LANES), width)] for j in wanted]
    store_bands(jnp.concatenate(taken, axis=1), weighted, outs)

    @pl.when(expert == pl.num_programs(0) - 1)
    def _():
        keep.wait()


def route(parts, tables, weighted, owned, bands):
    experts_here, _, units = weighted[0].shape
    slot_rows = sum(part.shape[1] for part in weighted)
    token_rows, tokens = sum(part.shape[0] for part in parts), tables[0].shape[2]
    columns = parts[0].shape[1]
    width = columns // owned.shape[0]
    out_specs, out_shape = band_outputs(bands, width, experts_here, units)
    wanted = [j for band in bands for j in band]
    return pl.pallas_call(
        functools.partial(route_kernel, len(parts), len(tables), wanted, width),
        grid=(experts_here,),
        in_specs=[SMEM]
        + [HBM] * len(parts)
        + [pl.BlockSpec(table.shape, lambda e: (0, 0, 0)) for table in tables]
        + [whole(part) for part in weighted],
        out_specs=out_specs + [HBM],
        out_shape=out_shape + [jax.ShapeDtypeStruct((experts_here, slot_rows, columns), BF16)],
        scratch_shapes=[
            pltpu.VMEM((token_rows, columns), BF16),
            pltpu.VMEM((experts_here, slot_rows, columns), BF16),
            pltpu.SemaphoreType.DMA((len(parts),)),
            pltpu.SemaphoreType.DMA,
        ],
        compiler_params=params(),
        cost_estimate=pl.CostEstimate(
            flops=2 * experts_here * slot_rows * columns * (units + tokens), bytes_accessed=10_000_000, transcendentals=0
        ),
        name="route",
    )(owned, *parts, *tables, *weighted)


def back_kernel(shares, seen_here, late_here, groups_here, slots_ref, routed_ref, *refs):
    last_weights, refs = refs[:shares], refs[shares:]
    first_weights, refs = refs[: shares * late_here], refs[shares * late_here :]
    late, refs = refs[:late_here], refs[late_here:]
    seen, refs = refs[:seen_here], refs[seen_here:]
    tables, refs = refs[:groups_here], refs[groups_here:]
    hidden_ref, grad_ref, prob_ref, held = refs
    expert = pl.program_id(0)
    experts_here = pl.num_programs(0)
    _, sources, cap, units = hidden_ref.shape
    cap_rows = held.shape[0] // sources
    before = [ref[0].astype(F32) for ref in seen]
    before += [dot(ref[0], joined(first_weights), ((1,), (1,))) for ref in late]
    held[...] = dot(routed_ref[0], joined(last_weights), ((1,), (1,))) + jnp.concatenate(before, axis=0)

    def finish(first, table_ref, s):
        at = first + s
        source = slots_ref[at]
        mine = held[pl.ds(pl.multiple_of(at * cap_rows, cap_rows), cap), :]
        hit, prob = hits(table_ref[s], expert, experts_here, cap)
        of_slot = jnp.sum(jnp.where(hit, prob, 0.0), axis=1, keepdims=True)
        grad_ref[0, pl.ds(source, 1)] = (of_slot * mine).astype(BF16)[None]
        inner = jnp.sum(mine * hidden_ref[0, source].astype(F32), axis=1, keepdims=True)
        gate = jnp.sum(jnp.where(hit, inner, 0.0), axis=0, keepdims=True)
        prob_ref[pl.ds(source, 1), pl.ds(expert, 1), :] = gate[None]

    first = 0
    for table_ref in tables:
        each(table_ref.shape[0], functools.partial(finish, first, table_ref))
        first += table_ref.shape[0]


def back(routed, slots, weight, hidden, start, replicas, seen, late, tables):
    experts_here, sources, cap, units = hidden.shape
    columns = routed.shape[2]
    tokens = tables[0].shape[2]
    saved = pl.BlockSpec((1, sources, cap, units), lambda e: (e, 0, 0, 0))
    return pl.pallas_call(
        functools.partial(back_kernel, replicas, len(seen), len(late), len(tables)),
        grid=(experts_here,),
        in_specs=[SMEM, whole(routed)]
        + weight_share(weight, columns, replicas, start)
        + weight_share(weight, columns, replicas, 0) * len(late)
        + [whole(part) for part in late]
        + [whole(part) for part in seen]
        + [pl.BlockSpec(table.shape, lambda e: (0, 0, 0)) for table in tables]
        + [saved],
        out_specs=[saved, pl.BlockSpec((sources, experts_here, tokens), lambda e: (0, 0, 0))],
        out_shape=[
            jax.ShapeDtypeStruct(hidden.shape, BF16),
            jax.ShapeDtypeStruct((sources, experts_here, tokens), F32),
        ],
        scratch_shapes=[pltpu.VMEM((routed.shape[1], units), F32)],
        compiler_params=params(),
        name="back",
    )(slots, routed, *[weight] * (replicas * (1 + len(late))), *late, *seen, *tables, hidden)


def rotate_kernel(count, experts_here, turn_ref, *refs):
    parts, out_ref = refs[:count], refs[-1]
    units = parts[0].shape[1] // experts_here
    total = parts[0][...].astype(F32)
    for ref in parts[1:]:
        total = total + ref[...].astype(F32)
    side = jnp.concatenate([total[:, e * units : (e + 1) * units] for e in range(experts_here)], axis=0)
    high = side.astype(BF16)
    low = (side - high.astype(F32)).astype(BF16)
    turn = turn_ref[0]
    turned = (dot(turn, high) + dot(turn, low)) * (1.0 / math.sqrt(BLOCK))
    out_ref[...] = turned.reshape(out_ref.shape)


def rotate(parts, turns, first_block, rows_out, experts_here, filled):
    rows, lines = parts[0].shape
    units = lines // experts_here
    extra = [] if filled is None else [filled]
    return pl.pallas_call(
        functools.partial(rotate_kernel, len(parts), experts_here),
        grid=(rows // BLOCK,),
        in_specs=[pl.BlockSpec((1,) + turns.shape[1:], lambda b: (first_block + b, 0, 0))]
        + [pl.BlockSpec((BLOCK, lines), lambda b: (b, 0)) for _ in parts]
        + [ANY] * len(extra),
        out_specs=pl.BlockSpec((BLOCK, experts_here, units), lambda b: (first_block + b, 0, 0)),
        out_shape=jax.ShapeDtypeStruct((rows_out, experts_here, units), F32),
        input_output_aliases={1 + len(parts): 0} if extra else {},
        compiler_params=params(),
        name="rotate",
    )(turns, *parts, *extra)


def turn_matrices(sign_seed, rows_own, experts_here):
    row = jnp.arange(BLOCK * experts_here, dtype=jnp.int32)
    anded = (row // experts_here)[:, None] & (row % BLOCK)[None, :]
    parity = sum(((anded >> shift) & 1) for shift in range(BLOCK.bit_length() - 1)) & 1
    same = (row % experts_here)[:, None] == (row // BLOCK)[None, :]
    matrix = jnp.where(same, 1 - 2 * parity, 0)
    own = lax.dynamic_slice_in_dim(2 * sign_seed - 1, lax.axis_index("dp") * rows_own, rows_own)
    signs = jnp.tile(own.reshape(-1, 1, BLOCK), (1, 1, experts_here))
    return (matrix[None] * signs).astype(BF16)


def shards(cotangent, gate_prob, routes, hidden, down_weight, sign_seed):
    tokens, features = cotangent.shape
    sources, replicas = lax.axis_size("expert"), lax.axis_size("dp")
    groups = replicas // CORES
    experts_here, units = down_weight.shape[0], down_weight.shape[1]
    rows_own = features // replicas
    saved = hidden[0]
    cap = saved.shape[2]
    width = rows_own // 2
    pieces = [(0, width), (width, width)]
    turns = turn_matrices(sign_seed, rows_own, experts_here)
    sent = pack(cotangent, gate_prob, routes, pieces, replicas)
    owned = owners(replicas)
    away_bands = [tuple(range(groups - 1)), tuple(range(groups, 2 * groups - 1))]
    here_bands = [(groups - 1,), (2 * groups - 1,)]

    def swap(value):
        return lax.ppermute(value, "dp", [(i, i ^ 1) for i in range(replicas)])

    def to_chips(value):
        moved = []
        for k in range(1, groups):
            pairs = [(i, (i // CORES + k) % groups * CORES + i % CORES) for i in range(replicas)]
            moved.append(lax.ppermute(value[(k - 1) * width : k * width], "dp", pairs))
        return moved

    def add_swapped(halves, kept):
        got = jnp.concatenate([swap(half) for half in halves], axis=0)
        return (got.astype(F32) + kept.astype(F32)).astype(BF16)

    def visit_first(parts, begin, with_product=True):
        return visit(parts, slots, begin, down_weight, saved, replicas, tokens, with_product)

    def bands_first(visits, bands):
        return grad_bands([made[0] for made in visits], [made[1] for made in visits], owned, bands)

    a, b = sent
    if sources == 2 * LINES:
        a_x, b_x, a_next, a_prev, a, b, turns, owned, slots = fence(
            across(a), across(b), along(a, 1), along(a, -1), a, b, turns, owned, line_slots()
        )
        a_opp, a_xnext, a_xprev = along(a, 2), across(a_next), across(a_prev)
        a_near = visit_first([a, a_x, a_next, a_prev], 0)
        a_opp, a_xnext, a_xprev, a_near, b = fence(a_opp, a_xnext, a_xprev, a_near, b)
        a_xopp, b_next, b_prev = across(a_opp), along(b, 1), along(b, -1)
        a_far = visit_first([a_opp, a_xnext, a_xprev], 4)
        a_xopp, b_next, b_prev, a_far, b = fence(a_xopp, b_next, b_prev, a_far, b)
        b_opp, b_xnext, b_xprev = along(b, 2), across(b_next), across(b_prev)
        a_made = [a_near, a_far, visit_first([a_xopp], 7, with_product=False)]
        made = bands_first(a_made, away_bands + here_bands)
        b_opp, b_xnext, b_xprev, made = fence(b_opp, b_xnext, b_xprev, made)
        *away_send, away_keep, here_send, here_keep = made
        b_xopp = across(b_opp)
        a_arrived = to_chips(add_swapped(away_send, away_keep))
        b_xopp, here_send = fence(b_xopp, here_send)
        b_parts = [b, b_x, b_next, b_prev, b_opp, b_xnext, b_xprev, b_xopp]
        seen, late = [a_near[3], a_far[3]], [a_made[2][0]]
    else:
        a, b = [lax.all_gather(part, "expert", axis=0, tiled=True) for part in sent]
        slots = jnp.arange(sources, dtype=jnp.int32)
        a_made = [visit_first([a], 0)]
        *away_send, away_keep, here_send, here_keep = bands_first(a_made, away_bands + here_bands)
        a_arrived = to_chips(add_swapped(away_send, away_keep))
        b_parts = [b]
        seen, late = [a_made[0][3]], []

    weighted = [made[1] for made in a_made]
    tables = [made[2] for made in a_made]
    made = route(b_parts, tables, weighted, owned, away_bands + here_bands)
    *away_send, away_keep, here_send_b, here_keep_b, routed_b = made
    away_keep, a_arrived = fence(away_keep, a_arrived)
    b_arrived = to_chips(add_swapped(away_send, away_keep))
    here_got, here_got_b = swap(here_send), swap(here_send_b)
    grad_hidden, grad_slots = back(routed_b, slots, down_weight, saved, width, replicas, seen, late, tables)
    returned = lax.all_to_all(grad_slots, "expert", split_axis=0, concat_axis=0, tiled=True)
    out = rotate([here_keep, here_got] + a_arrived, turns, 0, rows_own, experts_here, None)
    out, returned, *b_arrived = fence(out, returned, *b_arrived)
    of_token = returned.reshape(-1, 1, tokens)
    named = routes.T[None] == jnp.arange(of_token.shape[0], dtype=jnp.int32)[:, None, None]
    grad_prob = jnp.sum(jnp.where(named, of_token, 0.0), axis=0).T
    out = rotate([here_keep_b, here_got_b] + b_arrived, turns, width // BLOCK, rows_own, experts_here, out)
    return (grad_hidden[None], grad_prob, out)


def solution(mesh):
    in_specs = (
        P(("dp", "expert"), None),
        P(("dp", "expert"), None),
        P(("dp", "expert"), None),
        P("dp", "expert", None, None, None),
        P("expert", None, None),
        P(),
    )
    out_specs = (
        P("dp", "expert", None, None, None),
        P(("dp", "expert"), None),
        P("dp", "expert", None),
    )
    return jax.shard_map(shards, mesh=mesh, in_specs=in_specs, out_specs=out_specs, check_vma=False)
```

time: 121 us -> 116 us (0.959)
  waiting for transfers between devices: 40.3 us -> 32.7 us
  Pallas kernels: 40.9 us -> 47.3 us
  starting transfers between devices: 29.3 us -> 26.1 us
  local copies, waits for them, and re-layouts: 3.59 us -> 2.31 us
    ppermute x6, waiting for transfers between devices: 24.4 us -> 10.2 us  [along(): lax.ppermute(value, 'expert', [(2 * a + x, 2 * b + x) for a, b in pairs f...]
    pallas_call x4 -> x6, Pallas kernels: 32.4 us -> 38.8 us  [the longest x3 15.6 us: visit(): pl.pallas_call(functools.partial(visit_kernel, len(parts), len(shares), b...]
    ppermute x2, waiting for transfers between devices: 0.81 us -> 5.31 us  [to_chips(): moved.append(lax.ppermute(value[(k - 1) * width:k * width], 'dp', pairs))]
    ppermute x8, waiting for transfers between devices: 9.52 us -> 12.5 us  [across(): return lax.ppermute(value, 'expert', [(i, i ^ 1) for i in range(2 * LINES)])]
    ppermute x6, starting transfers between devices: 11.5 us -> 9.38 us  [along(): lax.ppermute(value, 'expert', [(2 * a + x, 2 * b + x) for a, b in pairs f...]
    ppermute x4 -> x6, waiting for transfers between devices: 3.21 us -> 1.46 us  [swap(): return lax.ppermute(value, 'dp', [(i, i ^ 1) for i in range(replicas)])]
    unnamed x40, local copies, waits for them, and re-layouts: 2.95 us -> 1.64 us
    ppermute x8, starting transfers between devices: 9.42 us -> 8.17 us  [across(): return lax.ppermute(value, 'expert', [(i, i ^ 1) for i in range(2 * LINES)])]
  transfers between devices with their start and end apart: 21 -> 23, of which waited for: 10 -> 10; matrix products, arithmetic and copies ran while one was open for 4% -> 6% of each run, Pallas kernels for 30% -> 36%
where the time goes in v3:
time: 116 us
  Pallas kernels  47.3 us (41%)
  waiting for transfers between devices  32.7 us (28%)
  starting transfers between devices  26.1 us (22%)
  other arithmetic  6.26 us (5%)
  local copies, waits for them, and re-layouts  2.31 us (2%)
    pallas_call x3, Pallas kernels, visit(): pl.pallas_call(functools.partial(visit_kernel, len(parts), len(shares), b...  15.6 us
    ppermute x8, waiting for transfers between devices, across(): return lax.ppermute(value, 'expert', [(i, i ^ 1) for i in range(2 * LINES)])  12.5 us
    ppermute x6, waiting for transfers between devices, along(): lax.ppermute(value, 'expert', [(2 * a + x, 2 * b + x) for a, b in pairs f...  10.2 us
    ppermute x6, starting transfers between devices, along(): lax.ppermute(value, 'expert', [(2 * a + x, 2 * b + x) for a, b in pairs f...  9.38 us
    pallas_call x1, Pallas kernels, back(): pl.pallas_call(functools.partial(back_kernel, replicas, len(seen), len(la...  8.45 us
    ppermute x8, starting transfers between devices, across(): return lax.ppermute(value, 'expert', [(i, i ^ 1) for i in range(2 * LINES)])  8.17 us
    pallas_call x1, Pallas kernels, route(): pl.pallas_call(functools.partial(route_kernel, len(parts), len(tables), w...  8.09 us
    pallas_call x1, Pallas kernels, grad_bands(): pl.pallas_call(functools.partial(bands_kernel, len(wanted), len(routed),...  6.69 us
  transfers between devices with their start and end apart: 23, of which 10 were waited for; matrix products, arithmetic and copies ran while one was open for 6% of the time, Pallas kernels for 36%

profile of v3, /device:TPU:0, one launch (start us, length us, event | category | flops | bytes accessed | tf_op | source)
XLA Modules:
  0.0 115.6 jit_solution(18110511996051057717)
XLA Ops:
  0.6 2.0 %pack.1 = (bf16[128,1152]{1,0:T(8,128)(2,1)}, bf16[128,1024]{1,0:T(8,128)(2,1)}) custom-call(bf16[128,2048]{1,0:T(8,128)(2,1)} %cot_ref.1, bf16[8,128]{1,0:T(8,128)(2,1)} %bitcast.34, s32[8,128]{1,0:T(8,128)} %bitcast.31), custom_call_target="tpu_custom_call" | custom-call | tf_op jit(solution)/shard_map/pack/pallas_call | solution.py:63
  2.6 5.0 %collective-permute-start.3 = (bf16[128,1152]{1,0:T(8,128)(2,1)}, bf16[128,1152]{1,0:T(8,128)(2,1)S(1)}, u32[]{:S(2)}, u32[]{:S(2)}) collective-permute-start(bf16[128,1152]{1,0:T(8,128)(2,1)} %get-tuple-element.73.refs_0_), channel_id=1, source_target_pairs={{0,6},{1,7},{2,0},{3,1},{4,2},{5,3},{6,4},{7,5},{8,14},{9,15},{10,... | collective-permute-start | bytes 884744 | tf_op jit(solution)/shard_map/ppermute | solution.py:76
  7.7 1.5 %collective-permute-start = (bf16[128,1152]{1,0:T(8,128)(2,1)}, bf16[128,1152]{1,0:T(8,128)(2,1)S(1)}, u32[]{:S(2)}, u32[]{:S(2)}) collective-permute-start(bf16[128,1152]{1,0:T(8,128)(2,1)} %get-tuple-element.73.refs_0_), channel_id=1, source_target_pairs={{0,1},{1,0},{2,3},{3,2},{4,5},{5,4},{6,7},{7,6},{8,9},{9,8},{10,11... | collective-permute-start | bytes 884744 | tf_op jit(solution)/shard_map/ppermute | solution.py:80
  9.2 0.5 collective-permute-start.1
  9.7 0.8 fusion.18
  10.5 0.3 fusion.10
  10.8 0.7 pad_add_fusion.owners_ref
  11.4 0.7 stack.55.slots_ref
  12.1 0.9 multiply_convert_fusion.turn_ref
  13.0 8.9 %collective-permute-done.1.refs_1_ = bf16[128,1024]{1,0:T(8,128)(2,1)S(1)} collective-permute-done((bf16[128,1024]{1,0:T(8,128)(2,1)}, bf16[128,1024]{1,0:T(8,128)(2,1)S(1)}, u32[]{:S(2)}, u32[]{:S(2)}) %collective-permute-start.1) | collective-permute-done | bytes 262176 | tf_op jit(solution)/shard_map/ppermute | solution.py:80
  22.0 0.8 collective-permute-start.4
  22.8 1.5 %collective-permute-start.5 = (bf16[128,1152]{1,0:T(8,128)(2,1)S(1)}, bf16[128,1152]{1,0:T(8,128)(2,1)S(1)}, u32[]{:S(2)}, u32[]{:S(2)}) collective-permute-start(bf16[128,1152]{1,0:T(8,128)(2,1)S(1)} %collective-permute-done.2.refs_2_), channel_id=1, source_target_pairs={{0,1},{1,0},{2,3},{3,2},{4,5},{5,4},{6,7},{7,6},{8,9},{9,8},{10,11... | collective-permute-start | bytes 884744 | tf_op jit(solution)/shard_map/ppermute | solution.py:80
  24.3 0.5 collective-permute-start.6
  24.8 6.8 %visit.3 = (bf16[2,384,1024]{2,1,0:T(8,128)(2,1)}, bf16[2,384,768]{2,1,0:T(8,128)(2,1)}, f32[4,8,128]{2,1,0:T(8,128)}, bf16[2,384,768]{2,1,0:T(8,128)(2,1)}) custom-call(s32[8]{0:T(128)} %stack.55.slots_ref, bf16[128,1152]{1,0:T(8,128)(2,1)} %get-tuple-element.73.refs_0_, bf16[128,1152]{1,0:T(8,128)(2,1)} %copy-done.9, bf16[128,1152]{1,0:T(8,128)(2,1)} %copy-done.8, ...), custom_call_target="tpu_custom_call" | custom-call | tf_op jit(solution)/shard_map/visit/pallas_call | solution.py:217
  31.7 5.4 %collective-permute-done.4.refs_0_ = bf16[128,1152]{1,0:T(8,128)(2,1)S(1)} collective-permute-done((bf16[128,1152]{1,0:T(8,128)(2,1)}, bf16[128,1152]{1,0:T(8,128)(2,1)S(1)}, u32[]{:S(2)}, u32[]{:S(2)}) %collective-permute-start.4) | collective-permute-done | bytes 294944 | tf_op jit(solution)/shard_map/ppermute | solution.py:76
  37.1 1.6 %collective-permute-start.7 = (bf16[128,1152]{1,0:T(8,128)(2,1)S(1)}, bf16[128,1152]{1,0:T(8,128)(2,1)S(1)}, u32[]{:S(2)}, u32[]{:S(2)}) collective-permute-start(bf16[128,1152]{1,0:T(8,128)(2,1)S(1)} %collective-permute-done.4.refs_0_), channel_id=1, source_target_pairs={{0,1},{1,0},{2,3},{3,2},{4,5},{5,4},{6,7},{7,6},{8,9},{9,8},{10,11... | collective-permute-start | bytes 884744 | tf_op jit(solution)/shard_map/ppermute | solution.py:80
  38.6 2.2 %collective-permute-start.9 = (bf16[128,1024]{1,0:T(8,128)(2,1)S(1)}, bf16[128,1024]{1,0:T(8,128)(2,1)S(1)}, u32[]{:S(2)}, u32[]{:S(2)}) collective-permute-start(bf16[128,1024]{1,0:T(8,128)(2,1)S(1)} %copy-done.11), channel_id=1, source_target_pairs={{0,6},{1,7},{2,0},{3,1},{4,2},{5,3},{6,4},{7,5},{8,14},{9,15},{10,... | collective-permute-start | bytes 786440 | tf_op jit(solution)/shard_map/ppermute | solution.py:76
  40.9 0.3 collective-permute-start.8
  41.2 5.9 %visit.4 = (bf16[2,288,1024]{2,1,0:T(8,128)(2,1)}, bf16[2,288,768]{2,1,0:T(8,128)(2,1)}, f32[3,8,128]{2,1,0:T(8,128)}, bf16[2,288,768]{2,1,0:T(8,128)(2,1)}) custom-call(s32[8]{0:T(128)} %stack.55.slots_ref, bf16[128,1152]{1,0:T(8,128)(2,1)} %copy-done.3, bf16[128,1152]{1,0:T(8,128)(2,1)} %copy-done.4, bf16[128,1152]{1,0:T(8,128)(2,1)} %copy-done.5, ...), custom_call_target="tpu_custom_call" | custom-call | tf_op jit(solution)/shard_map/visit/pallas_call | solution.py:217
  47.1 0.6 collective-permute-done.9.refs_3_
  47.7 4.2 %collective-permute-done.8.refs_2_ = bf16[128,1024]{1,0:T(8,128)(2,1)S(1)} collective-permute-done((bf16[128,1024]{1,0:T(8,128)(2,1)S(1)}, bf16[128,1024]{1,0:T(8,128)(2,1)S(1)}, u32[]{:S(2)}, u32[]{:S(2)}) %collective-permute-start.8) | collective-permute-done | bytes 262176 | tf_op jit(solution)/shard_map/ppermute | solution.py:76
  51.9 1.0 collective-permute-start.10
  52.9 0.5 collective-permute-start.11
  53.5 1.5 %collective-permute-start.12 = (bf16[128,1024]{1,0:T(8,128)(2,1)S(1)}, bf16[128,1024]{1,0:T(8,128)(2,1)S(1)}, u32[]{:S(2)}, u32[]{:S(2)}) collective-permute-start(bf16[128,1024]{1,0:T(8,128)(2,1)S(1)} %collective-permute-done.9.refs_3_), channel_id=1, source_target_pairs={{0,1},{1,0},{2,3},{3,2},{4,5},{5,4},{6,7},{7,6},{8,9},{9,8},{10,11... | collective-permute-start | bytes 786440 | tf_op jit(solution)/shard_map/ppermute | solution.py:80
  55.0 2.9 %visit.5 = (bf16[2,96,1024]{2,1,0:T(8,128)(2,1)}, bf16[2,96,768]{2,1,0:T(8,128)(2,1)}, f32[1,8,128]{2,1,0:T(8,128)}) custom-call(s32[8]{0:T(128)} %stack.55.slots_ref, bf16[128,1152]{1,0:T(8,128)(2,1)} %copy-done.6, bf16[2,8,96,768]{3,2,1,0:T(8,128)(2,1)} %bitcast.27), custom_call_target="tpu_custom_call" | custom-call | tf_op jit(solution)/shard_map/visit/pallas_call | solution.py:217
  57.9 6.7 %bands.1 = (bf16[128,1536]{1,0:T(8,128)(2,1)}, bf16[128,1536]{1,0:T(8,128)(2,1)}, bf16[256,1536]{1,0:T(8,128)(2,1)}, bf16[256,1536]{1,0:T(8,128)(2,1)}, bf16[256,1536]{1,0:T(8,128)(2,1)}) custom-call(s32[4]{0:T(128)} %pad_add_fusion.owners_ref, bf16[2,384,1024]{2,1,0:T(8,128)(2,1)} %get-tuple-element.94.refs_0_.refs_3_.refs_6_.refs_9_, ...), custom_call_target="tpu_custom_call" | custom-call | tf_op jit(solution)/shard_map/bands/pallas_call | solution.py:279
  64.6 0.2 collective-permute-done.12.refs_6_
  64.8 0.5 collective-permute-start.16
  65.3 0.5 collective-permute-start.13
  65.9 0.9 collective-permute-done.15
  66.8 0.6 collective-permute-done.16
  67.3 1.3 %add_convert_fusion.1 = bf16[256,1536]{1,0:T(8,128)(2,1)S(1)} fusion(bf16[256,1536]{1,0:T(8,128)(2,1)} %get-tuple-element.124, bf16[128,1536]{1,0:T(8,128)(2,1)S(1)} %collective-permute-done.16, bf16[128,1536]{1,0:T(8,128)(2,1)S(1)} %collective-permute-done.15), kind=kLoop, calls=%fused_computation.1 | loop fusion | flops 2752512 | bytes 2359296 | tf_op jit(solution)/shard_map/convert_element_type | solution.py:478
  68.7 1.6 %collective-permute-start.17 = (bf16[256,1536]{1,0:T(8,128)(2,1)S(1)}, bf16[256,1536]{1,0:T(8,128)(2,1)S(1)}, u32[]{:S(2)}, u32[]{:S(2)}) collective-permute-start(bf16[256,1536]{1,0:T(8,128)(2,1)S(1)} %add_convert_fusion.1), channel_id=1, source_target_pairs={{0,16},{8,24},{16,0},{24,8},{1,17},{9,25},{17,1},{25,9},{2,18},{10... | collective-permute-start | bytes 2359304 | tf_op jit(solution)/shard_map/ppermute | solution.py:473
  70.2 3.3 %collective-permute-done.13.refs_7_ = bf16[128,1024]{1,0:T(8,128)(2,1)S(1)} collective-permute-done((bf16[128,1024]{1,0:T(8,128)(2,1)S(1)}, bf16[128,1024]{1,0:T(8,128)(2,1)S(1)}, u32[]{:S(2)}, u32[]{:S(2)}) %collective-permute-start.13) | collective-permute-done | bytes 262176 | tf_op jit(solution)/shard_map/ppermute | solution.py:80
  73.6 0.7 copy-done.18
  74.2 8.1 %route.1 = (bf16[128,1536]{1,0:T(8,128)(2,1)}, bf16[128,1536]{1,0:T(8,128)(2,1)}, bf16[256,1536]{1,0:T(8,128)(2,1)}, bf16[256,1536]{1,0:T(8,128)(2,1)}, bf16[256...) custom-call(s32[4]{0:T(128)} %pad_add_fusion.owners_ref, bf16[128,1024]{1,0:T(8,128)(2,1)} %get-tuple-element.90.refs_0_, ...), custom_call_target="tpu_custom_call" | custom-call | flops 2818572288 | bytes 10000000 | tf_op jit(solution)/shard_map/route/pallas_call | solution.py:326
  82.4 0.5 collective-permute-start.19
  83.0 5.3 %collective-permute-done.17.refs_2_ = bf16[256,1536]{1,0:T(8,128)(2,1)S(1)} collective-permute-done((bf16[256,1536]{1,0:T(8,128)(2,1)S(1)}, bf16[256,1536]{1,0:T(8,128)(2,1)S(1)}, u32[]{:S(2)}, u32[]{:S(2)}) %collective-permute-start.17) | collective-permute-done | bytes 786464 | tf_op jit(solution)/shard_map/ppermute | solution.py:473
  88.3 1.6 %add_convert_fusion = bf16[256,1536]{1,0:T(8,128)(2,1)S(1)} fusion(bf16[256,1536]{1,0:T(8,128)(2,1)} %get-tuple-element.129, bf16[128,1536]{1,0:T(8,128)(2,1)S(1)} %collective-permute-done.19, bf16[128,1536]{1,0:T(8,128)(2,1)S(1)} %collective-permute-done.18), kind=kLoop, calls=%fused_computation | loop fusion | flops 2752512 | bytes 2359296 | tf_op jit(solution)/shard_map/convert_element_type | solution.py:478
  89.9 1.6 %collective-permute-start.20 = (bf16[256,1536]{1,0:T(8,128)(2,1)S(1)}, bf16[256,1536]{1,0:T(8,128)(2,1)S(1)}, u32[]{:S(2)}, u32[]{:S(2)}) collective-permute-start(bf16[256,1536]{1,0:T(8,128)(2,1)S(1)} %add_convert_fusion), channel_id=1, source_target_pairs={{0,16},{8,24},{16,0},{24,8},{1,17},{9,25},{17,1},{25,9},{2,18},{10... | collective-permute-start | bytes 2359304 | tf_op jit(solution)/shard_map/ppermute | solution.py:473
  91.5 8.5 %back.1 = (bf16[2,8,96,768]{3,2,1,0:T(8,128)(2,1)}, f32[8,2,128]{2,1,0:T(2,128)}) custom-call(s32[8]{0:T(128)} %stack.55.slots_ref, bf16[2,768,1024]{2,1,0:T(8,128)(2,1)} %get-tuple-element.114.routed_ref, bf16[2,768,2048]{2,1,0:T(8,128)(2,1)} %refs_7_.3, bf16[2,768,2048]{2,1,0:T(8,128)(2,1)} %refs_7_.3, bf16[2,768,2048]{2,1,0:T(8,128)(2,1)} %refs_7_.3, ...), custom_call_target="tpu_custom_call" | custom-call | tf_op jit(solution)/shard_map/back/pallas_call | solution.py:386
  100.0 4.3 %all-to-all-start = ((f32[8,2,128]{2,1,0:T(2,128)}), f32[8,2,128]{2,1,0:T(2,128)S(1)}, u32[]{:S(2)}, u32[]{:S(2)}) async-start(f32[8,2,128]{2,1,0:T(2,128)} %get-tuple-element.126), calls=%async_computation | async-start | bytes 16384 | tf_op jit(solution)/shard_map/all_to_all | solution.py:524
  104.3 3.2 %rotate.2.refs_3_ = f32[512,2,768]{2,1,0:T(2,128)} custom-call(bf16[4,256,256]{2,1,0:T(8,128)(2,1)} %multiply_convert_fusion.turn_ref, bf16[256,1536]{1,0:T(8,128)(2,1)} %get-tuple-element.119.refs_0_, bf16[256,1536]{1,0:T(8,128)(2,1)} %collective-permute-done.14.refs_1_, bf16[256,1536]{1,0:T(8,128)(2,1)} %copy-done.2), custom_call_target="tpu_custom_call" | custom-call | tf_op jit(solution)/shard_map/rotate/pallas_call | solution.py:425
  107.5 3.3 %all-to-all-done = f32[8,2,128]{2,1,0:T(2,128)S(1)} async-done(((f32[8,2,128]{2,1,0:T(2,128)}), f32[8,2,128]{2,1,0:T(2,128)S(1)}, u32[]{:S(2)}, u32[]{:S(2)}) %all-to-all-start) | async-done | bytes 8224 | tf_op jit(solution)/shard_map/all_to_all | solution.py:524
  110.8 0.7 select_reduce_fusion
  111.4 0.2 copy-done
  111.7 0.7 copy-done.1
  112.3 3.2 %rotate.3 = f32[512,2,768]{2,1,0:T(2,128)} custom-call(bf16[4,256,256]{2,1,0:T(8,128)(2,1)} %multiply_convert_fusion.turn_ref, bf16[256,1536]{1,0:T(8,128)(2,1)} %get-tuple-element.131.refs_0_, bf16[256,1536]{1,0:T(8,128)(2,1)} %copy-done.1, bf16[256,1536]{1,0:T(8,128)(2,1)} %copy-done, f32[512,2,768]{2,1,0:T(2,128)} %rotate.2.refs_3_), custom_call_target="tpu_custom_call", output_to_operand_aliasing={{}: (4, {})} | custom-call | tf_op jit(solution)/shard_map/rotate/pallas_call | solution.py:425
  (57 shorter events, 0.3 us)
Async XLA Ops:
  2.6 19.4 %collective-permute-start.3 = (bf16[128,1152]{1,0:T(8,128)(2,1)}, bf16[128,1152]{1,0:T(8,128)(2,1)S(1)}, u32[]{:S(2)}, u32[]{:S(2)}) collective-permute-start(bf16[128,1152]{1,0:T(8,128)(2,1)} %get-tuple-element.73.refs_0_), channel_id=1, source_target_pairs={{0,6},{1,7},{2,0},{3,1},{4,2},{5,3},{6,4},{7,5},{8,14},{9,15},{10,... | collective-permute-start | bytes 884744 | tf_op jit(solution)/shard_map/ppermute | solution.py:76
  7.7 14.3 %collective-permute-start.2 = (bf16[128,1152]{1,0:T(8,128)(2,1)}, bf16[128,1152]{1,0:T(8,128)(2,1)S(1)}, u32[]{:S(2)}, u32[]{:S(2)}) collective-permute-start(bf16[128,1152]{1,0:T(8,128)(2,1)} %get-tuple-element.73.refs_0_), channel_id=1, source_target_pairs={{0,2},{1,3},{2,4},{3,5},{4,6},{5,7},{6,0},{7,1},{8,10},{9,11},{10,... | collective-permute-start | bytes 884744 | tf_op jit(solution)/shard_map/ppermute | solution.py:76
  7.7 14.3 %collective-permute-start = (bf16[128,1152]{1,0:T(8,128)(2,1)}, bf16[128,1152]{1,0:T(8,128)(2,1)S(1)}, u32[]{:S(2)}, u32[]{:S(2)}) collective-permute-start(bf16[128,1152]{1,0:T(8,128)(2,1)} %get-tuple-element.73.refs_0_), channel_id=1, source_target_pairs={{0,1},{1,0},{2,3},{3,2},{4,5},{5,4},{6,7},{7,6},{8,9},{9,8},{10,11... | collective-permute-start | bytes 884744 | tf_op jit(solution)/shard_map/ppermute | solution.py:80
  9.2 12.8 %collective-permute-start.1 = (bf16[128,1024]{1,0:T(8,128)(2,1)}, bf16[128,1024]{1,0:T(8,128)(2,1)S(1)}, u32[]{:S(2)}, u32[]{:S(2)}) collective-permute-start(bf16[128,1024]{1,0:T(8,128)(2,1)} %get-tuple-element.90.refs_0_), channel_id=1, source_target_pairs={{0,1},{1,0},{2,3},{3,2},{4,5},{5,4},{6,7},{7,6},{8,9},{9,8},{10,11... | collective-permute-start | bytes 786440 | tf_op jit(solution)/shard_map/ppermute | solution.py:80
  22.0 9.7 %copy-start.12 = (bf16[128,1024]{1,0:T(8,128)(2,1)}, bf16[128,1024]{1,0:T(8,128)(2,1)S(1)}, u32[]{:S(2)}) copy-start(bf16[128,1024]{1,0:T(8,128)(2,1)S(1)} %collective-permute-done.1.refs_1_) | copy-start | bytes 786436
  22.0 2.9 %copy-start.7 = (bf16[128,1152]{1,0:T(8,128)(2,1)}, bf16[128,1152]{1,0:T(8,128)(2,1)S(1)}, u32[]{:S(2)}) copy-start(bf16[128,1152]{1,0:T(8,128)(2,1)S(1)} %collective-permute-done.3.refs_3_) | copy-start | bytes 884740
  22.0 2.9 %copy-start.8 = (bf16[128,1152]{1,0:T(8,128)(2,1)}, bf16[128,1152]{1,0:T(8,128)(2,1)S(1)}, u32[]{:S(2)}) copy-start(bf16[128,1152]{1,0:T(8,128)(2,1)S(1)} %collective-permute-done.2.refs_2_) | copy-start | bytes 884740
  22.0 2.8 %copy-start.9 = (bf16[128,1152]{1,0:T(8,128)(2,1)}, bf16[128,1152]{1,0:T(8,128)(2,1)S(1)}, u32[]{:S(2)}) copy-start(bf16[128,1152]{1,0:T(8,128)(2,1)S(1)} %collective-permute-done.refs_1_) | copy-start | bytes 884740
  22.0 15.1 %collective-permute-start.4 = (bf16[128,1152]{1,0:T(8,128)(2,1)}, bf16[128,1152]{1,0:T(8,128)(2,1)S(1)}, u32[]{:S(2)}, u32[]{:S(2)}) collective-permute-start(bf16[128,1152]{1,0:T(8,128)(2,1)} %get-tuple-element.73.refs_0_), channel_id=1, source_target_pairs={{0,4},{1,5},{2,6},{3,7},{4,0},{5,1},{6,2},{7,3},{8,12},{9,13},{10,... | collective-permute-start | bytes 884744 | tf_op jit(solution)/shard_map/ppermute | solution.py:76
  22.8 14.3 %collective-permute-start.5 = (bf16[128,1152]{1,0:T(8,128)(2,1)S(1)}, bf16[128,1152]{1,0:T(8,128)(2,1)S(1)}, u32[]{:S(2)}, u32[]{:S(2)}) collective-permute-start(bf16[128,1152]{1,0:T(8,128)(2,1)S(1)} %collective-permute-done.2.refs_2_), channel_id=1, source_target_pairs={{0,1},{1,0},{2,3},{3,2},{4,5},{5,4},{6,7},{7,6},{8,9},{9,8},{10,11... | collective-permute-start | bytes 884744 | tf_op jit(solution)/shard_map/ppermute | solution.py:80
  24.3 12.8 %collective-permute-start.6 = (bf16[128,1152]{1,0:T(8,128)(2,1)S(1)}, bf16[128,1152]{1,0:T(8,128)(2,1)S(1)}, u32[]{:S(2)}, u32[]{:S(2)}) collective-permute-start(bf16[128,1152]{1,0:T(8,128)(2,1)S(1)} %collective-permute-done.3.refs_3_), channel_id=1, source_target_pairs={{0,1},{1,0},{2,3},{3,2},{4,5},{5,4},{6,7},{7,6},{8,9},{9,8},{10,11... | collective-permute-start | bytes 884744 | tf_op jit(solution)/shard_map/ppermute | solution.py:80
  24.8 13.8 %copy-start.11 = (bf16[128,1024]{1,0:T(8,128)(2,1)S(1)}, bf16[128,1024]{1,0:T(8,128)(2,1)}, u32[]{:S(2)}) copy-start(bf16[128,1024]{1,0:T(8,128)(2,1)} %get-tuple-element.90.refs_0_) | copy-start | bytes 786436
  37.1 4.1 %copy-start.3 = (bf16[128,1152]{1,0:T(8,128)(2,1)}, bf16[128,1152]{1,0:T(8,128)(2,1)S(1)}, u32[]{:S(2)}) copy-start(bf16[128,1152]{1,0:T(8,128)(2,1)S(1)} %collective-permute-done.4.refs_0_) | copy-start | bytes 884740
  37.1 4.1 %copy-start.4 = (bf16[128,1152]{1,0:T(8,128)(2,1)}, bf16[128,1152]{1,0:T(8,128)(2,1)S(1)}, u32[]{:S(2)}) copy-start(bf16[128,1152]{1,0:T(8,128)(2,1)S(1)} %collective-permute-done.5.refs_1_) | copy-start | bytes 884740
  37.1 4.1 %copy-start.5 = (bf16[128,1152]{1,0:T(8,128)(2,1)}, bf16[128,1152]{1,0:T(8,128)(2,1)S(1)}, u32[]{:S(2)}) copy-start(bf16[128,1152]{1,0:T(8,128)(2,1)S(1)} %collective-permute-done.6.refs_2_) | copy-start | bytes 884740
  37.1 14.8 %collective-permute-start.7 = (bf16[128,1152]{1,0:T(8,128)(2,1)S(1)}, bf16[128,1152]{1,0:T(8,128)(2,1)S(1)}, u32[]{:S(2)}, u32[]{:S(2)}) collective-permute-start(bf16[128,1152]{1,0:T(8,128)(2,1)S(1)} %collective-permute-done.4.refs_0_), channel_id=1, source_target_pairs={{0,1},{1,0},{2,3},{3,2},{4,5},{5,4},{6,7},{7,6},{8,9},{9,8},{10,11... | collective-permute-start | bytes 884744 | tf_op jit(solution)/shard_map/ppermute | solution.py:80
  38.6 9.0 %collective-permute-start.9 = (bf16[128,1024]{1,0:T(8,128)(2,1)S(1)}, bf16[128,1024]{1,0:T(8,128)(2,1)S(1)}, u32[]{:S(2)}, u32[]{:S(2)}) collective-permute-start(bf16[128,1024]{1,0:T(8,128)(2,1)S(1)} %copy-done.11), channel_id=1, source_target_pairs={{0,6},{1,7},{2,0},{3,1},{4,2},{5,3},{6,4},{7,5},{8,14},{9,15},{10,... | collective-permute-start | bytes 786440 | tf_op jit(solution)/shard_map/ppermute | solution.py:76
  40.9 11.0 %collective-permute-start.8 = (bf16[128,1024]{1,0:T(8,128)(2,1)S(1)}, bf16[128,1024]{1,0:T(8,128)(2,1)S(1)}, u32[]{:S(2)}, u32[]{:S(2)}) collective-permute-start(bf16[128,1024]{1,0:T(8,128)(2,1)S(1)} %copy-done.11), channel_id=1, source_target_pairs={{0,2},{1,3},{2,4},{3,5},{4,6},{5,7},{6,0},{7,1},{8,10},{9,11},{10,... | collective-permute-start | bytes 786440 | tf_op jit(solution)/shard_map/ppermute | solution.py:76
  47.7 16.9 %copy-start.13 = (bf16[128,1024]{1,0:T(8,128)(2,1)}, bf16[128,1024]{1,0:T(8,128)(2,1)S(1)}, u32[]{:S(2)}) copy-start(bf16[128,1024]{1,0:T(8,128)(2,1)S(1)} %collective-permute-done.9.refs_3_) | copy-start | bytes 786436
  51.9 12.7 %copy-start.14 = (bf16[128,1024]{1,0:T(8,128)(2,1)}, bf16[128,1024]{1,0:T(8,128)(2,1)S(1)}, u32[]{:S(2)}) copy-start(bf16[128,1024]{1,0:T(8,128)(2,1)S(1)} %collective-permute-done.8.refs_2_) | copy-start | bytes 786436
  51.9 3.0 %copy-start.6 = (bf16[128,1152]{1,0:T(8,128)(2,1)}, bf16[128,1152]{1,0:T(8,128)(2,1)S(1)}, u32[]{:S(2)}) copy-start(bf16[128,1152]{1,0:T(8,128)(2,1)S(1)} %collective-permute-done.7.refs_0_) | copy-start | bytes 884740
  51.9 12.7 %collective-permute-start.10 = (bf16[128,1024]{1,0:T(8,128)(2,1)S(1)}, bf16[128,1024]{1,0:T(8,128)(2,1)S(1)}, u32[]{:S(2)}, u32[]{:S(2)}) collective-permute-start(bf16[128,1024]{1,0:T(8,128)(2,1)S(1)} %copy-done.11), channel_id=1, source_target_pairs={{0,4},{1,5},{2,6},{3,7},{4,0},{5,1},{6,2},{7,3},{8,12},{9,13},{10,... | collective-permute-start | bytes 786440 | tf_op jit(solution)/shard_map/ppermute | solution.py:76
  52.9 11.7 %collective-permute-start.11 = (bf16[128,1024]{1,0:T(8,128)(2,1)S(1)}, bf16[128,1024]{1,0:T(8,128)(2,1)S(1)}, u32[]{:S(2)}, u32[]{:S(2)}) collective-permute-start(bf16[128,1024]{1,0:T(8,128)(2,1)S(1)} %collective-permute-done.8.refs_2_), channel_id=1, source_target_pairs={{0,1},{1,0},{2,3},{3,2},{4,5},{5,4},{6,7},{7,6},{8,9},{9,8},{10,11... | collective-permute-start | bytes 786440 | tf_op jit(solution)/shard_map/ppermute | solution.py:80
  53.5 11.4 %collective-permute-start.12 = (bf16[128,1024]{1,0:T(8,128)(2,1)S(1)}, bf16[128,1024]{1,0:T(8,128)(2,1)S(1)}, u32[]{:S(2)}, u32[]{:S(2)}) collective-permute-start(bf16[128,1024]{1,0:T(8,128)(2,1)S(1)} %collective-permute-done.9.refs_3_), channel_id=1, source_target_pairs={{0,1},{1,0},{2,3},{3,2},{4,5},{5,4},{6,7},{7,6},{8,9},{9,8},{10,11... | collective-permute-start | bytes 786440 | tf_op jit(solution)/shard_map/ppermute | solution.py:80
  64.6 9.0 %copy-start.15 = (bf16[128,1024]{1,0:T(8,128)(2,1)}, bf16[128,1024]{1,0:T(8,128)(2,1)S(1)}, u32[]{:S(2)}) copy-start(bf16[128,1024]{1,0:T(8,128)(2,1)S(1)} %collective-permute-done.10.refs_4_) | copy-start | bytes 786436
  64.6 9.0 %copy-start.16 = (bf16[128,1024]{1,0:T(8,128)(2,1)}, bf16[128,1024]{1,0:T(8,128)(2,1)S(1)}, u32[]{:S(2)}) copy-start(bf16[128,1024]{1,0:T(8,128)(2,1)S(1)} %collective-permute-done.11.refs_5_) | copy-start | bytes 786436
  64.8 8.7 %copy-start.17 = (bf16[128,1024]{1,0:T(8,128)(2,1)}, bf16[128,1024]{1,0:T(8,128)(2,1)S(1)}, u32[]{:S(2)}) copy-start(bf16[128,1024]{1,0:T(8,128)(2,1)S(1)} %collective-permute-done.12.refs_6_) | copy-start | bytes 786436
  64.8 1.9 %collective-permute-start.15 = (bf16[128,1536]{1,0:T(8,128)(2,1)}, bf16[128,1536]{1,0:T(8,128)(2,1)S(1)}, u32[]{:S(2)}, u32[]{:S(2)}) collective-permute-start(bf16[128,1536]{1,0:T(8,128)(2,1)} %get-tuple-element.122), channel_id=1, source_target_pairs={{0,8},{8,0},{16,24},{24,16},{1,9},{9,1},{17,25},{25,17},{2,10},{10... | collective-permute-start | bytes 1179656 | tf_op jit(solution)/shard_map/ppermute | solution.py:467
  64.8 2.5 %collective-permute-start.16 = (bf16[128,1536]{1,0:T(8,128)(2,1)}, bf16[128,1536]{1,0:T(8,128)(2,1)S(1)}, u32[]{:S(2)}, u32[]{:S(2)}) collective-permute-start(bf16[128,1536]{1,0:T(8,128)(2,1)} %get-tuple-element.123), channel_id=1, source_target_pairs={{0,8},{8,0},{16,24},{24,16},{1,9},{9,1},{17,25},{25,17},{2,10},{10... | collective-permute-start | bytes 1179656 | tf_op jit(solution)/shard_map/ppermute | solution.py:467
  65.3 8.2 %collective-permute-start.13 = (bf16[128,1024]{1,0:T(8,128)(2,1)S(1)}, bf16[128,1024]{1,0:T(8,128)(2,1)S(1)}, u32[]{:S(2)}, u32[]{:S(2)}) collective-permute-start(bf16[128,1024]{1,0:T(8,128)(2,1)S(1)} %collective-permute-done.10.refs_4_), channel_id=1, source_target_pairs={{0,1},{1,0},{2,3},{3,2},{4,5},{5,4},{6,7},{7,6},{8,9},{9,8},{10,11... | collective-permute-start | bytes 786440 | tf_op jit(solution)/shard_map/ppermute | solution.py:80
  68.7 19.6 %collective-permute-start.17 = (bf16[256,1536]{1,0:T(8,128)(2,1)S(1)}, bf16[256,1536]{1,0:T(8,128)(2,1)S(1)}, u32[]{:S(2)}, u32[]{:S(2)}) collective-permute-start(bf16[256,1536]{1,0:T(8,128)(2,1)S(1)} %add_convert_fusion.1), channel_id=1, source_target_pairs={{0,16},{8,24},{16,0},{24,8},{1,17},{9,25},{17,1},{25,9},{2,18},{10... | collective-permute-start | bytes 2359304 | tf_op jit(solution)/shard_map/ppermute | solution.py:473
  73.6 0.7 copy-start.18
  82.3 6.0 %collective-permute-start.18 = (bf16[128,1536]{1,0:T(8,128)(2,1)}, bf16[128,1536]{1,0:T(8,128)(2,1)S(1)}, u32[]{:S(2)}, u32[]{:S(2)}) collective-permute-start(bf16[128,1536]{1,0:T(8,128)(2,1)} %get-tuple-element.127), channel_id=1, source_target_pairs={{0,8},{8,0},{16,24},{24,16},{1,9},{9,1},{17,25},{25,17},{2,10},{10... | collective-permute-start | bytes 1179656 | tf_op jit(solution)/shard_map/ppermute | solution.py:467
  82.4 5.9 %collective-permute-start.19 = (bf16[128,1536]{1,0:T(8,128)(2,1)}, bf16[128,1536]{1,0:T(8,128)(2,1)S(1)}, u32[]{:S(2)}, u32[]{:S(2)}) collective-permute-start(bf16[128,1536]{1,0:T(8,128)(2,1)} %get-tuple-element.128), channel_id=1, source_target_pairs={{0,8},{8,0},{16,24},{24,16},{1,9},{9,1},{17,25},{25,17},{2,10},{10... | collective-permute-start | bytes 1179656 | tf_op jit(solution)/shard_map/ppermute | solution.py:467
  82.9 21.3 %collective-permute-start.14 = (bf16[256,1536]{1,0:T(8,128)(2,1)}, bf16[256,1536]{1,0:T(8,128)(2,1)}, u32[]{:S(2)}, u32[]{:S(2)}) collective-permute-start(bf16[256,1536]{1,0:T(8,128)(2,1)} %get-tuple-element.120), channel_id=1, source_target_pairs={{0,8},{8,0},{16,24},{24,16},{1,9},{9,1},{17,25},{25,17},{2,10},{10... | collective-permute-start | bytes 2359304 | tf_op jit(solution)/shard_map/ppermute | solution.py:467
  88.3 11.7 %copy-start.2 = (bf16[256,1536]{1,0:T(8,128)(2,1)}, bf16[256,1536]{1,0:T(8,128)(2,1)S(1)}, u32[]{:S(2)}) copy-start(bf16[256,1536]{1,0:T(8,128)(2,1)S(1)} %collective-permute-done.17.refs_2_) | copy-start | bytes 2359300
  89.9 20.8 %collective-permute-start.20 = (bf16[256,1536]{1,0:T(8,128)(2,1)S(1)}, bf16[256,1536]{1,0:T(8,128)(2,1)S(1)}, u32[]{:S(2)}, u32[]{:S(2)}) collective-permute-start(bf16[256,1536]{1,0:T(8,128)(2,1)S(1)} %add_convert_fusion), channel_id=1, source_target_pairs={{0,16},{8,24},{16,0},{24,8},{1,17},{9,25},{17,1},{25,9},{2,18},{10... | collective-permute-start | bytes 2359304 | tf_op jit(solution)/shard_map/ppermute | solution.py:473
  91.5 19.9 %collective-permute-start.21 = (bf16[256,1536]{1,0:T(8,128)(2,1)}, bf16[256,1536]{1,0:T(8,128)(2,1)S(1)}, u32[]{:S(2)}, u32[]{:S(2)}) collective-permute-start(bf16[256,1536]{1,0:T(8,128)(2,1)} %get-tuple-element.132), channel_id=1, source_target_pairs={{0,8},{8,0},{16,24},{24,16},{1,9},{9,1},{17,25},{25,17},{2,10},{10... | collective-permute-start | bytes 2359304 | tf_op jit(solution)/shard_map/ppermute | solution.py:467
  100.0 10.8 %all-to-all-start = ((f32[8,2,128]{2,1,0:T(2,128)}), f32[8,2,128]{2,1,0:T(2,128)S(1)}, u32[]{:S(2)}, u32[]{:S(2)}) async-start(f32[8,2,128]{2,1,0:T(2,128)} %get-tuple-element.126), calls=%async_computation | async-start | bytes 16384 | tf_op jit(solution)/shard_map/all_to_all | solution.py:524
  104.2 6.5 %copy-start.10 = (s32[128,8]{0,1:T(8,128)S(1)}, s32[128,8]{0,1:T(8,128)}, u32[]{:S(2)}) copy-start(s32[128,8]{0,1:T(8,128)} %param.8) | copy-start | bytes 12292
  110.8 0.9 copy-start
  111.4 0.9 copy-start.1

commit v4 on v3

--- a/solution.py
+++ b/solution.py
@@ -523,11 +523,12 @@
     grad_hidden, grad_slots = back(routed_b, slots, down_weight, saved, width, replicas, seen, late, tables)
     returned = lax.all_to_all(grad_slots, "expert", split_axis=0, concat_axis=0, tiled=True)
     out = rotate([here_keep, here_got] + a_arrived, turns, 0, rows_own, experts_here, None)
-    out, returned, *b_arrived = fence(out, returned, *b_arrived)
+    out, *b_arrived = fence(out, *b_arrived)
+    out = rotate([here_keep_b, here_got_b] + b_arrived, turns, width // BLOCK, rows_own, experts_here, out)
+    returned, out = fence(returned, out)
     of_token = returned.reshape(-1, 1, tokens)
     named = routes.T[None] == jnp.arange(of_token.shape[0], dtype=jnp.int32)[:, None, None]
     grad_prob = jnp.sum(jnp.where(named, of_token, 0.0), axis=0).T
-    out = rotate([here_keep_b, here_got_b] + b_arrived, turns, width // BLOCK, rows_own, experts_here, out)
     return (grad_hidden[None], grad_prob, out)
 
 

time: 116 us -> 114 us (0.983)
  waiting for transfers between devices: 32.7 us -> 30.7 us
    all_to_all x1, waiting for transfers between devices: 3.25 us -> 0.01 us  [shards(): lax.all_to_all(grad_slots, 'expert', split_axis=0, concat_axis=0, tiled=T...]
    ppermute x2, waiting for transfers between devices: 5.31 us -> 6.55 us  [to_chips(): moved.append(lax.ppermute(value[(k - 1) * width:k * width], 'dp', pairs))]
  transfers between devices with their start and end apart: 23 -> 23, of which waited for: 10 -> 10; matrix products, arithmetic and copies ran while one was open for 6% -> 6% of each run, Pallas kernels for 36% -> 40%
where the time goes in v4:
time: 114 us
  Pallas kernels  47.3 us (41%)
  waiting for transfers between devices  30.7 us (27%)
  starting transfers between devices  26.1 us (23%)
  other arithmetic  6.2 us (5%)
  local copies, waits for them, and re-layouts  2.59 us (2%)
    pallas_call x3, Pallas kernels, visit(): pl.pallas_call(functools.partial(visit_kernel, len(parts), len(shares), b...  15.6 us
    ppermute x8, waiting for transfers between devices, across(): return lax.ppermute(value, 'expert', [(i, i ^ 1) for i in range(2 * LINES)])  12.5 us
    ppermute x6, waiting for transfers between devices, along(): lax.ppermute(value, 'expert', [(2 * a + x, 2 * b + x) for a, b in pairs f...  10.2 us
    ppermute x6, starting transfers between devices, along(): lax.ppermute(value, 'expert', [(2 * a + x, 2 * b + x) for a, b in pairs f...  9.38 us
    pallas_call x1, Pallas kernels, back(): pl.pallas_call(functools.partial(back_kernel, replicas, len(seen), len(la...  8.45 us
    ppermute x8, starting transfers between devices, across(): return lax.ppermute(value, 'expert', [(i, i ^ 1) for i in range(2 * LINES)])  8.17 us
    pallas_call x1, Pallas kernels, route(): pl.pallas_call(functools.partial(route_kernel, len(parts), len(tables), w...  8.09 us
    pallas_call x1, Pallas kernels, grad_bands(): pl.pallas_call(functools.partial(bands_kernel, len(wanted), len(routed),...  6.69 us
  transfers between devices with their start and end apart: 23, of which 10 were waited for; matrix products, arithmetic and copies ran while one was open for 6% of the time, Pallas kernels for 40%

profile of v4, /device:TPU:0, one launch (start us, length us, event | category | flops | bytes accessed | tf_op | source)
XLA Modules:
  0.0 113.8 jit_solution(6142825263550616645)
XLA Ops:
  0.6 2.0 %pack.1 = (bf16[128,1152]{1,0:T(8,128)(2,1)}, bf16[128,1024]{1,0:T(8,128)(2,1)}) custom-call(bf16[128,2048]{1,0:T(8,128)(2,1)} %cot_ref.1, bf16[8,128]{1,0:T(8,128)(2,1)} %bitcast.34, s32[8,128]{1,0:T(8,128)} %bitcast.31), custom_call_target="tpu_custom_call" | custom-call | tf_op jit(solution)/shard_map/pack/pallas_call | solution.py:63
  2.6 5.0 %collective-permute-start.3 = (bf16[128,1152]{1,0:T(8,128)(2,1)}, bf16[128,1152]{1,0:T(8,128)(2,1)S(1)}, u32[]{:S(2)}, u32[]{:S(2)}) collective-permute-start(bf16[128,1152]{1,0:T(8,128)(2,1)} %get-tuple-element.74.refs_0_), channel_id=1, source_target_pairs={{0,6},{1,7},{2,0},{3,1},{4,2},{5,3},{6,4},{7,5},{8,14},{9,15},{10,... | collective-permute-start | bytes 884744 | tf_op jit(solution)/shard_map/ppermute | solution.py:76
  7.7 1.5 %collective-permute-start = (bf16[128,1152]{1,0:T(8,128)(2,1)}, bf16[128,1152]{1,0:T(8,128)(2,1)S(1)}, u32[]{:S(2)}, u32[]{:S(2)}) collective-permute-start(bf16[128,1152]{1,0:T(8,128)(2,1)} %get-tuple-element.74.refs_0_), channel_id=1, source_target_pairs={{0,1},{1,0},{2,3},{3,2},{4,5},{5,4},{6,7},{7,6},{8,9},{9,8},{10,11... | collective-permute-start | bytes 884744 | tf_op jit(solution)/shard_map/ppermute | solution.py:80
  9.2 0.5 collective-permute-start.1
  9.7 0.8 fusion.18
  10.5 0.3 fusion.10
  10.8 0.7 pad_add_fusion.owners_ref
  11.4 0.7 stack.55.slots_ref
  12.1 0.9 multiply_convert_fusion.turn_ref
  13.0 8.9 %collective-permute-done.1.refs_1_ = bf16[128,1024]{1,0:T(8,128)(2,1)S(1)} collective-permute-done((bf16[128,1024]{1,0:T(8,128)(2,1)}, bf16[128,1024]{1,0:T(8,128)(2,1)S(1)}, u32[]{:S(2)}, u32[]{:S(2)}) %collective-permute-start.1) | collective-permute-done | bytes 262176 | tf_op jit(solution)/shard_map/ppermute | solution.py:80
  22.0 0.8 collective-permute-start.4
  22.8 1.5 %collective-permute-start.5 = (bf16[128,1152]{1,0:T(8,128)(2,1)S(1)}, bf16[128,1152]{1,0:T(8,128)(2,1)S(1)}, u32[]{:S(2)}, u32[]{:S(2)}) collective-permute-start(bf16[128,1152]{1,0:T(8,128)(2,1)S(1)} %collective-permute-done.2.refs_2_), channel_id=1, source_target_pairs={{0,1},{1,0},{2,3},{3,2},{4,5},{5,4},{6,7},{7,6},{8,9},{9,8},{10,11... | collective-permute-start | bytes 884744 | tf_op jit(solution)/shard_map/ppermute | solution.py:80
  24.3 0.5 collective-permute-start.6
  24.8 6.8 %visit.3 = (bf16[2,384,1024]{2,1,0:T(8,128)(2,1)}, bf16[2,384,768]{2,1,0:T(8,128)(2,1)}, f32[4,8,128]{2,1,0:T(8,128)}, bf16[2,384,768]{2,1,0:T(8,128)(2,1)}) custom-call(s32[8]{0:T(128)} %stack.55.slots_ref, bf16[128,1152]{1,0:T(8,128)(2,1)} %get-tuple-element.74.refs_0_, bf16[128,1152]{1,0:T(8,128)(2,1)} %copy-done.9, bf16[128,1152]{1,0:T(8,128)(2,1)} %copy-done.8, ...), custom_call_target="tpu_custom_call" | custom-call | tf_op jit(solution)/shard_map/visit/pallas_call | solution.py:217
  31.7 5.4 %collective-permute-done.4.refs_0_ = bf16[128,1152]{1,0:T(8,128)(2,1)S(1)} collective-permute-done((bf16[128,1152]{1,0:T(8,128)(2,1)}, bf16[128,1152]{1,0:T(8,128)(2,1)S(1)}, u32[]{:S(2)}, u32[]{:S(2)}) %collective-permute-start.4) | collective-permute-done | bytes 294944 | tf_op jit(solution)/shard_map/ppermute | solution.py:76
  37.1 1.6 %collective-permute-start.7 = (bf16[128,1152]{1,0:T(8,128)(2,1)S(1)}, bf16[128,1152]{1,0:T(8,128)(2,1)S(1)}, u32[]{:S(2)}, u32[]{:S(2)}) collective-permute-start(bf16[128,1152]{1,0:T(8,128)(2,1)S(1)} %collective-permute-done.4.refs_0_), channel_id=1, source_target_pairs={{0,1},{1,0},{2,3},{3,2},{4,5},{5,4},{6,7},{7,6},{8,9},{9,8},{10,11... | collective-permute-start | bytes 884744 | tf_op jit(solution)/shard_map/ppermute | solution.py:80
  38.6 2.2 %collective-permute-start.9 = (bf16[128,1024]{1,0:T(8,128)(2,1)S(1)}, bf16[128,1024]{1,0:T(8,128)(2,1)S(1)}, u32[]{:S(2)}, u32[]{:S(2)}) collective-permute-start(bf16[128,1024]{1,0:T(8,128)(2,1)S(1)} %copy-done.11), channel_id=1, source_target_pairs={{0,6},{1,7},{2,0},{3,1},{4,2},{5,3},{6,4},{7,5},{8,14},{9,15},{10,... | collective-permute-start | bytes 786440 | tf_op jit(solution)/shard_map/ppermute | solution.py:76
  40.9 0.3 collective-permute-start.8
  41.2 5.9 %visit.4 = (bf16[2,288,1024]{2,1,0:T(8,128)(2,1)}, bf16[2,288,768]{2,1,0:T(8,128)(2,1)}, f32[3,8,128]{2,1,0:T(8,128)}, bf16[2,288,768]{2,1,0:T(8,128)(2,1)}) custom-call(s32[8]{0:T(128)} %stack.55.slots_ref, bf16[128,1152]{1,0:T(8,128)(2,1)} %copy-done.3, bf16[128,1152]{1,0:T(8,128)(2,1)} %copy-done.4, bf16[128,1152]{1,0:T(8,128)(2,1)} %copy-done.5, ...), custom_call_target="tpu_custom_call" | custom-call | tf_op jit(solution)/shard_map/visit/pallas_call | solution.py:217
  47.1 0.6 collective-permute-done.9.refs_3_
  47.7 4.2 %collective-permute-done.8.refs_2_ = bf16[128,1024]{1,0:T(8,128)(2,1)S(1)} collective-permute-done((bf16[128,1024]{1,0:T(8,128)(2,1)S(1)}, bf16[128,1024]{1,0:T(8,128)(2,1)S(1)}, u32[]{:S(2)}, u32[]{:S(2)}) %collective-permute-start.8) | collective-permute-done | bytes 262176 | tf_op jit(solution)/shard_map/ppermute | solution.py:76
  51.9 1.0 collective-permute-start.10
  52.9 0.5 collective-permute-start.11
  53.5 1.5 %collective-permute-start.12 = (bf16[128,1024]{1,0:T(8,128)(2,1)S(1)}, bf16[128,1024]{1,0:T(8,128)(2,1)S(1)}, u32[]{:S(2)}, u32[]{:S(2)}) collective-permute-start(bf16[128,1024]{1,0:T(8,128)(2,1)S(1)} %collective-permute-done.9.refs_3_), channel_id=1, source_target_pairs={{0,1},{1,0},{2,3},{3,2},{4,5},{5,4},{6,7},{7,6},{8,9},{9,8},{10,11... | collective-permute-start | bytes 786440 | tf_op jit(solution)/shard_map/ppermute | solution.py:80
  55.0 2.9 %visit.5 = (bf16[2,96,1024]{2,1,0:T(8,128)(2,1)}, bf16[2,96,768]{2,1,0:T(8,128)(2,1)}, f32[1,8,128]{2,1,0:T(8,128)}) custom-call(s32[8]{0:T(128)} %stack.55.slots_ref, bf16[128,1152]{1,0:T(8,128)(2,1)} %copy-done.6, bf16[2,8,96,768]{3,2,1,0:T(8,128)(2,1)} %bitcast.27), custom_call_target="tpu_custom_call" | custom-call | tf_op jit(solution)/shard_map/visit/pallas_call | solution.py:217
  57.9 6.7 %bands.1 = (bf16[128,1536]{1,0:T(8,128)(2,1)}, bf16[128,1536]{1,0:T(8,128)(2,1)}, bf16[256,1536]{1,0:T(8,128)(2,1)}, bf16[256,1536]{1,0:T(8,128)(2,1)}, bf16[256,1536]{1,0:T(8,128)(2,1)}) custom-call(s32[4]{0:T(128)} %pad_add_fusion.owners_ref, bf16[2,384,1024]{2,1,0:T(8,128)(2,1)} %get-tuple-element.95.refs_0_.refs_3_.refs_6_.refs_9_, ...), custom_call_target="tpu_custom_call" | custom-call | tf_op jit(solution)/shard_map/bands/pallas_call | solution.py:279
  64.6 0.2 collective-permute-done.12.refs_6_
  64.8 0.5 collective-permute-start.17
  65.3 0.5 collective-permute-start.13
  65.9 0.9 collective-permute-done.16
  66.8 0.6 collective-permute-done.17
  67.3 1.3 %add_convert_fusion.1 = bf16[256,1536]{1,0:T(8,128)(2,1)S(1)} fusion(bf16[256,1536]{1,0:T(8,128)(2,1)} %get-tuple-element.128, bf16[128,1536]{1,0:T(8,128)(2,1)S(1)} %collective-permute-done.17, bf16[128,1536]{1,0:T(8,128)(2,1)S(1)} %collective-permute-done.16), kind=kLoop, calls=%fused_computation.1 | loop fusion | flops 2752512 | bytes 2359296 | tf_op jit(solution)/shard_map/convert_element_type | solution.py:478
  68.7 1.6 %collective-permute-start.18 = (bf16[256,1536]{1,0:T(8,128)(2,1)S(1)}, bf16[256,1536]{1,0:T(8,128)(2,1)S(1)}, u32[]{:S(2)}, u32[]{:S(2)}) collective-permute-start(bf16[256,1536]{1,0:T(8,128)(2,1)S(1)} %add_convert_fusion.1), channel_id=1, source_target_pairs={{0,16},{8,24},{16,0},{24,8},{1,17},{9,25},{17,1},{25,9},{2,18},{10... | collective-permute-start | bytes 2359304 | tf_op jit(solution)/shard_map/ppermute | solution.py:473
  70.2 3.3 %collective-permute-done.13.refs_7_ = bf16[128,1024]{1,0:T(8,128)(2,1)S(1)} collective-permute-done((bf16[128,1024]{1,0:T(8,128)(2,1)S(1)}, bf16[128,1024]{1,0:T(8,128)(2,1)S(1)}, u32[]{:S(2)}, u32[]{:S(2)}) %collective-permute-start.13) | collective-permute-done | bytes 262176 | tf_op jit(solution)/shard_map/ppermute | solution.py:80
  73.6 0.7 copy-done.18
  74.2 8.1 %route.1 = (bf16[128,1536]{1,0:T(8,128)(2,1)}, bf16[128,1536]{1,0:T(8,128)(2,1)}, bf16[256,1536]{1,0:T(8,128)(2,1)}, bf16[256,1536]{1,0:T(8,128)(2,1)}, bf16[256...) custom-call(s32[4]{0:T(128)} %pad_add_fusion.owners_ref, bf16[128,1024]{1,0:T(8,128)(2,1)} %get-tuple-element.91.refs_0_, ...), custom_call_target="tpu_custom_call" | custom-call | flops 2818572288 | bytes 10000000 | tf_op jit(solution)/shard_map/route/pallas_call | solution.py:326
  82.4 0.5 collective-permute-start.20
  83.0 5.3 %collective-permute-done.18.refs_2_ = bf16[256,1536]{1,0:T(8,128)(2,1)S(1)} collective-permute-done((bf16[256,1536]{1,0:T(8,128)(2,1)S(1)}, bf16[256,1536]{1,0:T(8,128)(2,1)S(1)}, u32[]{:S(2)}, u32[]{:S(2)}) %collective-permute-start.18) | collective-permute-done | bytes 786464 | tf_op jit(solution)/shard_map/ppermute | solution.py:473
  88.3 1.6 %add_convert_fusion = bf16[256,1536]{1,0:T(8,128)(2,1)S(1)} fusion(bf16[256,1536]{1,0:T(8,128)(2,1)} %get-tuple-element.132, bf16[128,1536]{1,0:T(8,128)(2,1)S(1)} %collective-permute-done.20, bf16[128,1536]{1,0:T(8,128)(2,1)S(1)} %collective-permute-done.19), kind=kLoop, calls=%fused_computation | loop fusion | flops 2752512 | bytes 2359296 | tf_op jit(solution)/shard_map/convert_element_type | solution.py:478
  89.9 1.6 %collective-permute-start.21 = (bf16[256,1536]{1,0:T(8,128)(2,1)S(1)}, bf16[256,1536]{1,0:T(8,128)(2,1)S(1)}, u32[]{:S(2)}, u32[]{:S(2)}) collective-permute-start(bf16[256,1536]{1,0:T(8,128)(2,1)S(1)} %add_convert_fusion), channel_id=1, source_target_pairs={{0,16},{8,24},{16,0},{24,8},{1,17},{9,25},{17,1},{25,9},{2,18},{10... | collective-permute-start | bytes 2359304 | tf_op jit(solution)/shard_map/ppermute | solution.py:473
  91.5 8.5 %back.1 = (bf16[2,8,96,768]{3,2,1,0:T(8,128)(2,1)}, f32[8,2,128]{2,1,0:T(2,128)}) custom-call(s32[8]{0:T(128)} %stack.55.slots_ref, bf16[2,768,1024]{2,1,0:T(8,128)(2,1)} %get-tuple-element.115.routed_ref, bf16[2,768,2048]{2,1,0:T(8,128)(2,1)} %refs_7_.3, bf16[2,768,2048]{2,1,0:T(8,128)(2,1)} %refs_7_.3, bf16[2,768,2048]{2,1,0:T(8,128)(2,1)} %refs_7_.3, ...), custom_call_target="tpu_custom_call" | custom-call | tf_op jit(solution)/shard_map/back/pallas_call | solution.py:386
  100.0 4.3 %all-to-all-start = ((f32[8,2,128]{2,1,0:T(2,128)}), f32[8,2,128]{2,1,0:T(2,128)S(1)}, u32[]{:S(2)}, u32[]{:S(2)}) async-start(f32[8,2,128]{2,1,0:T(2,128)} %get-tuple-element.119), calls=%async_computation | async-start | bytes 16384 | tf_op jit(solution)/shard_map/all_to_all | solution.py:524
  104.2 3.2 %rotate.2.refs_3_ = f32[512,2,768]{2,1,0:T(2,128)} custom-call(bf16[4,256,256]{2,1,0:T(8,128)(2,1)} %multiply_convert_fusion.turn_ref, bf16[256,1536]{1,0:T(8,128)(2,1)} %get-tuple-element.123.refs_0_, bf16[256,1536]{1,0:T(8,128)(2,1)} %collective-permute-done.15.refs_1_, bf16[256,1536]{1,0:T(8,128)(2,1)} %copy-done.2), custom_call_target="tpu_custom_call" | custom-call | tf_op jit(solution)/shard_map/rotate/pallas_call | solution.py:425
  107.5 1.2 %collective-permute-done.21.refs_2_ = bf16[256,1536]{1,0:T(8,128)(2,1)S(1)} collective-permute-done((bf16[256,1536]{1,0:T(8,128)(2,1)S(1)}, bf16[256,1536]{1,0:T(8,128)(2,1)S(1)}, u32[]{:S(2)}, u32[]{:S(2)}) %collective-permute-start.21) | collective-permute-done | bytes 786464 | tf_op jit(solution)/shard_map/ppermute | solution.py:473
  108.8 0.9 copy-done
  109.6 0.3 copy-done.1
  109.9 3.3 %rotate.3 = f32[512,2,768]{2,1,0:T(2,128)} custom-call(bf16[4,256,256]{2,1,0:T(8,128)(2,1)} %multiply_convert_fusion.turn_ref, bf16[256,1536]{1,0:T(8,128)(2,1)} %get-tuple-element.121.refs_0_, bf16[256,1536]{1,0:T(8,128)(2,1)} %copy-done.1, bf16[256,1536]{1,0:T(8,128)(2,1)} %copy-done, f32[512,2,768]{2,1,0:T(2,128)} %rotate.2.refs_3_), custom_call_target="tpu_custom_call", output_to_operand_aliasing={{}: (4, {})} | custom-call | tf_op jit(solution)/shard_map/rotate/pallas_call | solution.py:425
  113.2 0.6 select_reduce_fusion
  (57 shorter events, 0.3 us)
Async XLA Ops:
  2.6 19.4 %collective-permute-start.3 = (bf16[128,1152]{1,0:T(8,128)(2,1)}, bf16[128,1152]{1,0:T(8,128)(2,1)S(1)}, u32[]{:S(2)}, u32[]{:S(2)}) collective-permute-start(bf16[128,1152]{1,0:T(8,128)(2,1)} %get-tuple-element.74.refs_0_), channel_id=1, source_target_pairs={{0,6},{1,7},{2,0},{3,1},{4,2},{5,3},{6,4},{7,5},{8,14},{9,15},{10,... | collective-permute-start | bytes 884744 | tf_op jit(solution)/shard_map/ppermute | solution.py:76
  7.7 14.3 %collective-permute-start.2 = (bf16[128,1152]{1,0:T(8,128)(2,1)}, bf16[128,1152]{1,0:T(8,128)(2,1)S(1)}, u32[]{:S(2)}, u32[]{:S(2)}) collective-permute-start(bf16[128,1152]{1,0:T(8,128)(2,1)} %get-tuple-element.74.refs_0_), channel_id=1, source_target_pairs={{0,2},{1,3},{2,4},{3,5},{4,6},{5,7},{6,0},{7,1},{8,10},{9,11},{10,... | collective-permute-start | bytes 884744 | tf_op jit(solution)/shard_map/ppermute | solution.py:76
  7.7 14.3 %collective-permute-start = (bf16[128,1152]{1,0:T(8,128)(2,1)}, bf16[128,1152]{1,0:T(8,128)(2,1)S(1)}, u32[]{:S(2)}, u32[]{:S(2)}) collective-permute-start(bf16[128,1152]{1,0:T(8,128)(2,1)} %get-tuple-element.74.refs_0_), channel_id=1, source_target_pairs={{0,1},{1,0},{2,3},{3,2},{4,5},{5,4},{6,7},{7,6},{8,9},{9,8},{10,11... | collective-permute-start | bytes 884744 | tf_op jit(solution)/shard_map/ppermute | solution.py:80
  9.2 12.8 %collective-permute-start.1 = (bf16[128,1024]{1,0:T(8,128)(2,1)}, bf16[128,1024]{1,0:T(8,128)(2,1)S(1)}, u32[]{:S(2)}, u32[]{:S(2)}) collective-permute-start(bf16[128,1024]{1,0:T(8,128)(2,1)} %get-tuple-element.91.refs_0_), channel_id=1, source_target_pairs={{0,1},{1,0},{2,3},{3,2},{4,5},{5,4},{6,7},{7,6},{8,9},{9,8},{10,11... | collective-permute-start | bytes 786440 | tf_op jit(solution)/shard_map/ppermute | solution.py:80
  22.0 9.7 %copy-start.12 = (bf16[128,1024]{1,0:T(8,128)(2,1)}, bf16[128,1024]{1,0:T(8,128)(2,1)S(1)}, u32[]{:S(2)}) copy-start(bf16[128,1024]{1,0:T(8,128)(2,1)S(1)} %collective-permute-done.1.refs_1_) | copy-start | bytes 786436
  22.0 2.9 %copy-start.7 = (bf16[128,1152]{1,0:T(8,128)(2,1)}, bf16[128,1152]{1,0:T(8,128)(2,1)S(1)}, u32[]{:S(2)}) copy-start(bf16[128,1152]{1,0:T(8,128)(2,1)S(1)} %collective-permute-done.3.refs_3_) | copy-start | bytes 884740
  22.0 2.9 %copy-start.8 = (bf16[128,1152]{1,0:T(8,128)(2,1)}, bf16[128,1152]{1,0:T(8,128)(2,1)S(1)}, u32[]{:S(2)}) copy-start(bf16[128,1152]{1,0:T(8,128)(2,1)S(1)} %collective-permute-done.2.refs_2_) | copy-start | bytes 884740
  22.0 2.8 %copy-start.9 = (bf16[128,1152]{1,0:T(8,128)(2,1)}, bf16[128,1152]{1,0:T(8,128)(2,1)S(1)}, u32[]{:S(2)}) copy-start(bf16[128,1152]{1,0:T(8,128)(2,1)S(1)} %collective-permute-done.refs_1_) | copy-start | bytes 884740
  22.0 15.1 %collective-permute-start.4 = (bf16[128,1152]{1,0:T(8,128)(2,1)}, bf16[128,1152]{1,0:T(8,128)(2,1)S(1)}, u32[]{:S(2)}, u32[]{:S(2)}) collective-permute-start(bf16[128,1152]{1,0:T(8,128)(2,1)} %get-tuple-element.74.refs_0_), channel_id=1, source_target_pairs={{0,4},{1,5},{2,6},{3,7},{4,0},{5,1},{6,2},{7,3},{8,12},{9,13},{10,... | collective-permute-start | bytes 884744 | tf_op jit(solution)/shard_map/ppermute | solution.py:76
  22.8 14.3 %collective-permute-start.5 = (bf16[128,1152]{1,0:T(8,128)(2,1)S(1)}, bf16[128,1152]{1,0:T(8,128)(2,1)S(1)}, u32[]{:S(2)}, u32[]{:S(2)}) collective-permute-start(bf16[128,1152]{1,0:T(8,128)(2,1)S(1)} %collective-permute-done.2.refs_2_), channel_id=1, source_target_pairs={{0,1},{1,0},{2,3},{3,2},{4,5},{5,4},{6,7},{7,6},{8,9},{9,8},{10,11... | collective-permute-start | bytes 884744 | tf_op jit(solution)/shard_map/ppermute | solution.py:80
  24.3 12.8 %collective-permute-start.6 = (bf16[128,1152]{1,0:T(8,128)(2,1)S(1)}, bf16[128,1152]{1,0:T(8,128)(2,1)S(1)}, u32[]{:S(2)}, u32[]{:S(2)}) collective-permute-start(bf16[128,1152]{1,0:T(8,128)(2,1)S(1)} %collective-permute-done.3.refs_3_), channel_id=1, source_target_pairs={{0,1},{1,0},{2,3},{3,2},{4,5},{5,4},{6,7},{7,6},{8,9},{9,8},{10,11... | collective-permute-start | bytes 884744 | tf_op jit(solution)/shard_map/ppermute | solution.py:80
  24.8 13.8 %copy-start.11 = (bf16[128,1024]{1,0:T(8,128)(2,1)S(1)}, bf16[128,1024]{1,0:T(8,128)(2,1)}, u32[]{:S(2)}) copy-start(bf16[128,1024]{1,0:T(8,128)(2,1)} %get-tuple-element.91.refs_0_) | copy-start | bytes 786436
  37.1 4.1 %copy-start.3 = (bf16[128,1152]{1,0:T(8,128)(2,1)}, bf16[128,1152]{1,0:T(8,128)(2,1)S(1)}, u32[]{:S(2)}) copy-start(bf16[128,1152]{1,0:T(8,128)(2,1)S(1)} %collective-permute-done.4.refs_0_) | copy-start | bytes 884740
  37.1 4.1 %copy-start.4 = (bf16[128,1152]{1,0:T(8,128)(2,1)}, bf16[128,1152]{1,0:T(8,128)(2,1)S(1)}, u32[]{:S(2)}) copy-start(bf16[128,1152]{1,0:T(8,128)(2,1)S(1)} %collective-permute-done.5.refs_1_) | copy-start | bytes 884740
  37.1 4.1 %copy-start.5 = (bf16[128,1152]{1,0:T(8,128)(2,1)}, bf16[128,1152]{1,0:T(8,128)(2,1)S(1)}, u32[]{:S(2)}) copy-start(bf16[128,1152]{1,0:T(8,128)(2,1)S(1)} %collective-permute-done.6.refs_2_) | copy-start | bytes 884740
  37.1 14.8 %collective-permute-start.7 = (bf16[128,1152]{1,0:T(8,128)(2,1)S(1)}, bf16[128,1152]{1,0:T(8,128)(2,1)S(1)}, u32[]{:S(2)}, u32[]{:S(2)}) collective-permute-start(bf16[128,1152]{1,0:T(8,128)(2,1)S(1)} %collective-permute-done.4.refs_0_), channel_id=1, source_target_pairs={{0,1},{1,0},{2,3},{3,2},{4,5},{5,4},{6,7},{7,6},{8,9},{9,8},{10,11... | collective-permute-start | bytes 884744 | tf_op jit(solution)/shard_map/ppermute | solution.py:80
  38.6 9.0 %collective-permute-start.9 = (bf16[128,1024]{1,0:T(8,128)(2,1)S(1)}, bf16[128,1024]{1,0:T(8,128)(2,1)S(1)}, u32[]{:S(2)}, u32[]{:S(2)}) collective-permute-start(bf16[128,1024]{1,0:T(8,128)(2,1)S(1)} %copy-done.11), channel_id=1, source_target_pairs={{0,6},{1,7},{2,0},{3,1},{4,2},{5,3},{6,4},{7,5},{8,14},{9,15},{10,... | collective-permute-start | bytes 786440 | tf_op jit(solution)/shard_map/ppermute | solution.py:76
  40.9 11.0 %collective-permute-start.8 = (bf16[128,1024]{1,0:T(8,128)(2,1)S(1)}, bf16[128,1024]{1,0:T(8,128)(2,1)S(1)}, u32[]{:S(2)}, u32[]{:S(2)}) collective-permute-start(bf16[128,1024]{1,0:T(8,128)(2,1)S(1)} %copy-done.11), channel_id=1, source_target_pairs={{0,2},{1,3},{2,4},{3,5},{4,6},{5,7},{6,0},{7,1},{8,10},{9,11},{10,... | collective-permute-start | bytes 786440 | tf_op jit(solution)/shard_map/ppermute | solution.py:76
  47.7 16.9 %copy-start.13 = (bf16[128,1024]{1,0:T(8,128)(2,1)}, bf16[128,1024]{1,0:T(8,128)(2,1)S(1)}, u32[]{:S(2)}) copy-start(bf16[128,1024]{1,0:T(8,128)(2,1)S(1)} %collective-permute-done.9.refs_3_) | copy-start | bytes 786436
  51.9 12.7 %copy-start.14 = (bf16[128,1024]{1,0:T(8,128)(2,1)}, bf16[128,1024]{1,0:T(8,128)(2,1)S(1)}, u32[]{:S(2)}) copy-start(bf16[128,1024]{1,0:T(8,128)(2,1)S(1)} %collective-permute-done.8.refs_2_) | copy-start | bytes 786436
  51.9 3.0 %copy-start.6 = (bf16[128,1152]{1,0:T(8,128)(2,1)}, bf16[128,1152]{1,0:T(8,128)(2,1)S(1)}, u32[]{:S(2)}) copy-start(bf16[128,1152]{1,0:T(8,128)(2,1)S(1)} %collective-permute-done.7.refs_0_) | copy-start | bytes 884740
  51.9 12.7 %collective-permute-start.10 = (bf16[128,1024]{1,0:T(8,128)(2,1)S(1)}, bf16[128,1024]{1,0:T(8,128)(2,1)S(1)}, u32[]{:S(2)}, u32[]{:S(2)}) collective-permute-start(bf16[128,1024]{1,0:T(8,128)(2,1)S(1)} %copy-done.11), channel_id=1, source_target_pairs={{0,4},{1,5},{2,6},{3,7},{4,0},{5,1},{6,2},{7,3},{8,12},{9,13},{10,... | collective-permute-start | bytes 786440 | tf_op jit(solution)/shard_map/ppermute | solution.py:76
  52.9 11.7 %collective-permute-start.11 = (bf16[128,1024]{1,0:T(8,128)(2,1)S(1)}, bf16[128,1024]{1,0:T(8,128)(2,1)S(1)}, u32[]{:S(2)}, u32[]{:S(2)}) collective-permute-start(bf16[128,1024]{1,0:T(8,128)(2,1)S(1)} %collective-permute-done.8.refs_2_), channel_id=1, source_target_pairs={{0,1},{1,0},{2,3},{3,2},{4,5},{5,4},{6,7},{7,6},{8,9},{9,8},{10,11... | collective-permute-start | bytes 786440 | tf_op jit(solution)/shard_map/ppermute | solution.py:80
  53.5 11.4 %collective-permute-start.12 = (bf16[128,1024]{1,0:T(8,128)(2,1)S(1)}, bf16[128,1024]{1,0:T(8,128)(2,1)S(1)}, u32[]{:S(2)}, u32[]{:S(2)}) collective-permute-start(bf16[128,1024]{1,0:T(8,128)(2,1)S(1)} %collective-permute-done.9.refs_3_), channel_id=1, source_target_pairs={{0,1},{1,0},{2,3},{3,2},{4,5},{5,4},{6,7},{7,6},{8,9},{9,8},{10,11... | collective-permute-start | bytes 786440 | tf_op jit(solution)/shard_map/ppermute | solution.py:80
  64.6 9.0 %copy-start.15 = (bf16[128,1024]{1,0:T(8,128)(2,1)}, bf16[128,1024]{1,0:T(8,128)(2,1)S(1)}, u32[]{:S(2)}) copy-start(bf16[128,1024]{1,0:T(8,128)(2,1)S(1)} %collective-permute-done.10.refs_4_) | copy-start | bytes 786436
  64.6 9.0 %copy-start.16 = (bf16[128,1024]{1,0:T(8,128)(2,1)}, bf16[128,1024]{1,0:T(8,128)(2,1)S(1)}, u32[]{:S(2)}) copy-start(bf16[128,1024]{1,0:T(8,128)(2,1)S(1)} %collective-permute-done.11.refs_5_) | copy-start | bytes 786436
  64.8 8.7 %copy-start.17 = (bf16[128,1024]{1,0:T(8,128)(2,1)}, bf16[128,1024]{1,0:T(8,128)(2,1)S(1)}, u32[]{:S(2)}) copy-start(bf16[128,1024]{1,0:T(8,128)(2,1)S(1)} %collective-permute-done.12.refs_6_) | copy-start | bytes 786436
  64.8 1.9 %collective-permute-start.16 = (bf16[128,1536]{1,0:T(8,128)(2,1)}, bf16[128,1536]{1,0:T(8,128)(2,1)S(1)}, u32[]{:S(2)}, u32[]{:S(2)}) collective-permute-start(bf16[128,1536]{1,0:T(8,128)(2,1)} %get-tuple-element.126), channel_id=1, source_target_pairs={{0,8},{8,0},{16,24},{24,16},{1,9},{9,1},{17,25},{25,17},{2,10},{10... | collective-permute-start | bytes 1179656 | tf_op jit(solution)/shard_map/ppermute | solution.py:467
  64.8 2.5 %collective-permute-start.17 = (bf16[128,1536]{1,0:T(8,128)(2,1)}, bf16[128,1536]{1,0:T(8,128)(2,1)S(1)}, u32[]{:S(2)}, u32[]{:S(2)}) collective-permute-start(bf16[128,1536]{1,0:T(8,128)(2,1)} %get-tuple-element.127), channel_id=1, source_target_pairs={{0,8},{8,0},{16,24},{24,16},{1,9},{9,1},{17,25},{25,17},{2,10},{10... | collective-permute-start | bytes 1179656 | tf_op jit(solution)/shard_map/ppermute | solution.py:467
  65.3 8.2 %collective-permute-start.13 = (bf16[128,1024]{1,0:T(8,128)(2,1)S(1)}, bf16[128,1024]{1,0:T(8,128)(2,1)S(1)}, u32[]{:S(2)}, u32[]{:S(2)}) collective-permute-start(bf16[128,1024]{1,0:T(8,128)(2,1)S(1)} %collective-permute-done.10.refs_4_), channel_id=1, source_target_pairs={{0,1},{1,0},{2,3},{3,2},{4,5},{5,4},{6,7},{7,6},{8,9},{9,8},{10,11... | collective-permute-start | bytes 786440 | tf_op jit(solution)/shard_map/ppermute | solution.py:80
  68.7 19.6 %collective-permute-start.18 = (bf16[256,1536]{1,0:T(8,128)(2,1)S(1)}, bf16[256,1536]{1,0:T(8,128)(2,1)S(1)}, u32[]{:S(2)}, u32[]{:S(2)}) collective-permute-start(bf16[256,1536]{1,0:T(8,128)(2,1)S(1)} %add_convert_fusion.1), channel_id=1, source_target_pairs={{0,16},{8,24},{16,0},{24,8},{1,17},{9,25},{17,1},{25,9},{2,18},{10... | collective-permute-start | bytes 2359304 | tf_op jit(solution)/shard_map/ppermute | solution.py:473
  73.6 0.7 copy-start.18
  82.3 6.0 %collective-permute-start.19 = (bf16[128,1536]{1,0:T(8,128)(2,1)}, bf16[128,1536]{1,0:T(8,128)(2,1)S(1)}, u32[]{:S(2)}, u32[]{:S(2)}) collective-permute-start(bf16[128,1536]{1,0:T(8,128)(2,1)} %get-tuple-element.130), channel_id=1, source_target_pairs={{0,8},{8,0},{16,24},{24,16},{1,9},{9,1},{17,25},{25,17},{2,10},{10... | collective-permute-start | bytes 1179656 | tf_op jit(solution)/shard_map/ppermute | solution.py:467
  82.4 5.9 %collective-permute-start.20 = (bf16[128,1536]{1,0:T(8,128)(2,1)}, bf16[128,1536]{1,0:T(8,128)(2,1)S(1)}, u32[]{:S(2)}, u32[]{:S(2)}) collective-permute-start(bf16[128,1536]{1,0:T(8,128)(2,1)} %get-tuple-element.131), channel_id=1, source_target_pairs={{0,8},{8,0},{16,24},{24,16},{1,9},{9,1},{17,25},{25,17},{2,10},{10... | collective-permute-start | bytes 1179656 | tf_op jit(solution)/shard_map/ppermute | solution.py:467
  82.9 21.3 %collective-permute-start.15 = (bf16[256,1536]{1,0:T(8,128)(2,1)}, bf16[256,1536]{1,0:T(8,128)(2,1)}, u32[]{:S(2)}, u32[]{:S(2)}) collective-permute-start(bf16[256,1536]{1,0:T(8,128)(2,1)} %get-tuple-element.124), channel_id=1, source_target_pairs={{0,8},{8,0},{16,24},{24,16},{1,9},{9,1},{17,25},{25,17},{2,10},{10... | collective-permute-start | bytes 2359304 | tf_op jit(solution)/shard_map/ppermute | solution.py:467
  88.3 11.7 %copy-start.2 = (bf16[256,1536]{1,0:T(8,128)(2,1)}, bf16[256,1536]{1,0:T(8,128)(2,1)S(1)}, u32[]{:S(2)}) copy-start(bf16[256,1536]{1,0:T(8,128)(2,1)S(1)} %collective-permute-done.18.refs_2_) | copy-start | bytes 2359300
  89.9 18.8 %collective-permute-start.21 = (bf16[256,1536]{1,0:T(8,128)(2,1)S(1)}, bf16[256,1536]{1,0:T(8,128)(2,1)S(1)}, u32[]{:S(2)}, u32[]{:S(2)}) collective-permute-start(bf16[256,1536]{1,0:T(8,128)(2,1)S(1)} %add_convert_fusion), channel_id=1, source_target_pairs={{0,16},{8,24},{16,0},{24,8},{1,17},{9,25},{17,1},{25,9},{2,18},{10... | collective-permute-start | bytes 2359304 | tf_op jit(solution)/shard_map/ppermute | solution.py:473
  91.5 17.2 %collective-permute-start.14 = (bf16[256,1536]{1,0:T(8,128)(2,1)}, bf16[256,1536]{1,0:T(8,128)(2,1)S(1)}, u32[]{:S(2)}, u32[]{:S(2)}) collective-permute-start(bf16[256,1536]{1,0:T(8,128)(2,1)} %get-tuple-element.122), channel_id=1, source_target_pairs={{0,8},{8,0},{16,24},{24,16},{1,9},{9,1},{17,25},{25,17},{2,10},{10... | collective-permute-start | bytes 2359304 | tf_op jit(solution)/shard_map/ppermute | solution.py:467
  100.0 13.2 %all-to-all-start = ((f32[8,2,128]{2,1,0:T(2,128)}), f32[8,2,128]{2,1,0:T(2,128)S(1)}, u32[]{:S(2)}, u32[]{:S(2)}) async-start(f32[8,2,128]{2,1,0:T(2,128)} %get-tuple-element.119), calls=%async_computation | async-start | bytes 16384 | tf_op jit(solution)/shard_map/all_to_all | solution.py:524
  108.7 0.9 copy-start
  108.8 1.2 %copy-start.1 = (bf16[256,1536]{1,0:T(8,128)(2,1)}, bf16[256,1536]{1,0:T(8,128)(2,1)S(1)}, u32[]{:S(2)}) copy-start(bf16[256,1536]{1,0:T(8,128)(2,1)S(1)} %collective-permute-done.14.refs_1_) | copy-start | bytes 2359300
  109.9 3.3 %copy-start.10 = (s32[128,8]{0,1:T(8,128)S(1)}, s32[128,8]{0,1:T(8,128)}, u32[]{:S(2)}) copy-start(s32[128,8]{0,1:T(8,128)} %param.8) | copy-start | bytes 12292

commit v5 on v4

--- a/solution.py
+++ b/solution.py
@@ -12,7 +12,7 @@
 LANES = 128
 CORES = 2
 NO_SLOT = 512.0
-VMEM = 56 * 1024 * 1024
+VMEM = 32 * 1024 * 1024
 F32 = jnp.float32
 BF16 = jnp.bfloat16
 
@@ -493,12 +493,13 @@
         a_opp, a_xnext, a_xprev, a_near, b = fence(a_opp, a_xnext, a_xprev, a_near, b)
         a_xopp, b_next, b_prev = across(a_opp), along(b, 1), along(b, -1)
         a_far = visit_first([a_opp, a_xnext, a_xprev], 4)
-        a_xopp, b_next, b_prev, a_far, b = fence(a_xopp, b_next, b_prev, a_far, b)
-        b_opp, b_xnext, b_xprev = along(b, 2), across(b_next), across(b_prev)
+        a_xopp, a_far, b = fence(a_xopp, a_far, b)
         a_made = [a_near, a_far, visit_first([a_xopp], 7, with_product=False)]
         made = bands_first(a_made, away_bands + here_bands)
-        b_opp, b_xnext, b_xprev, made = fence(b_opp, b_xnext, b_xprev, made)
+        b_next, b_prev, made, b = fence(b_next, b_prev, made, b)
+        b_opp, b_xnext, b_xprev = along(b, 2), across(b_next), across(b_prev)
         *away_send, away_keep, here_send, here_keep = made
+        b_opp, b_xnext, b_xprev = fence(b_opp, b_xnext, b_xprev)
         b_xopp = across(b_opp)
         a_arrived = to_chips(add_swapped(away_send, away_keep))
         b_xopp, here_send = fence(b_xopp, here_send)
@@ -516,8 +517,8 @@
     weighted = [made[1] for made in a_made]
     tables = [made[2] for made in a_made]
     made = route(b_parts, tables, weighted, owned, away_bands + here_bands)
+    made, a_arrived = fence(made, a_arrived)
     *away_send, away_keep, here_send_b, here_keep_b, routed_b = made
-    away_keep, a_arrived = fence(away_keep, a_arrived)
     b_arrived = to_chips(add_swapped(away_send, away_keep))
     here_got, here_got_b = swap(here_send), swap(here_send_b)
     grad_hidden, grad_slots = back(routed_b, slots, down_weight, saved, width, replicas, seen, late, tables)

time: 114 us -> 107 us (0.939)
  Pallas kernels: 47.3 us -> 30.4 us
  local copies, waits for them, and re-layouts: 2.59 us -> 9.23 us
  waiting for transfers between devices: 30.7 us -> 35.8 us
  other arithmetic: 6.2 us -> 3.15 us
  starting transfers between devices: 26.1 us -> 27.6 us
    pallas_call x3, Pallas kernels: 15.6 us -> 8 us  [visit(): pl.pallas_call(functools.partial(visit_kernel, len(parts), len(shares), b...]
    unnamed x40 -> x26, local copies, waits for them, and re-layouts: 1.93 us -> 9.14 us
    ppermute x8, waiting for transfers between devices: 12.5 us -> 17.4 us  [across(): return lax.ppermute(value, 'expert', [(i, i ^ 1) for i in range(2 * LINES)])]
    ppermute x2, waiting for transfers between devices: 6.55 us -> 2.25 us  [to_chips(): moved.append(lax.ppermute(value[(k - 1) * width:k * width], 'dp', pairs))]
    ppermute x6, waiting for transfers between devices: 10.2 us -> 13.9 us  [along(): lax.ppermute(value, 'expert', [(2 * a + x, 2 * b + x) for a, b in pairs f...]
    pallas_call x1, Pallas kernels: 8.09 us -> 5.93 us  [route(): pl.pallas_call(functools.partial(route_kernel, len(parts), len(tables), w...]
    pallas_call x1, Pallas kernels: 8.45 us -> 6.34 us  [back(): pl.pallas_call(functools.partial(back_kernel, replicas, len(seen), len(la...]
    pallas_call x1, Pallas kernels: 1.98 us -> 0.22 us  [pack(): pl.pallas_call(functools.partial(pack_kernel, pieces, replicas), out_shap...]
  transfers between devices with their start and end apart: 23 -> 23, of which waited for: 10 -> 9; matrix products, arithmetic and copies ran while one was open for 6% -> 2% of each run, Pallas kernels for 40% -> 28%
where the time goes in v5:
time: 107 us
  waiting for transfers between devices  35.8 us (33%)
  Pallas kernels  30.4 us (28%)
  starting transfers between devices  27.6 us (26%)
  local copies, waits for them, and re-layouts  9.23 us (9%)
  other arithmetic  3.15 us (3%)
    ppermute x8, waiting for transfers between devices, across(): return lax.ppermute(value, 'expert', [(i, i ^ 1) for i in range(2 * LINES)])  17.4 us
    ppermute x6, waiting for transfers between devices, along(): lax.ppermute(value, 'expert', [(2 * a + x, 2 * b + x) for a, b in pairs f...  13.9 us
    ppermute x6, starting transfers between devices, along(): lax.ppermute(value, 'expert', [(2 * a + x, 2 * b + x) for a, b in pairs f...  9.94 us
    unnamed x26, local copies, waits for them, and re-layouts  9.14 us
    ppermute x8, starting transfers between devices, across(): return lax.ppermute(value, 'expert', [(i, i ^ 1) for i in range(2 * LINES)])  8.89 us
    pallas_call x3, Pallas kernels, visit(): pl.pallas_call(functools.partial(visit_kernel, len(parts), len(shares), b...  8 us
    pallas_call x1, Pallas kernels, back(): pl.pallas_call(functools.partial(back_kernel, replicas, len(seen), len(la...  6.34 us
    pallas_call x1, Pallas kernels, route(): pl.pallas_call(functools.partial(route_kernel, len(parts), len(tables), w...  5.93 us
  transfers between devices with their start and end apart: 23, of which 9 were waited for; matrix products, arithmetic and copies ran while one was open for 2% of the time, Pallas kernels for 28%

profile of v5, /device:TPU:0, one launch (start us, length us, event | category | flops | bytes accessed | tf_op | source)
XLA Modules:
  0.0 107.0 jit_solution(11782751580438335104)
XLA Ops:
  0.6 1.0 copy-done.8
  1.7 0.7 copy-done.9
  2.4 0.7 copy-done.11
  3.0 0.2 pack.1
  3.3 5.1 %collective-permute-start.3 = (bf16[128,1152]{1,0:T(8,128)(2,1)S(1)}, bf16[128,1152]{1,0:T(8,128)(2,1)S(1)}, u32[]{:S(2)}, u32[]{:S(2)}) collective-permute-start(bf16[128,1152]{1,0:T(8,128)(2,1)S(1)} %get-tuple-element.80.refs_0_), channel_id=1, source_target_pairs={{0,6},{1,7},{2,0},{3,1},{4,2},{5,3},{6,4},{7,5},{8,14},{9,15},{10,... | collective-permute-start | bytes 884744 | tf_op jit(solution)/shard_map/ppermute | solution.py:76
  8.4 1.5 %collective-permute-start = (bf16[128,1152]{1,0:T(8,128)(2,1)S(1)}, bf16[128,1152]{1,0:T(8,128)(2,1)S(1)}, u32[]{:S(2)}, u32[]{:S(2)}) collective-permute-start(bf16[128,1152]{1,0:T(8,128)(2,1)S(1)} %get-tuple-element.80.refs_0_), channel_id=1, source_target_pairs={{0,1},{1,0},{2,3},{3,2},{4,5},{5,4},{6,7},{7,6},{8,9},{9,8},{10,11... | collective-permute-start | bytes 884744 | tf_op jit(solution)/shard_map/ppermute | solution.py:80
  9.8 0.5 collective-permute-start.1
  10.4 0.8 fusion.18
  11.2 0.3 fusion.10
  11.8 10.7 %collective-permute-done.1.refs_1_ = bf16[128,1024]{1,0:T(8,128)(2,1)S(1)} collective-permute-done((bf16[128,1024]{1,0:T(8,128)(2,1)S(1)}, bf16[128,1024]{1,0:T(8,128)(2,1)S(1)}, u32[]{:S(2)}, u32[]{:S(2)}) %collective-permute-start.1) | collective-permute-done | bytes 262176 | tf_op jit(solution)/shard_map/ppermute | solution.py:80
  22.5 0.8 collective-permute-start.4
  23.2 1.5 %collective-permute-start.5 = (bf16[128,1152]{1,0:T(8,128)(2,1)S(1)}, bf16[128,1152]{1,0:T(8,128)(2,1)S(1)}, u32[]{:S(2)}, u32[]{:S(2)}) collective-permute-start(bf16[128,1152]{1,0:T(8,128)(2,1)S(1)} %collective-permute-done.2.refs_2_), channel_id=1, source_target_pairs={{0,1},{1,0},{2,3},{3,2},{4,5},{5,4},{6,7},{7,6},{8,9},{9,8},{10,11... | collective-permute-start | bytes 884744 | tf_op jit(solution)/shard_map/ppermute | solution.py:80
  24.7 0.5 collective-permute-start.6
  25.3 2.8 %copy-done = bf16[2,768,2048]{2,1,0:T(8,128)(2,1)S(1)} copy-done((bf16[2,768,2048]{2,1,0:T(8,128)(2,1)S(1)}, bf16[2,768,2048]{2,1,0:T(8,128)(2,1)}, u32[]{:S(2)}) %copy-start) | copy-done | bytes 6291480
  28.1 1.7 %copy-done.2 = bf16[1,2,8,96,768]{4,3,2,1,0:T(8,128)(2,1)S(1)} copy-done((bf16[1,2,8,96,768]{4,3,2,1,0:T(8,128)(2,1)S(1)}, bf16[1,2,8,96,768]{4,3,2,1,0:T(8,128)(2,1)}, u32[]{:S(2)}) %copy-start.2) | copy-done | bytes 2359320
  29.7 3.6 %visit.3 = (bf16[2,384,1024]{2,1,0:T(8,128)(2,1)S(1)}, bf16[2,384,768]{2,1,0:T(8,128)(2,1)S(1)}, f32[4,8,128]{2,1,0:T(8,128)S(1)}, bf16[2,384,768]{2,1,0:T(8,128)(2,1)S(1)}) custom-call(s32[8]{0:T(128)S(1)} %stack.55.slots_ref, bf16[128,1152]{1,0:T(8,128)(2,1)S(1)} %get-tuple-element.80.refs_0_, bf16[128,1152]{1,0:T(8,128)(2,1)S(1)} %collective-permute-done.refs_1_, ...), custom_call_target="tpu_custom_call" | custom-call | tf_op jit(solution)/shard_map/visit/pallas_call | solution.py:217
  33.4 3.9 %collective-permute-done.4.refs_0_ = bf16[128,1152]{1,0:T(8,128)(2,1)S(1)} collective-permute-done((bf16[128,1152]{1,0:T(8,128)(2,1)S(1)}, bf16[128,1152]{1,0:T(8,128)(2,1)S(1)}, u32[]{:S(2)}, u32[]{:S(2)}) %collective-permute-start.4) | collective-permute-done | bytes 294944 | tf_op jit(solution)/shard_map/ppermute | solution.py:76
  37.3 1.5 %collective-permute-start.9 = (bf16[128,1152]{1,0:T(8,128)(2,1)S(1)}, bf16[128,1152]{1,0:T(8,128)(2,1)S(1)}, u32[]{:S(2)}, u32[]{:S(2)}) collective-permute-start(bf16[128,1152]{1,0:T(8,128)(2,1)S(1)} %collective-permute-done.4.refs_0_), channel_id=1, source_target_pairs={{0,1},{1,0},{2,3},{3,2},{4,5},{5,4},{6,7},{7,6},{8,9},{9,8},{10,11... | collective-permute-start | bytes 884744 | tf_op jit(solution)/shard_map/ppermute | solution.py:80
  38.8 2.5 %collective-permute-start.8 = (bf16[128,1024]{1,0:T(8,128)(2,1)S(1)}, bf16[128,1024]{1,0:T(8,128)(2,1)S(1)}, u32[]{:S(2)}, u32[]{:S(2)}) collective-permute-start(bf16[128,1024]{1,0:T(8,128)(2,1)S(1)} %get-tuple-element.110.refs_0_), channel_id=1, source_target_pairs={{0,6},{1,7},{2,0},{3,1},{4,2},{5,3},{6,4},{7,5},{8,14},{9,15},{10,... | collective-permute-start | bytes 786440 | tf_op jit(solution)/shard_map/ppermute | solution.py:76
  41.3 0.3 collective-permute-start.7
  41.6 3.1 %visit.4 = (bf16[2,288,1024]{2,1,0:T(8,128)(2,1)S(1)}, bf16[2,288,768]{2,1,0:T(8,128)(2,1)S(1)}, f32[3,8,128]{2,1,0:T(8,128)S(1)}, bf16[2,288,768]{2,1,0:T(8,128)(2,1)S(1)}) custom-call(s32[8]{0:T(128)S(1)} %stack.55.slots_ref, bf16[128,1152]{1,0:T(8,128)(2,1)S(1)} %collective-permute-done.4.refs_0_, bf16[128,1152]{1,0:T(8,128)(2,1)S(1)} %collective-permute-done.5.refs_1_, ...), custom_call_target="tpu_custom_call" | custom-call | tf_op jit(solution)/shard_map/visit/pallas_call | solution.py:217
  44.7 0.7 collective-permute-done.9.refs_0_
  45.4 1.3 %visit.5 = (bf16[2,96,1024]{2,1,0:T(8,128)(2,1)S(1)}, bf16[2,96,768]{2,1,0:T(8,128)(2,1)S(1)}, f32[1,8,128]{2,1,0:T(8,128)S(1)}) custom-call(s32[8]{0:T(128)S(1)} %stack.55.slots_ref, bf16[128,1152]{1,0:T(8,128)(2,1)S(1)} %collective-permute-done.9.refs_0_, bf16[2,8,96,768]{3,2,1,0:T(8,128)(2,1)S(1)} %bitcast.27), custom_call_target="tpu_custom_call" | custom-call | tf_op jit(solution)/shard_map/visit/pallas_call | solution.py:217
  46.7 5.1 %bands.1 = (bf16[128,1536]{1,0:T(8,128)(2,1)S(1)}, bf16[128,1536]{1,0:T(8,128)(2,1)S(1)}, bf16[256,1536]{1,0:T(8,128)(2,1)S(1)}, bf16[256,1536]{1,0:T(8,128)(2,1)}, bf16[256,1536]{1,0:T(8,128)(2,1)S(1)}) custom-call(s32[4]{0:T(128)S(1)} %pad_add_fusion.owners_ref, bf16[2,384,1024]{2,1,0:T(8,128)(2,1)S(1)} %get-tuple-element.90.refs_0_.refs_3_.refs_6_.refs_9_, ...), custom_call_target="tpu_custom_call" | custom-call | tf_op jit(solution)/shard_map/bands/pallas_call | solution.py:279
  51.8 0.3 collective-permute-done.7.refs_2_
  52.1 0.5 collective-permute-start.15
  52.6 1.2 %collective-permute-start.10 = (bf16[128,1024]{1,0:T(8,128)(2,1)S(1)}, bf16[128,1024]{1,0:T(8,128)(2,1)S(1)}, u32[]{:S(2)}, u32[]{:S(2)}) collective-permute-start(bf16[128,1024]{1,0:T(8,128)(2,1)S(1)} %get-tuple-element.110.refs_0_), channel_id=1, source_target_pairs={{0,4},{1,5},{2,6},{3,7},{4,0},{5,1},{6,2},{7,3},{8,12},{9,13},{10,... | collective-permute-start | bytes 786440 | tf_op jit(solution)/shard_map/ppermute | solution.py:76
  53.8 0.5 collective-permute-start.11
  54.3 1.5 %collective-permute-start.12 = (bf16[128,1024]{1,0:T(8,128)(2,1)S(1)}, bf16[128,1024]{1,0:T(8,128)(2,1)S(1)}, u32[]{:S(2)}, u32[]{:S(2)}) collective-permute-start(bf16[128,1024]{1,0:T(8,128)(2,1)S(1)} %collective-permute-done.8.refs_3_), channel_id=1, source_target_pairs={{0,1},{1,0},{2,3},{3,2},{4,5},{5,4},{6,7},{7,6},{8,9},{9,8},{10,11... | collective-permute-start | bytes 786440 | tf_op jit(solution)/shard_map/ppermute | solution.py:80
  55.8 0.2 add_convert_fusion.1
  56.0 1.6 %collective-permute-start.16 = (bf16[256,1536]{1,0:T(8,128)(2,1)S(1)}, bf16[256,1536]{1,0:T(8,128)(2,1)S(1)}, u32[]{:S(2)}, u32[]{:S(2)}) collective-permute-start(bf16[256,1536]{1,0:T(8,128)(2,1)S(1)} %add_convert_fusion.1), channel_id=1, source_target_pairs={{0,16},{8,24},{16,0},{24,8},{1,17},{9,25},{17,1},{25,9},{2,18},{10... | collective-permute-start | bytes 2359304 | tf_op jit(solution)/shard_map/ppermute | solution.py:473
  57.6 9.7 %collective-permute-done.10.refs_4_ = bf16[128,1024]{1,0:T(8,128)(2,1)S(1)} collective-permute-done((bf16[128,1024]{1,0:T(8,128)(2,1)S(1)}, bf16[128,1024]{1,0:T(8,128)(2,1)S(1)}, u32[]{:S(2)}, u32[]{:S(2)}) %collective-permute-start.10) | collective-permute-done | bytes 262176 | tf_op jit(solution)/shard_map/ppermute | solution.py:76
  67.4 1.3 %collective-permute-start.13 = (bf16[128,1024]{1,0:T(8,128)(2,1)S(1)}, bf16[128,1024]{1,0:T(8,128)(2,1)S(1)}, u32[]{:S(2)}, u32[]{:S(2)}) collective-permute-start(bf16[128,1024]{1,0:T(8,128)(2,1)S(1)} %collective-permute-done.10.refs_4_), channel_id=1, source_target_pairs={{0,1},{1,0},{2,3},{3,2},{4,5},{5,4},{6,7},{7,6},{8,9},{9,8},{10,11... | collective-permute-start | bytes 786440 | tf_op jit(solution)/shard_map/ppermute | solution.py:80
  68.7 6.0 %collective-permute-done.13.refs_7_ = bf16[128,1024]{1,0:T(8,128)(2,1)S(1)} collective-permute-done((bf16[128,1024]{1,0:T(8,128)(2,1)S(1)}, bf16[128,1024]{1,0:T(8,128)(2,1)S(1)}, u32[]{:S(2)}, u32[]{:S(2)}) %collective-permute-start.13) | collective-permute-done | bytes 262176 | tf_op jit(solution)/shard_map/ppermute | solution.py:80
  74.7 5.9 %route.1 = (bf16[128,1536]{1,0:T(8,128)(2,1)S(1)}, bf16[128,1536]{1,0:T(8,128)(2,1)S(1)}, bf16[256,1536]{1,0:T(8,128)(2,1)S(1)}, bf16[256,1536]{1,0:T(8,128)(2,1...) custom-call(s32[4]{0:T(128)S(1)} %pad_add_fusion.owners_ref, ...), custom_call_target="tpu_custom_call" | custom-call | flops 2818572288 | bytes 10000000 | tf_op jit(solution)/shard_map/route/pallas_call | solution.py:326
  80.7 0.5 collective-permute-start.20
  81.3 1.1 %collective-permute-done.19 = bf16[128,1536]{1,0:T(8,128)(2,1)S(1)} collective-permute-done((bf16[128,1536]{1,0:T(8,128)(2,1)S(1)}, bf16[128,1536]{1,0:T(8,128)(2,1)S(1)}, u32[]{:S(2)}, u32[]{:S(2)}) %collective-permute-start.19) | collective-permute-done | bytes 393248 | tf_op jit(solution)/shard_map/ppermute | solution.py:467
  82.4 1.1 %collective-permute-done.20 = bf16[128,1536]{1,0:T(8,128)(2,1)S(1)} collective-permute-done((bf16[128,1536]{1,0:T(8,128)(2,1)S(1)}, bf16[128,1536]{1,0:T(8,128)(2,1)S(1)}, u32[]{:S(2)}, u32[]{:S(2)}) %collective-permute-start.20) | collective-permute-done | bytes 393248 | tf_op jit(solution)/shard_map/ppermute | solution.py:467
  83.6 1.1 %add_convert_fusion = bf16[256,1536]{1,0:T(8,128)(2,1)} fusion(bf16[256,1536]{1,0:T(8,128)(2,1)S(1)} %get-tuple-element.144, bf16[128,1536]{1,0:T(8,128)(2,1)S(1)} %collective-permute-done.20, bf16[128,1536]{1,0:T(8,128)(2,1)S(1)} %collective-permute-done.19), kind=kLoop, calls=%fused_computation | loop fusion | flops 2752512 | bytes 2359296 | tf_op jit(solution)/shard_map/convert_element_type | solution.py:478
  84.7 1.6 %collective-permute-start.21 = (bf16[256,1536]{1,0:T(8,128)(2,1)}, bf16[256,1536]{1,0:T(8,128)(2,1)S(1)}, u32[]{:S(2)}, u32[]{:S(2)}) collective-permute-start(bf16[256,1536]{1,0:T(8,128)(2,1)} %add_convert_fusion), channel_id=1, source_target_pairs={{0,16},{8,24},{16,0},{24,8},{1,17},{9,25},{17,1},{25,9},{2,18},{10... | collective-permute-start | bytes 2359304 | tf_op jit(solution)/shard_map/ppermute | solution.py:473
  86.2 6.3 %back.1 = (bf16[2,8,96,768]{3,2,1,0:T(8,128)(2,1)}, f32[8,2,128]{2,1,0:T(2,128)}) custom-call(s32[8]{0:T(128)S(1)} %stack.55.slots_ref, bf16[2,768,1024]{2,1,0:T(8,128)(2,1)S(1)} %get-tuple-element.131.routed_ref, bf16[2,768,2048]{2,1,0:T(8,128)(2,1)S(1)} %copy-done.1, bf16[2,768,2048]{2,1,0:T(8,128)(2,1)S(1)} %copy-done.1, ...), custom_call_target="tpu_custom_call" | custom-call | tf_op jit(solution)/shard_map/back/pallas_call | solution.py:386
  92.6 4.5 %all-to-all-start = ((f32[8,2,128]{2,1,0:T(2,128)}), f32[8,2,128]{2,1,0:T(2,128)S(1)}, u32[]{:S(2)}, u32[]{:S(2)}) async-start(f32[8,2,128]{2,1,0:T(2,128)} %get-tuple-element.135), calls=%async_computation | async-start | bytes 16384 | tf_op jit(solution)/shard_map/all_to_all | solution.py:525
  97.0 1.1 %copy-done.5 = bf16[256,1536]{1,0:T(8,128)(2,1)S(1)} copy-done((bf16[256,1536]{1,0:T(8,128)(2,1)S(1)}, bf16[256,1536]{1,0:T(8,128)(2,1)}, u32[]{:S(2)}) %copy-start.5) | copy-done | bytes 786456
  98.2 1.1 %copy-done.7 = bf16[256,1536]{1,0:T(8,128)(2,1)S(1)} copy-done((bf16[256,1536]{1,0:T(8,128)(2,1)S(1)}, bf16[256,1536]{1,0:T(8,128)(2,1)}, u32[]{:S(2)}) %copy-start.7) | copy-done | bytes 786456
  99.3 2.9 %rotate.2.refs_3_ = f32[512,2,768]{2,1,0:T(2,128)} custom-call(bf16[4,256,256]{2,1,0:T(8,128)(2,1)S(1)} %multiply_convert_fusion.turn_ref, bf16[256,1536]{1,0:T(8,128)(2,1)S(1)} %copy-done.5, bf16[256,1536]{1,0:T(8,128)(2,1)} %collective-permute-done.18.refs_1_, bf16[256,1536]{1,0:T(8,128)(2,1)S(1)} %copy-done.7), custom_call_target="tpu_custom_call" | custom-call | tf_op jit(solution)/shard_map/rotate/pallas_call | solution.py:425
  102.2 2.2 %collective-permute-done.21.refs_2_ = bf16[256,1536]{1,0:T(8,128)(2,1)S(1)} collective-permute-done((bf16[256,1536]{1,0:T(8,128)(2,1)}, bf16[256,1536]{1,0:T(8,128)(2,1)S(1)}, u32[]{:S(2)}, u32[]{:S(2)}) %collective-permute-start.21) | collective-permute-done | bytes 786464 | tf_op jit(solution)/shard_map/ppermute | solution.py:473
  104.5 1.9 %rotate.3 = f32[512,2,768]{2,1,0:T(2,128)} custom-call(bf16[4,256,256]{2,1,0:T(8,128)(2,1)S(1)} %multiply_convert_fusion.turn_ref, bf16[256,1536]{1,0:T(8,128)(2,1)S(1)} %get-tuple-element.137.refs_0_, bf16[256,1536]{1,0:T(8,128)(2,1)S(1)} %collective-permute-done.17.refs_1_, ...), custom_call_target="tpu_custom_call", output_to_operand_aliasing={{}: (4, {})} | custom-call | tf_op jit(solution)/shard_map/rotate/pallas_call | solution.py:425
  106.4 0.6 select_reduce_fusion
  (43 shorter events, 0.6 us)
Async XLA Ops:
  0.6 1.0 copy-start.8
  1.7 0.7 copy-start.9
  2.4 0.7 copy-start.11
  3.3 19.2 %collective-permute-start.3 = (bf16[128,1152]{1,0:T(8,128)(2,1)S(1)}, bf16[128,1152]{1,0:T(8,128)(2,1)S(1)}, u32[]{:S(2)}, u32[]{:S(2)}) collective-permute-start(bf16[128,1152]{1,0:T(8,128)(2,1)S(1)} %get-tuple-element.80.refs_0_), channel_id=1, source_target_pairs={{0,6},{1,7},{2,0},{3,1},{4,2},{5,3},{6,4},{7,5},{8,14},{9,15},{10,... | collective-permute-start | bytes 884744 | tf_op jit(solution)/shard_map/ppermute | solution.py:76
  8.4 14.1 %collective-permute-start.2 = (bf16[128,1152]{1,0:T(8,128)(2,1)S(1)}, bf16[128,1152]{1,0:T(8,128)(2,1)S(1)}, u32[]{:S(2)}, u32[]{:S(2)}) collective-permute-start(bf16[128,1152]{1,0:T(8,128)(2,1)S(1)} %get-tuple-element.80.refs_0_), channel_id=1, source_target_pairs={{0,2},{1,3},{2,4},{3,5},{4,6},{5,7},{6,0},{7,1},{8,10},{9,11},{10,... | collective-permute-start | bytes 884744 | tf_op jit(solution)/shard_map/ppermute | solution.py:76
  8.4 14.1 %collective-permute-start = (bf16[128,1152]{1,0:T(8,128)(2,1)S(1)}, bf16[128,1152]{1,0:T(8,128)(2,1)S(1)}, u32[]{:S(2)}, u32[]{:S(2)}) collective-permute-start(bf16[128,1152]{1,0:T(8,128)(2,1)S(1)} %get-tuple-element.80.refs_0_), channel_id=1, source_target_pairs={{0,1},{1,0},{2,3},{3,2},{4,5},{5,4},{6,7},{7,6},{8,9},{9,8},{10,11... | collective-permute-start | bytes 884744 | tf_op jit(solution)/shard_map/ppermute | solution.py:80
  9.8 12.6 %collective-permute-start.1 = (bf16[128,1024]{1,0:T(8,128)(2,1)S(1)}, bf16[128,1024]{1,0:T(8,128)(2,1)S(1)}, u32[]{:S(2)}, u32[]{:S(2)}) collective-permute-start(bf16[128,1024]{1,0:T(8,128)(2,1)S(1)} %get-tuple-element.110.refs_0_), channel_id=1, source_target_pairs={{0,1},{1,0},{2,3},{3,2},{4,5},{5,4},{6,7},{7,6},{8,9},{9,8},{10,11... | collective-permute-start | bytes 786440 | tf_op jit(solution)/shard_map/ppermute | solution.py:80
  22.5 14.8 %collective-permute-start.4 = (bf16[128,1152]{1,0:T(8,128)(2,1)S(1)}, bf16[128,1152]{1,0:T(8,128)(2,1)S(1)}, u32[]{:S(2)}, u32[]{:S(2)}) collective-permute-start(bf16[128,1152]{1,0:T(8,128)(2,1)S(1)} %get-tuple-element.80.refs_0_), channel_id=1, source_target_pairs={{0,4},{1,5},{2,6},{3,7},{4,0},{5,1},{6,2},{7,3},{8,12},{9,13},{10,... | collective-permute-start | bytes 884744 | tf_op jit(solution)/shard_map/ppermute | solution.py:76
  23.2 14.0 %collective-permute-start.5 = (bf16[128,1152]{1,0:T(8,128)(2,1)S(1)}, bf16[128,1152]{1,0:T(8,128)(2,1)S(1)}, u32[]{:S(2)}, u32[]{:S(2)}) collective-permute-start(bf16[128,1152]{1,0:T(8,128)(2,1)S(1)} %collective-permute-done.2.refs_2_), channel_id=1, source_target_pairs={{0,1},{1,0},{2,3},{3,2},{4,5},{5,4},{6,7},{7,6},{8,9},{9,8},{10,11... | collective-permute-start | bytes 884744 | tf_op jit(solution)/shard_map/ppermute | solution.py:80
  24.7 12.6 %collective-permute-start.6 = (bf16[128,1152]{1,0:T(8,128)(2,1)S(1)}, bf16[128,1152]{1,0:T(8,128)(2,1)S(1)}, u32[]{:S(2)}, u32[]{:S(2)}) collective-permute-start(bf16[128,1152]{1,0:T(8,128)(2,1)S(1)} %collective-permute-done.3.refs_3_), channel_id=1, source_target_pairs={{0,1},{1,0},{2,3},{3,2},{4,5},{5,4},{6,7},{7,6},{8,9},{9,8},{10,11... | collective-permute-start | bytes 884744 | tf_op jit(solution)/shard_map/ppermute | solution.py:80
  25.3 2.8 %copy-start = (bf16[2,768,2048]{2,1,0:T(8,128)(2,1)S(1)}, bf16[2,768,2048]{2,1,0:T(8,128)(2,1)}, u32[]{:S(2)}) copy-start(bf16[2,768,2048]{2,1,0:T(8,128)(2,1)} %refs_7_.3) | copy-start | bytes 18874372
  28.1 1.7 %copy-start.2 = (bf16[1,2,8,96,768]{4,3,2,1,0:T(8,128)(2,1)S(1)}, bf16[1,2,8,96,768]{4,3,2,1,0:T(8,128)(2,1)}, u32[]{:S(2)}) copy-start(bf16[1,2,8,96,768]{4,3,2,1,0:T(8,128)(2,1)} %param.9) | copy-start | bytes 7077892
  29.7 11.9 %copy-start.1 = (bf16[2,768,2048]{2,1,0:T(8,128)(2,1)S(1)}, bf16[2,768,2048]{2,1,0:T(8,128)(2,1)}, u32[]{:S(2)}) copy-start(bf16[2,768,2048]{2,1,0:T(8,128)(2,1)} %refs_7_.3) | copy-start | bytes 18874372
  29.7 11.9 %copy-start.3 = (bf16[1,2,8,96,768]{4,3,2,1,0:T(8,128)(2,1)S(1)}, bf16[1,2,8,96,768]{4,3,2,1,0:T(8,128)(2,1)}, u32[]{:S(2)}) copy-start(bf16[1,2,8,96,768]{4,3,2,1,0:T(8,128)(2,1)} %param.9) | copy-start | bytes 7077892
  37.3 8.1 %collective-permute-start.9 = (bf16[128,1152]{1,0:T(8,128)(2,1)S(1)}, bf16[128,1152]{1,0:T(8,128)(2,1)S(1)}, u32[]{:S(2)}, u32[]{:S(2)}) collective-permute-start(bf16[128,1152]{1,0:T(8,128)(2,1)S(1)} %collective-permute-done.4.refs_0_), channel_id=1, source_target_pairs={{0,1},{1,0},{2,3},{3,2},{4,5},{5,4},{6,7},{7,6},{8,9},{9,8},{10,11... | collective-permute-start | bytes 884744 | tf_op jit(solution)/shard_map/ppermute | solution.py:80
  38.8 13.0 %collective-permute-start.8 = (bf16[128,1024]{1,0:T(8,128)(2,1)S(1)}, bf16[128,1024]{1,0:T(8,128)(2,1)S(1)}, u32[]{:S(2)}, u32[]{:S(2)}) collective-permute-start(bf16[128,1024]{1,0:T(8,128)(2,1)S(1)} %get-tuple-element.110.refs_0_), channel_id=1, source_target_pairs={{0,6},{1,7},{2,0},{3,1},{4,2},{5,3},{6,4},{7,5},{8,14},{9,15},{10,... | collective-permute-start | bytes 786440 | tf_op jit(solution)/shard_map/ppermute | solution.py:76
  41.3 10.8 %collective-permute-start.7 = (bf16[128,1024]{1,0:T(8,128)(2,1)S(1)}, bf16[128,1024]{1,0:T(8,128)(2,1)S(1)}, u32[]{:S(2)}, u32[]{:S(2)}) collective-permute-start(bf16[128,1024]{1,0:T(8,128)(2,1)S(1)} %get-tuple-element.110.refs_0_), channel_id=1, source_target_pairs={{0,2},{1,3},{2,4},{3,5},{4,6},{5,7},{6,0},{7,1},{8,10},{9,11},{10,... | collective-permute-start | bytes 786440 | tf_op jit(solution)/shard_map/ppermute | solution.py:76
  51.8 28.8 %copy-start.4 = (bf16[256,1536]{1,0:T(8,128)(2,1)}, bf16[256,1536]{1,0:T(8,128)(2,1)S(1)}, u32[]{:S(2)}) copy-start(bf16[256,1536]{1,0:T(8,128)(2,1)S(1)} %get-tuple-element.139.refs_0_) | copy-start | bytes 2359300
  52.1 3.8 %collective-permute-start.14 = (bf16[128,1536]{1,0:T(8,128)(2,1)S(1)}, bf16[128,1536]{1,0:T(8,128)(2,1)S(1)}, u32[]{:S(2)}, u32[]{:S(2)}) collective-permute-start(bf16[128,1536]{1,0:T(8,128)(2,1)S(1)} %get-tuple-element.128), channel_id=1, source_target_pairs={{0,8},{8,0},{16,24},{24,16},{1,9},{9,1},{17,25},{25,17},{2,10},{10... | collective-permute-start | bytes 1179656 | tf_op jit(solution)/shard_map/ppermute | solution.py:467
  52.1 3.8 %collective-permute-start.15 = (bf16[128,1536]{1,0:T(8,128)(2,1)S(1)}, bf16[128,1536]{1,0:T(8,128)(2,1)S(1)}, u32[]{:S(2)}, u32[]{:S(2)}) collective-permute-start(bf16[128,1536]{1,0:T(8,128)(2,1)S(1)} %get-tuple-element.129), channel_id=1, source_target_pairs={{0,8},{8,0},{16,24},{24,16},{1,9},{9,1},{17,25},{25,17},{2,10},{10... | collective-permute-start | bytes 1179656 | tf_op jit(solution)/shard_map/ppermute | solution.py:467
  52.6 14.7 %collective-permute-start.10 = (bf16[128,1024]{1,0:T(8,128)(2,1)S(1)}, bf16[128,1024]{1,0:T(8,128)(2,1)S(1)}, u32[]{:S(2)}, u32[]{:S(2)}) collective-permute-start(bf16[128,1024]{1,0:T(8,128)(2,1)S(1)} %get-tuple-element.110.refs_0_), channel_id=1, source_target_pairs={{0,4},{1,5},{2,6},{3,7},{4,0},{5,1},{6,2},{7,3},{8,12},{9,13},{10,... | collective-permute-start | bytes 786440 | tf_op jit(solution)/shard_map/ppermute | solution.py:76
  53.8 13.5 %collective-permute-start.11 = (bf16[128,1024]{1,0:T(8,128)(2,1)S(1)}, bf16[128,1024]{1,0:T(8,128)(2,1)S(1)}, u32[]{:S(2)}, u32[]{:S(2)}) collective-permute-start(bf16[128,1024]{1,0:T(8,128)(2,1)S(1)} %collective-permute-done.7.refs_2_), channel_id=1, source_target_pairs={{0,1},{1,0},{2,3},{3,2},{4,5},{5,4},{6,7},{7,6},{8,9},{9,8},{10,11... | collective-permute-start | bytes 786440 | tf_op jit(solution)/shard_map/ppermute | solution.py:80
  54.3 13.0 %collective-permute-start.12 = (bf16[128,1024]{1,0:T(8,128)(2,1)S(1)}, bf16[128,1024]{1,0:T(8,128)(2,1)S(1)}, u32[]{:S(2)}, u32[]{:S(2)}) collective-permute-start(bf16[128,1024]{1,0:T(8,128)(2,1)S(1)} %collective-permute-done.8.refs_3_), channel_id=1, source_target_pairs={{0,1},{1,0},{2,3},{3,2},{4,5},{5,4},{6,7},{7,6},{8,9},{9,8},{10,11... | collective-permute-start | bytes 786440 | tf_op jit(solution)/shard_map/ppermute | solution.py:80
  56.0 24.6 %collective-permute-start.16 = (bf16[256,1536]{1,0:T(8,128)(2,1)S(1)}, bf16[256,1536]{1,0:T(8,128)(2,1)S(1)}, u32[]{:S(2)}, u32[]{:S(2)}) collective-permute-start(bf16[256,1536]{1,0:T(8,128)(2,1)S(1)} %add_convert_fusion.1), channel_id=1, source_target_pairs={{0,16},{8,24},{16,0},{24,8},{1,17},{9,25},{17,1},{25,9},{2,18},{10... | collective-permute-start | bytes 2359304 | tf_op jit(solution)/shard_map/ppermute | solution.py:473
  67.4 7.3 %collective-permute-start.13 = (bf16[128,1024]{1,0:T(8,128)(2,1)S(1)}, bf16[128,1024]{1,0:T(8,128)(2,1)S(1)}, u32[]{:S(2)}, u32[]{:S(2)}) collective-permute-start(bf16[128,1024]{1,0:T(8,128)(2,1)S(1)} %collective-permute-done.10.refs_4_), channel_id=1, source_target_pairs={{0,1},{1,0},{2,3},{3,2},{4,5},{5,4},{6,7},{7,6},{8,9},{9,8},{10,11... | collective-permute-start | bytes 786440 | tf_op jit(solution)/shard_map/ppermute | solution.py:80
  80.6 11.9 %copy-start.6 = (bf16[256,1536]{1,0:T(8,128)(2,1)}, bf16[256,1536]{1,0:T(8,128)(2,1)S(1)}, u32[]{:S(2)}) copy-start(bf16[256,1536]{1,0:T(8,128)(2,1)S(1)} %collective-permute-done.16.refs_2_) | copy-start | bytes 2359300
  80.6 1.8 %collective-permute-start.19 = (bf16[128,1536]{1,0:T(8,128)(2,1)S(1)}, bf16[128,1536]{1,0:T(8,128)(2,1)S(1)}, u32[]{:S(2)}, u32[]{:S(2)}) collective-permute-start(bf16[128,1536]{1,0:T(8,128)(2,1)S(1)} %get-tuple-element.142), channel_id=1, source_target_pairs={{0,8},{8,0},{16,24},{24,16},{1,9},{9,1},{17,25},{25,17},{2,10},{10... | collective-permute-start | bytes 1179656 | tf_op jit(solution)/shard_map/ppermute | solution.py:467
  80.7 2.8 %collective-permute-start.20 = (bf16[128,1536]{1,0:T(8,128)(2,1)S(1)}, bf16[128,1536]{1,0:T(8,128)(2,1)S(1)}, u32[]{:S(2)}, u32[]{:S(2)}) collective-permute-start(bf16[128,1536]{1,0:T(8,128)(2,1)S(1)} %get-tuple-element.143), channel_id=1, source_target_pairs={{0,8},{8,0},{16,24},{24,16},{1,9},{9,1},{17,25},{25,17},{2,10},{10... | collective-permute-start | bytes 1179656 | tf_op jit(solution)/shard_map/ppermute | solution.py:467
  81.2 15.8 %collective-permute-start.18 = (bf16[256,1536]{1,0:T(8,128)(2,1)}, bf16[256,1536]{1,0:T(8,128)(2,1)}, u32[]{:S(2)}, u32[]{:S(2)}) collective-permute-start(bf16[256,1536]{1,0:T(8,128)(2,1)} %get-tuple-element.140), channel_id=1, source_target_pairs={{0,8},{8,0},{16,24},{24,16},{1,9},{9,1},{17,25},{25,17},{2,10},{10... | collective-permute-start | bytes 2359304 | tf_op jit(solution)/shard_map/ppermute | solution.py:467
  84.7 19.8 %collective-permute-start.21 = (bf16[256,1536]{1,0:T(8,128)(2,1)}, bf16[256,1536]{1,0:T(8,128)(2,1)S(1)}, u32[]{:S(2)}, u32[]{:S(2)}) collective-permute-start(bf16[256,1536]{1,0:T(8,128)(2,1)} %add_convert_fusion), channel_id=1, source_target_pairs={{0,16},{8,24},{16,0},{24,8},{1,17},{9,25},{17,1},{25,9},{2,18},{10... | collective-permute-start | bytes 2359304 | tf_op jit(solution)/shard_map/ppermute | solution.py:473
  86.2 18.2 %collective-permute-start.17 = (bf16[256,1536]{1,0:T(8,128)(2,1)}, bf16[256,1536]{1,0:T(8,128)(2,1)S(1)}, u32[]{:S(2)}, u32[]{:S(2)}) collective-permute-start(bf16[256,1536]{1,0:T(8,128)(2,1)} %get-tuple-element.138), channel_id=1, source_target_pairs={{0,8},{8,0},{16,24},{24,16},{1,9},{9,1},{17,25},{25,17},{2,10},{10... | collective-permute-start | bytes 2359304 | tf_op jit(solution)/shard_map/ppermute | solution.py:467
  92.6 13.8 %all-to-all-start = ((f32[8,2,128]{2,1,0:T(2,128)}), f32[8,2,128]{2,1,0:T(2,128)S(1)}, u32[]{:S(2)}, u32[]{:S(2)}) async-start(f32[8,2,128]{2,1,0:T(2,128)} %get-tuple-element.135), calls=%async_computation | async-start | bytes 16384 | tf_op jit(solution)/shard_map/all_to_all | solution.py:525
  97.0 1.1 %copy-start.5 = (bf16[256,1536]{1,0:T(8,128)(2,1)S(1)}, bf16[256,1536]{1,0:T(8,128)(2,1)}, u32[]{:S(2)}) copy-start(bf16[256,1536]{1,0:T(8,128)(2,1)} %copy-done.4) | copy-start | bytes 2359300
  98.2 1.1 %copy-start.7 = (bf16[256,1536]{1,0:T(8,128)(2,1)S(1)}, bf16[256,1536]{1,0:T(8,128)(2,1)}, u32[]{:S(2)}) copy-start(bf16[256,1536]{1,0:T(8,128)(2,1)} %copy-done.6) | copy-start | bytes 2359300
  102.2 4.2 %copy-start.10 = (s32[128,8]{0,1:T(8,128)S(1)}, s32[128,8]{0,1:T(8,128)}, u32[]{:S(2)}) copy-start(s32[128,8]{0,1:T(8,128)} %param.8) | copy-start | bytes 12292

commit v6 on v5

--- a/solution.py
+++ b/solution.py
@@ -63,7 +63,7 @@
     return pl.pallas_call(
         functools.partial(pack_kernel, pieces, replicas),
         out_shape=[jax.ShapeDtypeStruct((tokens, width), BF16) for width in widths],
-        compiler_params=params(),
+        compiler_params=params(56 * 1024 * 1024),
         name="pack",
     )(cotangent, gate_prob.T, routes.T)
 
@@ -250,9 +250,10 @@
         at += out_ref.shape[0]
 
 
-def band_outputs(bands, width, experts_here, units):
+def band_outputs(bands, width, experts_here, units, halves):
     rows = [len(band) * width for band in bands]
-    rows = [rows[0] // 2, rows[0] // 2] + rows[1:]
+    if halves:
+        rows = [rows[0] // 2, rows[0] // 2] + rows[1:]
     specs = [pl.BlockSpec((size, units), lambda e, *_: (0, e)) for size in rows]
     shapes = [jax.ShapeDtypeStruct((size, experts_here * units), BF16) for size in rows]
     return specs, shapes
@@ -267,11 +268,11 @@
     store_bands(jnp.concatenate(taken, axis=1), refs[:weighted_here], refs[weighted_here:])
 
 
-def grad_bands(routed, weighted, owned, bands):
+def grad_bands(routed, weighted, owned, bands, halves=True):
     experts_here, _, units = weighted[0].shape
     width = routed[0].shape[2] // owned.shape[0]
     wanted = [j for band in bands for j in band]
-    out_specs, out_shape = band_outputs(bands, width, experts_here, units)
+    out_specs, out_shape = band_outputs(bands, width, experts_here, units, halves)
 
     def share(part, j):
         return pl.BlockSpec((1, part.shape[1], width), lambda e, owned: (e, 0, owned[j]))
@@ -321,7 +322,7 @@
     token_rows, tokens = sum(part.shape[0] for part in parts), tables[0].shape[2]
     columns = parts[0].shape[1]
     width = columns // owned.shape[0]
-    out_specs, out_shape = band_outputs(bands, width, experts_here, units)
+    out_specs, out_shape = band_outputs(bands, width, experts_here, units, True)
     wanted = [j for band in bands for j in band]
     return pl.pallas_call(
         functools.partial(route_kernel, len(parts), len(tables), wanted, width),
@@ -480,8 +481,8 @@
     def visit_first(parts, begin, with_product=True):
         return visit(parts, slots, begin, down_weight, saved, replicas, tokens, with_product)
 
-    def bands_first(visits, bands):
-        return grad_bands([made[0] for made in visits], [made[1] for made in visits], owned, bands)
+    def bands_first(visits, bands, halves=True):
+        return grad_bands([made[0] for made in visits], [made[1] for made in visits], owned, bands, halves)
 
     a, b = sent
     if sources == 2 * LINES:
@@ -494,17 +495,18 @@
         a_xopp, b_next, b_prev = across(a_opp), along(b, 1), along(b, -1)
         a_far = visit_first([a_opp, a_xnext, a_xprev], 4)
         a_xopp, a_far, b = fence(a_xopp, a_far, b)
-        a_made = [a_near, a_far, visit_first([a_xopp], 7, with_product=False)]
-        made = bands_first(a_made, away_bands + here_bands)
+        a_made = [a_near, a_far, visit_first([a_xopp], 7)]
+        made = bands_first(a_made, away_bands)
         b_next, b_prev, made, b = fence(b_next, b_prev, made, b)
         b_opp, b_xnext, b_xprev = along(b, 2), across(b_next), across(b_prev)
-        *away_send, away_keep, here_send, here_keep = made
-        b_opp, b_xnext, b_xprev = fence(b_opp, b_xnext, b_xprev)
+        *away_send, away_keep = made
+        here_send, here_keep = bands_first(a_made, here_bands, halves=False)
+        b_opp, b_xnext, b_xprev, here_send, here_keep = fence(b_opp, b_xnext, b_xprev, here_send, here_keep)
         b_xopp = across(b_opp)
         a_arrived = to_chips(add_swapped(away_send, away_keep))
         b_xopp, here_send = fence(b_xopp, here_send)
         b_parts = [b, b_x, b_next, b_prev, b_opp, b_xnext, b_xprev, b_xopp]
-        seen, late = [a_near[3], a_far[3]], [a_made[2][0]]
+        seen, late = [made[3] for made in a_made], []
     else:
         a, b = [lax.all_gather(part, "expert", axis=0, tiled=True) for part in sent]
         slots = jnp.arange(sources, dtype=jnp.int32)
@@ -516,9 +518,10 @@
 
     weighted = [made[1] for made in a_made]
     tables = [made[2] for made in a_made]
-    made = route(b_parts, tables, weighted, owned, away_bands + here_bands)
+    made = route(b_parts, tables, weighted, owned, away_bands)
     made, a_arrived = fence(made, a_arrived)
-    *away_send, away_keep, here_send_b, here_keep_b, routed_b = made
+    *away_send, away_keep, routed_b = made
+    here_send_b, here_keep_b = grad_bands([routed_b], weighted, owned, here_bands, halves=False)
     b_arrived = to_chips(add_swapped(away_send, away_keep))
     here_got, here_got_b = swap(here_send), swap(here_send_b)
     grad_hidden, grad_slots = back(routed_b, slots, down_weight, saved, width, replicas, seen, late, tables)
@@ -529,8 +532,8 @@
     returned, out = fence(returned, out)
     of_token = returned.reshape(-1, 1, tokens)
     named = routes.T[None] == jnp.arange(of_token.shape[0], dtype=jnp.int32)[:, None, None]
-    grad_prob = jnp.sum(jnp.where(named, of_token, 0.0), axis=0).T
-    return (grad_hidden[None], grad_prob, out)
+    grad_prob = jnp.sum(jnp.where(named, of_token, 0.0), axis=0)
+    return (grad_hidden[None], grad_prob.T, out)
 
 
 def solution(mesh):

time: 107 us -> 105 us (0.981)
  Pallas kernels: 30.4 us -> 34.4 us
  local copies, waits for them, and re-layouts: 9.23 us -> 6.83 us
  waiting for transfers between devices: 35.8 us -> 33.7 us
  starting transfers between devices: 27.6 us -> 25.8 us
    pallas_call x1 -> x3, Pallas kernels: 5.08 us -> 9.17 us  [grad_bands(): pl.pallas_call(functools.partial(bands_kernel, len(wanted), len(routed),...]
    unnamed x26 -> x24, local copies, waits for them, and re-layouts: 9.14 us -> 6.74 us
    pallas_call x1, Pallas kernels: 5.93 us -> 3.9 us  [route(): pl.pallas_call(functools.partial(route_kernel, len(parts), len(tables), w...]
    ppermute x6, waiting for transfers between devices: 13.9 us -> 12.1 us  [along(): lax.ppermute(value, 'expert', [(2 * a + x, 2 * b + x) for a, b in pairs f...]
    pallas_call x1, Pallas kernels: 0.22 us -> 1.98 us  [pack(): pl.pallas_call(functools.partial(pack_kernel, pieces, replicas), out_shap...]
    ppermute x2, waiting for transfers between devices: 2.25 us -> 0.68 us  [to_chips(): moved.append(lax.ppermute(value[(k - 1) * width:k * width], 'dp', pairs))]
    pallas_call x3, Pallas kernels: 8 us -> 9.27 us  [visit(): pl.pallas_call(functools.partial(visit_kernel, len(parts), len(shares), b...]
    ppermute x8, waiting for transfers between devices: 17.4 us -> 18.6 us  [across(): return lax.ppermute(value, 'expert', [(i, i ^ 1) for i in range(2 * LINES)])]
  transfers between devices with their start and end apart: 23 -> 23, of which waited for: 9 -> 9; matrix products, arithmetic and copies ran while one was open for 2% -> 2% of each run, Pallas kernels for 28% -> 31%
where the time goes in v6:
time: 105 us
  Pallas kernels  34.4 us (33%)
  waiting for transfers between devices  33.7 us (32%)
  starting transfers between devices  25.8 us (25%)
  local copies, waits for them, and re-layouts  6.83 us (7%)
  other arithmetic  3.11 us (3%)
    ppermute x8, waiting for transfers between devices, across(): return lax.ppermute(value, 'expert', [(i, i ^ 1) for i in range(2 * LINES)])  18.6 us
    ppermute x6, waiting for transfers between devices, along(): lax.ppermute(value, 'expert', [(2 * a + x, 2 * b + x) for a, b in pairs f...  12.1 us
    ppermute x6, starting transfers between devices, along(): lax.ppermute(value, 'expert', [(2 * a + x, 2 * b + x) for a, b in pairs f...  9.48 us
    pallas_call x3, Pallas kernels, visit(): pl.pallas_call(functools.partial(visit_kernel, len(parts), len(shares), b...  9.27 us
    pallas_call x3, Pallas kernels, grad_bands(): pl.pallas_call(functools.partial(bands_kernel, len(wanted), len(routed),...  9.17 us
    ppermute x8, starting transfers between devices, across(): return lax.ppermute(value, 'expert', [(i, i ^ 1) for i in range(2 * LINES)])  8.11 us
    unnamed x24, local copies, waits for them, and re-layouts  6.74 us
    pallas_call x1, Pallas kernels, back(): pl.pallas_call(functools.partial(back_kernel, replicas, len(seen), len(la...  5.26 us
  transfers between devices with their start and end apart: 23, of which 9 were waited for; matrix products, arithmetic and copies ran while one was open for 2% of the time, Pallas kernels for 31%

profile of v6, /device:TPU:0, one launch (start us, length us, event | category | flops | bytes accessed | tf_op | source)
XLA Modules:
  0.0 104.7 jit_solution(1828910762251998525)
XLA Ops:
  0.6 2.0 %pack.1 = (bf16[128,1152]{1,0:T(8,128)(2,1)}, bf16[128,1024]{1,0:T(8,128)(2,1)}) custom-call(bf16[128,2048]{1,0:T(8,128)(2,1)} %cot_ref.1, bf16[8,128]{1,0:T(8,128)(2,1)} %bitcast.34, s32[8,128]{1,0:T(8,128)} %bitcast.31), custom_call_target="tpu_custom_call" | custom-call | tf_op jit(solution)/shard_map/pack/pallas_call | solution.py:63
  2.6 5.0 %collective-permute-start.3 = (bf16[128,1152]{1,0:T(8,128)(2,1)}, bf16[128,1152]{1,0:T(8,128)(2,1)S(1)}, u32[]{:S(2)}, u32[]{:S(2)}) collective-permute-start(bf16[128,1152]{1,0:T(8,128)(2,1)} %get-tuple-element.79.refs_0_), channel_id=1, source_target_pairs={{0,6},{1,7},{2,0},{3,1},{4,2},{5,3},{6,4},{7,5},{8,14},{9,15},{10,... | collective-permute-start | bytes 884744 | tf_op jit(solution)/shard_map/ppermute | solution.py:76
  7.7 1.5 %collective-permute-start = (bf16[128,1152]{1,0:T(8,128)(2,1)}, bf16[128,1152]{1,0:T(8,128)(2,1)S(1)}, u32[]{:S(2)}, u32[]{:S(2)}) collective-permute-start(bf16[128,1152]{1,0:T(8,128)(2,1)} %get-tuple-element.79.refs_0_), channel_id=1, source_target_pairs={{0,1},{1,0},{2,3},{3,2},{4,5},{5,4},{6,7},{7,6},{8,9},{9,8},{10,11... | collective-permute-start | bytes 884744 | tf_op jit(solution)/shard_map/ppermute | solution.py:80
  9.2 0.5 collective-permute-start.1
  9.7 0.8 fusion.18
  10.5 0.3 fusion.10
  11.0 0.1 multiply_convert_fusion.turn_ref
  11.1 10.9 %collective-permute-done.1.refs_1_ = bf16[128,1024]{1,0:T(8,128)(2,1)S(1)} collective-permute-done((bf16[128,1024]{1,0:T(8,128)(2,1)}, bf16[128,1024]{1,0:T(8,128)(2,1)S(1)}, u32[]{:S(2)}, u32[]{:S(2)}) %collective-permute-start.1) | collective-permute-done | bytes 262176 | tf_op jit(solution)/shard_map/ppermute | solution.py:80
  22.0 0.8 collective-permute-start.4
  22.8 1.5 %collective-permute-start.5 = (bf16[128,1152]{1,0:T(8,128)(2,1)S(1)}, bf16[128,1152]{1,0:T(8,128)(2,1)S(1)}, u32[]{:S(2)}, u32[]{:S(2)}) collective-permute-start(bf16[128,1152]{1,0:T(8,128)(2,1)S(1)} %collective-permute-done.2.refs_2_), channel_id=1, source_target_pairs={{0,1},{1,0},{2,3},{3,2},{4,5},{5,4},{6,7},{7,6},{8,9},{9,8},{10,11... | collective-permute-start | bytes 884744 | tf_op jit(solution)/shard_map/ppermute | solution.py:80
  24.3 0.5 collective-permute-start.6
  24.8 2.8 %copy-done = bf16[2,768,2048]{2,1,0:T(8,128)(2,1)S(1)} copy-done((bf16[2,768,2048]{2,1,0:T(8,128)(2,1)S(1)}, bf16[2,768,2048]{2,1,0:T(8,128)(2,1)}, u32[]{:S(2)}) %copy-start) | copy-done | bytes 6291480
  27.6 1.7 %copy-done.2 = bf16[1,2,8,96,768]{4,3,2,1,0:T(8,128)(2,1)S(1)} copy-done((bf16[1,2,8,96,768]{4,3,2,1,0:T(8,128)(2,1)S(1)}, bf16[1,2,8,96,768]{4,3,2,1,0:T(8,128)(2,1)}, u32[]{:S(2)}) %copy-start.2) | copy-done | bytes 2359320
  29.3 3.6 %visit.3 = (bf16[2,384,1024]{2,1,0:T(8,128)(2,1)S(1)}, bf16[2,384,768]{2,1,0:T(8,128)(2,1)S(1)}, f32[4,8,128]{2,1,0:T(8,128)S(1)}, bf16[2,384,768]{2,1,0:T(8,128)(2,1)S(1)}) custom-call(s32[8]{0:T(128)S(1)} %stack.55.slots_ref, bf16[128,1152]{1,0:T(8,128)(2,1)S(1)} %copy-done.8, bf16[128,1152]{1,0:T(8,128)(2,1)S(1)} %collective-permute-done.refs_1_, ...), custom_call_target="tpu_custom_call" | custom-call | tf_op jit(solution)/shard_map/visit/pallas_call | solution.py:217
  32.9 4.1 %collective-permute-done.4.refs_0_ = bf16[128,1152]{1,0:T(8,128)(2,1)S(1)} collective-permute-done((bf16[128,1152]{1,0:T(8,128)(2,1)}, bf16[128,1152]{1,0:T(8,128)(2,1)S(1)}, u32[]{:S(2)}, u32[]{:S(2)}) %collective-permute-start.4) | collective-permute-done | bytes 294944 | tf_op jit(solution)/shard_map/ppermute | solution.py:76
  37.0 1.5 %collective-permute-start.9 = (bf16[128,1152]{1,0:T(8,128)(2,1)S(1)}, bf16[128,1152]{1,0:T(8,128)(2,1)S(1)}, u32[]{:S(2)}, u32[]{:S(2)}) collective-permute-start(bf16[128,1152]{1,0:T(8,128)(2,1)S(1)} %collective-permute-done.4.refs_0_), channel_id=1, source_target_pairs={{0,1},{1,0},{2,3},{3,2},{4,5},{5,4},{6,7},{7,6},{8,9},{9,8},{10,11... | collective-permute-start | bytes 884744 | tf_op jit(solution)/shard_map/ppermute | solution.py:80
  38.5 2.3 %collective-permute-start.8 = (bf16[128,1024]{1,0:T(8,128)(2,1)S(1)}, bf16[128,1024]{1,0:T(8,128)(2,1)S(1)}, u32[]{:S(2)}, u32[]{:S(2)}) collective-permute-start(bf16[128,1024]{1,0:T(8,128)(2,1)S(1)} %copy-done.9), channel_id=1, source_target_pairs={{0,6},{1,7},{2,0},{3,1},{4,2},{5,3},{6,4},{7,5},{8,14},{9,15},{10,... | collective-permute-start | bytes 786440 | tf_op jit(solution)/shard_map/ppermute | solution.py:76
  40.8 0.3 collective-permute-start.7
  41.1 3.1 %visit.4 = (bf16[2,288,1024]{2,1,0:T(8,128)(2,1)S(1)}, bf16[2,288,768]{2,1,0:T(8,128)(2,1)S(1)}, f32[3,8,128]{2,1,0:T(8,128)S(1)}, bf16[2,288,768]{2,1,0:T(8,128)(2,1)S(1)}) custom-call(s32[8]{0:T(128)S(1)} %stack.55.slots_ref, bf16[128,1152]{1,0:T(8,128)(2,1)S(1)} %collective-permute-done.4.refs_0_, bf16[128,1152]{1,0:T(8,128)(2,1)S(1)} %collective-permute-done.5.refs_1_, ...), custom_call_target="tpu_custom_call" | custom-call | tf_op jit(solution)/shard_map/visit/pallas_call | solution.py:217
  44.3 0.9 collective-permute-done.9.refs_0_
  45.2 2.5 %visit.5 = (bf16[2,96,1024]{2,1,0:T(8,128)(2,1)S(1)}, bf16[2,96,768]{2,1,0:T(8,128)(2,1)S(1)}, f32[1,8,128]{2,1,0:T(8,128)S(1)}, bf16[2,96,768]{2,1,0:T(8,128)(2,1)S(1)}) custom-call(s32[8]{0:T(128)S(1)} %stack.55.slots_ref, bf16[128,1152]{1,0:T(8,128)(2,1)S(1)} %collective-permute-done.9.refs_0_, bf16[2,768,2048]{2,1,0:T(8,128)(2,1)S(1)} %copy-done.1, ...), custom_call_target="tpu_custom_call" | custom-call | tf_op jit(solution)/shard_map/visit/pallas_call | solution.py:217
  47.7 2.7 %bands.3 = (bf16[128,1536]{1,0:T(8,128)(2,1)S(1)}, bf16[128,1536]{1,0:T(8,128)(2,1)S(1)}, bf16[256,1536]{1,0:T(8,128)(2,1)S(1)}) custom-call(s32[4]{0:T(128)S(1)} %pad_add_fusion.owners_ref, bf16[2,384,1024]{2,1,0:T(8,128)(2,1)S(1)} %get-tuple-element.89.refs_0_.refs_3_, bf16[2,288,1024]{2,1,0:T(8,128)(2,1)S(1)} %get-tuple-element.97.refs_1_.refs_4_, ...), custom_call_target="tpu_custom_call" | custom-call | tf_op jit(solution)/shard_map/bands/pallas_call | solution.py:280
  50.4 1.4 %collective-permute-done.7.refs_2_ = bf16[128,1024]{1,0:T(8,128)(2,1)S(1)} collective-permute-done((bf16[128,1024]{1,0:T(8,128)(2,1)S(1)}, bf16[128,1024]{1,0:T(8,128)(2,1)S(1)}, u32[]{:S(2)}, u32[]{:S(2)}) %collective-permute-start.7) | collective-permute-done | bytes 262176 | tf_op jit(solution)/shard_map/ppermute | solution.py:76
  51.8 0.5 collective-permute-start.15
  52.3 1.0 collective-permute-start.10
  53.3 0.5 collective-permute-start.11
  53.9 1.5 %collective-permute-start.12 = (bf16[128,1024]{1,0:T(8,128)(2,1)S(1)}, bf16[128,1024]{1,0:T(8,128)(2,1)S(1)}, u32[]{:S(2)}, u32[]{:S(2)}) collective-permute-start(bf16[128,1024]{1,0:T(8,128)(2,1)S(1)} %collective-permute-done.8.refs_3_), channel_id=1, source_target_pairs={{0,1},{1,0},{2,3},{3,2},{4,5},{5,4},{6,7},{7,6},{8,9},{9,8},{10,11... | collective-permute-start | bytes 786440 | tf_op jit(solution)/shard_map/ppermute | solution.py:80
  55.4 0.2 add_convert_fusion.1
  55.6 1.6 %collective-permute-start.16 = (bf16[256,1536]{1,0:T(8,128)(2,1)S(1)}, bf16[256,1536]{1,0:T(8,128)(2,1)S(1)}, u32[]{:S(2)}, u32[]{:S(2)}) collective-permute-start(bf16[256,1536]{1,0:T(8,128)(2,1)S(1)} %add_convert_fusion.1), channel_id=1, source_target_pairs={{0,16},{8,24},{16,0},{24,8},{1,17},{9,25},{17,1},{25,9},{2,18},{10... | collective-permute-start | bytes 2359304 | tf_op jit(solution)/shard_map/ppermute | solution.py:474
  57.1 3.3 %bands.4 = (bf16[256,1536]{1,0:T(8,128)(2,1)}, bf16[256,1536]{1,0:T(8,128)(2,1)S(1)}) custom-call(s32[4]{0:T(128)S(1)} %pad_add_fusion.owners_ref, bf16[2,384,1024]{2,1,0:T(8,128)(2,1)S(1)} %get-tuple-element.89.refs_0_.refs_3_, bf16[2,288,1024]{2,1,0:T(8,128)(2,1)S(1)} %get-tuple-element.97.refs_1_.refs_4_, ...), custom_call_target="tpu_custom_call" | custom-call | tf_op jit(solution)/shard_map/bands/pallas_call | solution.py:280
  60.4 6.6 %collective-permute-done.10.refs_4_ = bf16[128,1024]{1,0:T(8,128)(2,1)S(1)} collective-permute-done((bf16[128,1024]{1,0:T(8,128)(2,1)S(1)}, bf16[128,1024]{1,0:T(8,128)(2,1)S(1)}, u32[]{:S(2)}, u32[]{:S(2)}) %collective-permute-start.10) | collective-permute-done | bytes 262176 | tf_op jit(solution)/shard_map/ppermute | solution.py:76
  67.0 0.5 collective-permute-start.13
  67.6 6.8 %collective-permute-done.13.refs_7_ = bf16[128,1024]{1,0:T(8,128)(2,1)S(1)} collective-permute-done((bf16[128,1024]{1,0:T(8,128)(2,1)S(1)}, bf16[128,1024]{1,0:T(8,128)(2,1)S(1)}, u32[]{:S(2)}, u32[]{:S(2)}) %collective-permute-start.13) | collective-permute-done | bytes 262176 | tf_op jit(solution)/shard_map/ppermute | solution.py:80
  74.4 3.9 %route.1 = (bf16[128,1536]{1,0:T(8,128)(2,1)S(1)}, bf16[128,1536]{1,0:T(8,128)(2,1)S(1)}, bf16[256,1536]{1,0:T(8,128)(2,1)S(1)}, bf16[2,768,1024]{2,1,0:T(8,128)(2,1)S(1)}) custom-call(s32[4]{0:T(128)S(1)} %pad_add_fusion.owners_ref, bf16[128,1024]{1,0:T(8,128)(2,1)S(1)} %copy-done.9, bf16[128,1024]{1,0:T(8,128)(2,1)S(1)} %collective-permute-done.1.refs_1_, ...), custom_call_target="tpu_custom_call" | custom-call | flops 2818572288 | bytes 10000000 | tf_op jit(solution)/shard_map/route/pallas_call | solution.py:327
  78.4 0.5 collective-permute-start.20
  79.0 1.1 %collective-permute-done.19 = bf16[128,1536]{1,0:T(8,128)(2,1)S(1)} collective-permute-done((bf16[128,1536]{1,0:T(8,128)(2,1)S(1)}, bf16[128,1536]{1,0:T(8,128)(2,1)S(1)}, u32[]{:S(2)}, u32[]{:S(2)}) %collective-permute-start.19) | collective-permute-done | bytes 393248 | tf_op jit(solution)/shard_map/ppermute | solution.py:468
  80.1 1.1 %collective-permute-done.20 = bf16[128,1536]{1,0:T(8,128)(2,1)S(1)} collective-permute-done((bf16[128,1536]{1,0:T(8,128)(2,1)S(1)}, bf16[128,1536]{1,0:T(8,128)(2,1)S(1)}, u32[]{:S(2)}, u32[]{:S(2)}) %collective-permute-start.20) | collective-permute-done | bytes 393248 | tf_op jit(solution)/shard_map/ppermute | solution.py:468
  81.3 1.1 %add_convert_fusion = bf16[256,1536]{1,0:T(8,128)(2,1)} fusion(bf16[256,1536]{1,0:T(8,128)(2,1)S(1)} %get-tuple-element.142, bf16[128,1536]{1,0:T(8,128)(2,1)S(1)} %collective-permute-done.20, bf16[128,1536]{1,0:T(8,128)(2,1)S(1)} %collective-permute-done.19), kind=kLoop, calls=%fused_computation | loop fusion | flops 2752512 | bytes 2359296 | tf_op jit(solution)/shard_map/convert_element_type | solution.py:479
  82.3 1.5 %collective-permute-start.21 = (bf16[256,1536]{1,0:T(8,128)(2,1)}, bf16[256,1536]{1,0:T(8,128)(2,1)S(1)}, u32[]{:S(2)}, u32[]{:S(2)}) collective-permute-start(bf16[256,1536]{1,0:T(8,128)(2,1)} %add_convert_fusion), channel_id=1, source_target_pairs={{0,16},{8,24},{16,0},{24,8},{1,17},{9,25},{17,1},{25,9},{2,18},{10... | collective-permute-start | bytes 2359304 | tf_op jit(solution)/shard_map/ppermute | solution.py:474
  83.9 3.2 %bands.5 = (bf16[256,1536]{1,0:T(8,128)(2,1)}, bf16[256,1536]{1,0:T(8,128)(2,1)S(1)}) custom-call(s32[4]{0:T(128)S(1)} %pad_add_fusion.owners_ref, bf16[2,768,1024]{2,1,0:T(8,128)(2,1)S(1)} %get-tuple-element.128.routed_ref.refs_0_.refs_1_, bf16[2,768,1024]{2,1,0:T(8,128)(2,1)S(1)} %get-tuple-element.128.routed_ref.refs_0_.refs_1_, ...), custom_call_target="tpu_custom_call" | custom-call | tf_op jit(solution)/shard_map/bands/pallas_call | solution.py:280
  87.1 5.3 %back.1 = (bf16[2,8,96,768]{3,2,1,0:T(8,128)(2,1)}, f32[8,2,128]{2,1,0:T(2,128)}) custom-call(s32[8]{0:T(128)S(1)} %stack.55.slots_ref, bf16[2,768,1024]{2,1,0:T(8,128)(2,1)S(1)} %get-tuple-element.128.routed_ref.refs_0_.refs_1_, bf16[2,768,2048]{2,1,0:T(8,128)(2,1)S(1)} %copy-done.1, bf16[2,768,2048]{2,1,0:T(8,128)(2,1)S(1)} %copy-done.1, ...), custom_call_target="tpu_custom_call" | custom-call | tf_op jit(solution)/shard_map/back/pallas_call | solution.py:387
  92.3 3.9 %all-to-all-start = ((f32[8,2,128]{2,1,0:T(2,128)}), f32[8,2,128]{2,1,0:T(2,128)S(1)}, u32[]{:S(2)}, u32[]{:S(2)}) async-start(f32[8,2,128]{2,1,0:T(2,128)} %get-tuple-element.133), calls=%async_computation | async-start | bytes 16384 | tf_op jit(solution)/shard_map/all_to_all | solution.py:528
  96.3 1.1 %copy-done.5 = bf16[256,1536]{1,0:T(8,128)(2,1)S(1)} copy-done((bf16[256,1536]{1,0:T(8,128)(2,1)S(1)}, bf16[256,1536]{1,0:T(8,128)(2,1)}, u32[]{:S(2)}) %copy-start.5) | copy-done | bytes 786456
  97.4 1.1 %copy-done.7 = bf16[256,1536]{1,0:T(8,128)(2,1)S(1)} copy-done((bf16[256,1536]{1,0:T(8,128)(2,1)S(1)}, bf16[256,1536]{1,0:T(8,128)(2,1)}, u32[]{:S(2)}) %copy-start.7) | copy-done | bytes 786456
  98.5 2.9 %rotate.2.refs_3_ = f32[512,2,768]{2,1,0:T(2,128)} custom-call(bf16[4,256,256]{2,1,0:T(8,128)(2,1)S(1)} %multiply_convert_fusion.turn_ref, bf16[256,1536]{1,0:T(8,128)(2,1)S(1)} %copy-done.7, bf16[256,1536]{1,0:T(8,128)(2,1)} %collective-permute-done.18.refs_1_, bf16[256,1536]{1,0:T(8,128)(2,1)S(1)} %copy-done.5), custom_call_target="tpu_custom_call" | custom-call | tf_op jit(solution)/shard_map/rotate/pallas_call | solution.py:426
  101.5 0.7 collective-permute-done.21.refs_2_
  102.1 1.9 %rotate.3 = f32[512,2,768]{2,1,0:T(2,128)} custom-call(bf16[4,256,256]{2,1,0:T(8,128)(2,1)S(1)} %multiply_convert_fusion.turn_ref, bf16[256,1536]{1,0:T(8,128)(2,1)S(1)} %get-tuple-element.135.refs_0_, bf16[256,1536]{1,0:T(8,128)(2,1)S(1)} %collective-permute-done.17.refs_1_, ...), custom_call_target="tpu_custom_call", output_to_operand_aliasing={{}: (4, {})} | custom-call | tf_op jit(solution)/shard_map/rotate/pallas_call | solution.py:426
  104.1 0.6 select_reduce_fusion
  (43 shorter events, 0.4 us)
Async XLA Ops:
  2.6 22.2 %copy-start.8 = (bf16[128,1152]{1,0:T(8,128)(2,1)S(1)}, bf16[128,1152]{1,0:T(8,128)(2,1)}, u32[]{:S(2)}) copy-start(bf16[128,1152]{1,0:T(8,128)(2,1)} %get-tuple-element.79.refs_0_) | copy-start | bytes 884740
  2.6 19.4 %collective-permute-start.3 = (bf16[128,1152]{1,0:T(8,128)(2,1)}, bf16[128,1152]{1,0:T(8,128)(2,1)S(1)}, u32[]{:S(2)}, u32[]{:S(2)}) collective-permute-start(bf16[128,1152]{1,0:T(8,128)(2,1)} %get-tuple-element.79.refs_0_), channel_id=1, source_target_pairs={{0,6},{1,7},{2,0},{3,1},{4,2},{5,3},{6,4},{7,5},{8,14},{9,15},{10,... | collective-permute-start | bytes 884744 | tf_op jit(solution)/shard_map/ppermute | solution.py:76
  7.7 14.3 %collective-permute-start.2 = (bf16[128,1152]{1,0:T(8,128)(2,1)}, bf16[128,1152]{1,0:T(8,128)(2,1)S(1)}, u32[]{:S(2)}, u32[]{:S(2)}) collective-permute-start(bf16[128,1152]{1,0:T(8,128)(2,1)} %get-tuple-element.79.refs_0_), channel_id=1, source_target_pairs={{0,2},{1,3},{2,4},{3,5},{4,6},{5,7},{6,0},{7,1},{8,10},{9,11},{10,... | collective-permute-start | bytes 884744 | tf_op jit(solution)/shard_map/ppermute | solution.py:76
  7.7 14.3 %collective-permute-start = (bf16[128,1152]{1,0:T(8,128)(2,1)}, bf16[128,1152]{1,0:T(8,128)(2,1)S(1)}, u32[]{:S(2)}, u32[]{:S(2)}) collective-permute-start(bf16[128,1152]{1,0:T(8,128)(2,1)} %get-tuple-element.79.refs_0_), channel_id=1, source_target_pairs={{0,1},{1,0},{2,3},{3,2},{4,5},{5,4},{6,7},{7,6},{8,9},{9,8},{10,11... | collective-permute-start | bytes 884744 | tf_op jit(solution)/shard_map/ppermute | solution.py:80
  9.2 12.8 %collective-permute-start.1 = (bf16[128,1024]{1,0:T(8,128)(2,1)}, bf16[128,1024]{1,0:T(8,128)(2,1)S(1)}, u32[]{:S(2)}, u32[]{:S(2)}) collective-permute-start(bf16[128,1024]{1,0:T(8,128)(2,1)} %get-tuple-element.107.refs_0_), channel_id=1, source_target_pairs={{0,1},{1,0},{2,3},{3,2},{4,5},{5,4},{6,7},{7,6},{8,9},{9,8},{10,11... | collective-permute-start | bytes 786440 | tf_op jit(solution)/shard_map/ppermute | solution.py:80
  22.0 15.1 %collective-permute-start.4 = (bf16[128,1152]{1,0:T(8,128)(2,1)}, bf16[128,1152]{1,0:T(8,128)(2,1)S(1)}, u32[]{:S(2)}, u32[]{:S(2)}) collective-permute-start(bf16[128,1152]{1,0:T(8,128)(2,1)} %get-tuple-element.79.refs_0_), channel_id=1, source_target_pairs={{0,4},{1,5},{2,6},{3,7},{4,0},{5,1},{6,2},{7,3},{8,12},{9,13},{10,... | collective-permute-start | bytes 884744 | tf_op jit(solution)/shard_map/ppermute | solution.py:76
  22.8 14.3 %collective-permute-start.5 = (bf16[128,1152]{1,0:T(8,128)(2,1)S(1)}, bf16[128,1152]{1,0:T(8,128)(2,1)S(1)}, u32[]{:S(2)}, u32[]{:S(2)}) collective-permute-start(bf16[128,1152]{1,0:T(8,128)(2,1)S(1)} %collective-permute-done.2.refs_2_), channel_id=1, source_target_pairs={{0,1},{1,0},{2,3},{3,2},{4,5},{5,4},{6,7},{7,6},{8,9},{9,8},{10,11... | collective-permute-start | bytes 884744 | tf_op jit(solution)/shard_map/ppermute | solution.py:80
  24.3 12.8 %collective-permute-start.6 = (bf16[128,1152]{1,0:T(8,128)(2,1)S(1)}, bf16[128,1152]{1,0:T(8,128)(2,1)S(1)}, u32[]{:S(2)}, u32[]{:S(2)}) collective-permute-start(bf16[128,1152]{1,0:T(8,128)(2,1)S(1)} %collective-permute-done.3.refs_3_), channel_id=1, source_target_pairs={{0,1},{1,0},{2,3},{3,2},{4,5},{5,4},{6,7},{7,6},{8,9},{9,8},{10,11... | collective-permute-start | bytes 884744 | tf_op jit(solution)/shard_map/ppermute | solution.py:80
  24.8 2.8 %copy-start = (bf16[2,768,2048]{2,1,0:T(8,128)(2,1)S(1)}, bf16[2,768,2048]{2,1,0:T(8,128)(2,1)}, u32[]{:S(2)}) copy-start(bf16[2,768,2048]{2,1,0:T(8,128)(2,1)} %refs_3_.5) | copy-start | bytes 18874372
  27.6 1.7 %copy-start.2 = (bf16[1,2,8,96,768]{4,3,2,1,0:T(8,128)(2,1)S(1)}, bf16[1,2,8,96,768]{4,3,2,1,0:T(8,128)(2,1)}, u32[]{:S(2)}) copy-start(bf16[1,2,8,96,768]{4,3,2,1,0:T(8,128)(2,1)} %param.9) | copy-start | bytes 7077892
  29.3 9.3 %copy-start.9 = (bf16[128,1024]{1,0:T(8,128)(2,1)S(1)}, bf16[128,1024]{1,0:T(8,128)(2,1)}, u32[]{:S(2)}) copy-start(bf16[128,1024]{1,0:T(8,128)(2,1)} %get-tuple-element.107.refs_0_) | copy-start | bytes 786436
  29.3 11.9 %copy-start.1 = (bf16[2,768,2048]{2,1,0:T(8,128)(2,1)S(1)}, bf16[2,768,2048]{2,1,0:T(8,128)(2,1)}, u32[]{:S(2)}) copy-start(bf16[2,768,2048]{2,1,0:T(8,128)(2,1)} %refs_3_.5) | copy-start | bytes 18874372
  29.3 11.9 %copy-start.3 = (bf16[1,2,8,96,768]{4,3,2,1,0:T(8,128)(2,1)S(1)}, bf16[1,2,8,96,768]{4,3,2,1,0:T(8,128)(2,1)}, u32[]{:S(2)}) copy-start(bf16[1,2,8,96,768]{4,3,2,1,0:T(8,128)(2,1)} %param.9) | copy-start | bytes 7077892
  37.0 8.1 %collective-permute-start.9 = (bf16[128,1152]{1,0:T(8,128)(2,1)S(1)}, bf16[128,1152]{1,0:T(8,128)(2,1)S(1)}, u32[]{:S(2)}, u32[]{:S(2)}) collective-permute-start(bf16[128,1152]{1,0:T(8,128)(2,1)S(1)} %collective-permute-done.4.refs_0_), channel_id=1, source_target_pairs={{0,1},{1,0},{2,3},{3,2},{4,5},{5,4},{6,7},{7,6},{8,9},{9,8},{10,11... | collective-permute-start | bytes 884744 | tf_op jit(solution)/shard_map/ppermute | solution.py:80
  38.5 11.9 %collective-permute-start.8 = (bf16[128,1024]{1,0:T(8,128)(2,1)S(1)}, bf16[128,1024]{1,0:T(8,128)(2,1)S(1)}, u32[]{:S(2)}, u32[]{:S(2)}) collective-permute-start(bf16[128,1024]{1,0:T(8,128)(2,1)S(1)} %copy-done.9), channel_id=1, source_target_pairs={{0,6},{1,7},{2,0},{3,1},{4,2},{5,3},{6,4},{7,5},{8,14},{9,15},{10,... | collective-permute-start | bytes 786440 | tf_op jit(solution)/shard_map/ppermute | solution.py:76
  40.8 11.0 %collective-permute-start.7 = (bf16[128,1024]{1,0:T(8,128)(2,1)S(1)}, bf16[128,1024]{1,0:T(8,128)(2,1)S(1)}, u32[]{:S(2)}, u32[]{:S(2)}) collective-permute-start(bf16[128,1024]{1,0:T(8,128)(2,1)S(1)} %copy-done.9), channel_id=1, source_target_pairs={{0,2},{1,3},{2,4},{3,5},{4,6},{5,7},{6,0},{7,1},{8,10},{9,11},{10,... | collective-permute-start | bytes 786440 | tf_op jit(solution)/shard_map/ppermute | solution.py:76
  51.8 3.6 %collective-permute-start.14 = (bf16[128,1536]{1,0:T(8,128)(2,1)S(1)}, bf16[128,1536]{1,0:T(8,128)(2,1)S(1)}, u32[]{:S(2)}, u32[]{:S(2)}) collective-permute-start(bf16[128,1536]{1,0:T(8,128)(2,1)S(1)} %get-tuple-element.125), channel_id=1, source_target_pairs={{0,8},{8,0},{16,24},{24,16},{1,9},{9,1},{17,25},{25,17},{2,10},{10... | collective-permute-start | bytes 1179656 | tf_op jit(solution)/shard_map/ppermute | solution.py:468
  51.8 3.6 %collective-permute-start.15 = (bf16[128,1536]{1,0:T(8,128)(2,1)S(1)}, bf16[128,1536]{1,0:T(8,128)(2,1)S(1)}, u32[]{:S(2)}, u32[]{:S(2)}) collective-permute-start(bf16[128,1536]{1,0:T(8,128)(2,1)S(1)} %get-tuple-element.126), channel_id=1, source_target_pairs={{0,8},{8,0},{16,24},{24,16},{1,9},{9,1},{17,25},{25,17},{2,10},{10... | collective-permute-start | bytes 1179656 | tf_op jit(solution)/shard_map/ppermute | solution.py:468
  52.3 14.7 %collective-permute-start.10 = (bf16[128,1024]{1,0:T(8,128)(2,1)S(1)}, bf16[128,1024]{1,0:T(8,128)(2,1)S(1)}, u32[]{:S(2)}, u32[]{:S(2)}) collective-permute-start(bf16[128,1024]{1,0:T(8,128)(2,1)S(1)} %copy-done.9), channel_id=1, source_target_pairs={{0,4},{1,5},{2,6},{3,7},{4,0},{5,1},{6,2},{7,3},{8,12},{9,13},{10,... | collective-permute-start | bytes 786440 | tf_op jit(solution)/shard_map/ppermute | solution.py:76
  53.3 13.7 %collective-permute-start.11 = (bf16[128,1024]{1,0:T(8,128)(2,1)S(1)}, bf16[128,1024]{1,0:T(8,128)(2,1)S(1)}, u32[]{:S(2)}, u32[]{:S(2)}) collective-permute-start(bf16[128,1024]{1,0:T(8,128)(2,1)S(1)} %collective-permute-done.7.refs_2_), channel_id=1, source_target_pairs={{0,1},{1,0},{2,3},{3,2},{4,5},{5,4},{6,7},{7,6},{8,9},{9,8},{10,11... | collective-permute-start | bytes 786440 | tf_op jit(solution)/shard_map/ppermute | solution.py:80
  53.9 13.2 %collective-permute-start.12 = (bf16[128,1024]{1,0:T(8,128)(2,1)S(1)}, bf16[128,1024]{1,0:T(8,128)(2,1)S(1)}, u32[]{:S(2)}, u32[]{:S(2)}) collective-permute-start(bf16[128,1024]{1,0:T(8,128)(2,1)S(1)} %collective-permute-done.8.refs_3_), channel_id=1, source_target_pairs={{0,1},{1,0},{2,3},{3,2},{4,5},{5,4},{6,7},{7,6},{8,9},{9,8},{10,11... | collective-permute-start | bytes 786440 | tf_op jit(solution)/shard_map/ppermute | solution.py:80
  55.6 22.8 %collective-permute-start.16 = (bf16[256,1536]{1,0:T(8,128)(2,1)S(1)}, bf16[256,1536]{1,0:T(8,128)(2,1)S(1)}, u32[]{:S(2)}, u32[]{:S(2)}) collective-permute-start(bf16[256,1536]{1,0:T(8,128)(2,1)S(1)} %add_convert_fusion.1), channel_id=1, source_target_pairs={{0,16},{8,24},{16,0},{24,8},{1,17},{9,25},{17,1},{25,9},{2,18},{10... | collective-permute-start | bytes 2359304 | tf_op jit(solution)/shard_map/ppermute | solution.py:474
  60.4 17.9 %copy-start.6 = (bf16[256,1536]{1,0:T(8,128)(2,1)}, bf16[256,1536]{1,0:T(8,128)(2,1)S(1)}, u32[]{:S(2)}) copy-start(bf16[256,1536]{1,0:T(8,128)(2,1)S(1)} %get-tuple-element.137.refs_0_) | copy-start | bytes 2359300
  67.0 7.4 %collective-permute-start.13 = (bf16[128,1024]{1,0:T(8,128)(2,1)S(1)}, bf16[128,1024]{1,0:T(8,128)(2,1)S(1)}, u32[]{:S(2)}, u32[]{:S(2)}) collective-permute-start(bf16[128,1024]{1,0:T(8,128)(2,1)S(1)} %collective-permute-done.10.refs_4_), channel_id=1, source_target_pairs={{0,1},{1,0},{2,3},{3,2},{4,5},{5,4},{6,7},{7,6},{8,9},{9,8},{10,11... | collective-permute-start | bytes 786440 | tf_op jit(solution)/shard_map/ppermute | solution.py:80
  78.3 8.7 %copy-start.4 = (bf16[256,1536]{1,0:T(8,128)(2,1)}, bf16[256,1536]{1,0:T(8,128)(2,1)S(1)}, u32[]{:S(2)}) copy-start(bf16[256,1536]{1,0:T(8,128)(2,1)S(1)} %collective-permute-done.16.refs_2_) | copy-start | bytes 2359300
  78.3 1.8 %collective-permute-start.19 = (bf16[128,1536]{1,0:T(8,128)(2,1)S(1)}, bf16[128,1536]{1,0:T(8,128)(2,1)S(1)}, u32[]{:S(2)}, u32[]{:S(2)}) collective-permute-start(bf16[128,1536]{1,0:T(8,128)(2,1)S(1)} %get-tuple-element.140), channel_id=1, source_target_pairs={{0,8},{8,0},{16,24},{24,16},{1,9},{9,1},{17,25},{25,17},{2,10},{10... | collective-permute-start | bytes 1179656 | tf_op jit(solution)/shard_map/ppermute | solution.py:468
  78.4 2.8 %collective-permute-start.20 = (bf16[128,1536]{1,0:T(8,128)(2,1)S(1)}, bf16[128,1536]{1,0:T(8,128)(2,1)S(1)}, u32[]{:S(2)}, u32[]{:S(2)}) collective-permute-start(bf16[128,1536]{1,0:T(8,128)(2,1)S(1)} %get-tuple-element.141), channel_id=1, source_target_pairs={{0,8},{8,0},{16,24},{24,16},{1,9},{9,1},{17,25},{25,17},{2,10},{10... | collective-permute-start | bytes 1179656 | tf_op jit(solution)/shard_map/ppermute | solution.py:468
  78.9 17.3 %collective-permute-start.18 = (bf16[256,1536]{1,0:T(8,128)(2,1)}, bf16[256,1536]{1,0:T(8,128)(2,1)}, u32[]{:S(2)}, u32[]{:S(2)}) collective-permute-start(bf16[256,1536]{1,0:T(8,128)(2,1)} %get-tuple-element.138), channel_id=1, source_target_pairs={{0,8},{8,0},{16,24},{24,16},{1,9},{9,1},{17,25},{25,17},{2,10},{10... | collective-permute-start | bytes 2359304 | tf_op jit(solution)/shard_map/ppermute | solution.py:468
  82.3 19.8 %collective-permute-start.21 = (bf16[256,1536]{1,0:T(8,128)(2,1)}, bf16[256,1536]{1,0:T(8,128)(2,1)S(1)}, u32[]{:S(2)}, u32[]{:S(2)}) collective-permute-start(bf16[256,1536]{1,0:T(8,128)(2,1)} %add_convert_fusion), channel_id=1, source_target_pairs={{0,16},{8,24},{16,0},{24,8},{1,17},{9,25},{17,1},{25,9},{2,18},{10... | collective-permute-start | bytes 2359304 | tf_op jit(solution)/shard_map/ppermute | solution.py:474
  87.1 15.1 %collective-permute-start.17 = (bf16[256,1536]{1,0:T(8,128)(2,1)}, bf16[256,1536]{1,0:T(8,128)(2,1)S(1)}, u32[]{:S(2)}, u32[]{:S(2)}) collective-permute-start(bf16[256,1536]{1,0:T(8,128)(2,1)} %get-tuple-element.136), channel_id=1, source_target_pairs={{0,8},{8,0},{16,24},{24,16},{1,9},{9,1},{17,25},{25,17},{2,10},{10... | collective-permute-start | bytes 2359304 | tf_op jit(solution)/shard_map/ppermute | solution.py:468
  92.3 11.7 %all-to-all-start = ((f32[8,2,128]{2,1,0:T(2,128)}), f32[8,2,128]{2,1,0:T(2,128)S(1)}, u32[]{:S(2)}, u32[]{:S(2)}) async-start(f32[8,2,128]{2,1,0:T(2,128)} %get-tuple-element.133), calls=%async_computation | async-start | bytes 16384 | tf_op jit(solution)/shard_map/all_to_all | solution.py:528
  96.3 1.1 %copy-start.5 = (bf16[256,1536]{1,0:T(8,128)(2,1)S(1)}, bf16[256,1536]{1,0:T(8,128)(2,1)}, u32[]{:S(2)}) copy-start(bf16[256,1536]{1,0:T(8,128)(2,1)} %copy-done.4) | copy-start | bytes 2359300
  97.4 1.1 %copy-start.7 = (bf16[256,1536]{1,0:T(8,128)(2,1)S(1)}, bf16[256,1536]{1,0:T(8,128)(2,1)}, u32[]{:S(2)}) copy-start(bf16[256,1536]{1,0:T(8,128)(2,1)} %copy-done.6) | copy-start | bytes 2359300
  102.1 1.9 %copy-start.10 = (s32[128,8]{0,1:T(8,128)S(1)}, s32[128,8]{0,1:T(8,128)}, u32[]{:S(2)}) copy-start(s32[128,8]{0,1:T(8,128)} %param.8) | copy-start | bytes 12292

commit v7 on v6

--- a/solution.py
+++ b/solution.py
@@ -518,9 +518,10 @@
 
     weighted = [made[1] for made in a_made]
     tables = [made[2] for made in a_made]
-    made = route(b_parts, tables, weighted, owned, away_bands)
+    made = route(b_parts, tables, weighted, owned, away_bands[:1])
     made, a_arrived = fence(made, a_arrived)
-    *away_send, away_keep, routed_b = made
+    *away_send, routed_b = made
+    (away_keep,) = grad_bands([routed_b], weighted, owned, away_bands[1:], halves=False)
     here_send_b, here_keep_b = grad_bands([routed_b], weighted, owned, here_bands, halves=False)
     b_arrived = to_chips(add_swapped(away_send, away_keep))
     here_got, here_got_b = swap(here_send), swap(here_send_b)

time: 105 us -> 105 us (level)
  waiting for transfers between devices: 33.7 us -> 32 us
  Pallas kernels: 34.4 us -> 35.5 us
    pallas_call x3 -> x4, Pallas kernels: 9.17 us -> 10.9 us  [grad_bands(): pl.pallas_call(functools.partial(bands_kernel, len(wanted), len(routed),...]
    ppermute x6, waiting for transfers between devices: 2.27 us -> 0.55 us  [swap(): return lax.ppermute(value, 'dp', [(i, i ^ 1) for i in range(replicas)])]
  transfers between devices with their start and end apart: 23 -> 23, of which waited for: 9 -> 8; matrix products, arithmetic and copies ran while one was open for 2% -> 2% of each run, Pallas kernels for 31% -> 32%
where the time goes in v7:
time: 105 us
  Pallas kernels  35.5 us (34%)
  waiting for transfers between devices  32 us (30%)
  starting transfers between devices  25.7 us (24%)
  local copies, waits for them, and re-layouts  7.69 us (7%)
  other arithmetic  3.11 us (3%)
    ppermute x8, waiting for transfers between devices, across(): return lax.ppermute(value, 'expert', [(i, i ^ 1) for i in range(2 * LINES)])  18.6 us
    ppermute x6, waiting for transfers between devices, along(): lax.ppermute(value, 'expert', [(2 * a + x, 2 * b + x) for a, b in pairs f...  12.1 us
    pallas_call x4, Pallas kernels, grad_bands(): pl.pallas_call(functools.partial(bands_kernel, len(wanted), len(routed),...  10.9 us
    ppermute x6, starting transfers between devices, along(): lax.ppermute(value, 'expert', [(2 * a + x, 2 * b + x) for a, b in pairs f...  9.48 us
    pallas_call x3, Pallas kernels, visit(): pl.pallas_call(functools.partial(visit_kernel, len(parts), len(shares), b...  9.27 us
    ppermute x8, starting transfers between devices, across(): return lax.ppermute(value, 'expert', [(i, i ^ 1) for i in range(2 * LINES)])  8.11 us
    unnamed x24, local copies, waits for them, and re-layouts  7.6 us
    pallas_call x1, Pallas kernels, back(): pl.pallas_call(functools.partial(back_kernel, replicas, len(seen), len(la...  5.25 us
  transfers between devices with their start and end apart: 23, of which 8 were waited for; matrix products, arithmetic and copies ran while one was open for 2% of the time, Pallas kernels for 32%

profile of v7, /device:TPU:0, one launch (start us, length us, event | category | flops | bytes accessed | tf_op | source)
XLA Modules:
  0.0 104.8 jit_solution(12629150125673513636)
XLA Ops:
  0.6 2.0 %pack.1 = (bf16[128,1152]{1,0:T(8,128)(2,1)}, bf16[128,1024]{1,0:T(8,128)(2,1)}) custom-call(bf16[128,2048]{1,0:T(8,128)(2,1)} %cot_ref.1, bf16[8,128]{1,0:T(8,128)(2,1)} %bitcast.34, s32[8,128]{1,0:T(8,128)} %bitcast.31), custom_call_target="tpu_custom_call" | custom-call | tf_op jit(solution)/shard_map/pack/pallas_call | solution.py:63
  2.6 5.0 %collective-permute-start.3 = (bf16[128,1152]{1,0:T(8,128)(2,1)}, bf16[128,1152]{1,0:T(8,128)(2,1)S(1)}, u32[]{:S(2)}, u32[]{:S(2)}) collective-permute-start(bf16[128,1152]{1,0:T(8,128)(2,1)} %get-tuple-element.77.refs_0_), channel_id=1, source_target_pairs={{0,6},{1,7},{2,0},{3,1},{4,2},{5,3},{6,4},{7,5},{8,14},{9,15},{10,... | collective-permute-start | bytes 884744 | tf_op jit(solution)/shard_map/ppermute | solution.py:76
  7.7 1.5 %collective-permute-start = (bf16[128,1152]{1,0:T(8,128)(2,1)}, bf16[128,1152]{1,0:T(8,128)(2,1)S(1)}, u32[]{:S(2)}, u32[]{:S(2)}) collective-permute-start(bf16[128,1152]{1,0:T(8,128)(2,1)} %get-tuple-element.77.refs_0_), channel_id=1, source_target_pairs={{0,1},{1,0},{2,3},{3,2},{4,5},{5,4},{6,7},{7,6},{8,9},{9,8},{10,11... | collective-permute-start | bytes 884744 | tf_op jit(solution)/shard_map/ppermute | solution.py:80
  9.2 0.5 collective-permute-start.1
  9.7 0.8 fusion.18
  10.5 0.3 fusion.10
  11.1 10.9 %collective-permute-done.1.refs_1_ = bf16[128,1024]{1,0:T(8,128)(2,1)S(1)} collective-permute-done((bf16[128,1024]{1,0:T(8,128)(2,1)}, bf16[128,1024]{1,0:T(8,128)(2,1)S(1)}, u32[]{:S(2)}, u32[]{:S(2)}) %collective-permute-start.1) | collective-permute-done | bytes 262176 | tf_op jit(solution)/shard_map/ppermute | solution.py:80
  22.0 0.8 collective-permute-start.4
  22.8 1.5 %collective-permute-start.5 = (bf16[128,1152]{1,0:T(8,128)(2,1)S(1)}, bf16[128,1152]{1,0:T(8,128)(2,1)S(1)}, u32[]{:S(2)}, u32[]{:S(2)}) collective-permute-start(bf16[128,1152]{1,0:T(8,128)(2,1)S(1)} %collective-permute-done.2.refs_2_), channel_id=1, source_target_pairs={{0,1},{1,0},{2,3},{3,2},{4,5},{5,4},{6,7},{7,6},{8,9},{9,8},{10,11... | collective-permute-start | bytes 884744 | tf_op jit(solution)/shard_map/ppermute | solution.py:80
  24.3 0.5 collective-permute-start.6
  24.8 2.8 %copy-done = bf16[2,768,2048]{2,1,0:T(8,128)(2,1)S(1)} copy-done((bf16[2,768,2048]{2,1,0:T(8,128)(2,1)S(1)}, bf16[2,768,2048]{2,1,0:T(8,128)(2,1)}, u32[]{:S(2)}) %copy-start) | copy-done | bytes 6291480
  27.6 1.7 %copy-done.2 = bf16[1,2,8,96,768]{4,3,2,1,0:T(8,128)(2,1)S(1)} copy-done((bf16[1,2,8,96,768]{4,3,2,1,0:T(8,128)(2,1)S(1)}, bf16[1,2,8,96,768]{4,3,2,1,0:T(8,128)(2,1)}, u32[]{:S(2)}) %copy-start.2) | copy-done | bytes 2359320
  29.3 3.6 %visit.3 = (bf16[2,384,1024]{2,1,0:T(8,128)(2,1)S(1)}, bf16[2,384,768]{2,1,0:T(8,128)(2,1)S(1)}, f32[4,8,128]{2,1,0:T(8,128)S(1)}, bf16[2,384,768]{2,1,0:T(8,128)(2,1)S(1)}) custom-call(s32[8]{0:T(128)S(1)} %stack.55.slots_ref, bf16[128,1152]{1,0:T(8,128)(2,1)S(1)} %copy-done.8, bf16[128,1152]{1,0:T(8,128)(2,1)S(1)} %collective-permute-done.refs_1_, ...), custom_call_target="tpu_custom_call" | custom-call | tf_op jit(solution)/shard_map/visit/pallas_call | solution.py:217
  32.9 4.1 %collective-permute-done.4.refs_0_ = bf16[128,1152]{1,0:T(8,128)(2,1)S(1)} collective-permute-done((bf16[128,1152]{1,0:T(8,128)(2,1)}, bf16[128,1152]{1,0:T(8,128)(2,1)S(1)}, u32[]{:S(2)}, u32[]{:S(2)}) %collective-permute-start.4) | collective-permute-done | bytes 294944 | tf_op jit(solution)/shard_map/ppermute | solution.py:76
  37.0 1.5 %collective-permute-start.9 = (bf16[128,1152]{1,0:T(8,128)(2,1)S(1)}, bf16[128,1152]{1,0:T(8,128)(2,1)S(1)}, u32[]{:S(2)}, u32[]{:S(2)}) collective-permute-start(bf16[128,1152]{1,0:T(8,128)(2,1)S(1)} %collective-permute-done.4.refs_0_), channel_id=1, source_target_pairs={{0,1},{1,0},{2,3},{3,2},{4,5},{5,4},{6,7},{7,6},{8,9},{9,8},{10,11... | collective-permute-start | bytes 884744 | tf_op jit(solution)/shard_map/ppermute | solution.py:80
  38.5 2.3 %collective-permute-start.8 = (bf16[128,1024]{1,0:T(8,128)(2,1)S(1)}, bf16[128,1024]{1,0:T(8,128)(2,1)S(1)}, u32[]{:S(2)}, u32[]{:S(2)}) collective-permute-start(bf16[128,1024]{1,0:T(8,128)(2,1)S(1)} %copy-done.9), channel_id=1, source_target_pairs={{0,6},{1,7},{2,0},{3,1},{4,2},{5,3},{6,4},{7,5},{8,14},{9,15},{10,... | collective-permute-start | bytes 786440 | tf_op jit(solution)/shard_map/ppermute | solution.py:76
  40.8 0.3 collective-permute-start.7
  41.1 3.1 %visit.4 = (bf16[2,288,1024]{2,1,0:T(8,128)(2,1)S(1)}, bf16[2,288,768]{2,1,0:T(8,128)(2,1)S(1)}, f32[3,8,128]{2,1,0:T(8,128)S(1)}, bf16[2,288,768]{2,1,0:T(8,128)(2,1)S(1)}) custom-call(s32[8]{0:T(128)S(1)} %stack.55.slots_ref, bf16[128,1152]{1,0:T(8,128)(2,1)S(1)} %collective-permute-done.4.refs_0_, bf16[128,1152]{1,0:T(8,128)(2,1)S(1)} %collective-permute-done.5.refs_1_, ...), custom_call_target="tpu_custom_call" | custom-call | tf_op jit(solution)/shard_map/visit/pallas_call | solution.py:217
  44.3 0.9 collective-permute-done.9.refs_0_
  45.2 2.5 %visit.5 = (bf16[2,96,1024]{2,1,0:T(8,128)(2,1)S(1)}, bf16[2,96,768]{2,1,0:T(8,128)(2,1)S(1)}, f32[1,8,128]{2,1,0:T(8,128)S(1)}, bf16[2,96,768]{2,1,0:T(8,128)(2,1)S(1)}) custom-call(s32[8]{0:T(128)S(1)} %stack.55.slots_ref, bf16[128,1152]{1,0:T(8,128)(2,1)S(1)} %collective-permute-done.9.refs_0_, bf16[2,768,2048]{2,1,0:T(8,128)(2,1)S(1)} %copy-done.1, ...), custom_call_target="tpu_custom_call" | custom-call | tf_op jit(solution)/shard_map/visit/pallas_call | solution.py:217
  47.7 2.7 %bands.4 = (bf16[128,1536]{1,0:T(8,128)(2,1)S(1)}, bf16[128,1536]{1,0:T(8,128)(2,1)S(1)}, bf16[256,1536]{1,0:T(8,128)(2,1)S(1)}) custom-call(s32[4]{0:T(128)S(1)} %pad_add_fusion.owners_ref, bf16[2,384,1024]{2,1,0:T(8,128)(2,1)S(1)} %get-tuple-element.87.refs_0_.refs_3_, bf16[2,288,1024]{2,1,0:T(8,128)(2,1)S(1)} %get-tuple-element.95.refs_1_.refs_4_, ...), custom_call_target="tpu_custom_call" | custom-call | tf_op jit(solution)/shard_map/bands/pallas_call | solution.py:280
  50.4 1.4 %collective-permute-done.7.refs_2_ = bf16[128,1024]{1,0:T(8,128)(2,1)S(1)} collective-permute-done((bf16[128,1024]{1,0:T(8,128)(2,1)S(1)}, bf16[128,1024]{1,0:T(8,128)(2,1)S(1)}, u32[]{:S(2)}, u32[]{:S(2)}) %collective-permute-start.7) | collective-permute-done | bytes 262176 | tf_op jit(solution)/shard_map/ppermute | solution.py:76
  51.8 0.5 collective-permute-start.15
  52.3 1.0 collective-permute-start.10
  53.3 0.5 collective-permute-start.11
  53.9 1.5 %collective-permute-start.12 = (bf16[128,1024]{1,0:T(8,128)(2,1)S(1)}, bf16[128,1024]{1,0:T(8,128)(2,1)S(1)}, u32[]{:S(2)}, u32[]{:S(2)}) collective-permute-start(bf16[128,1024]{1,0:T(8,128)(2,1)S(1)} %collective-permute-done.8.refs_3_), channel_id=1, source_target_pairs={{0,1},{1,0},{2,3},{3,2},{4,5},{5,4},{6,7},{7,6},{8,9},{9,8},{10,11... | collective-permute-start | bytes 786440 | tf_op jit(solution)/shard_map/ppermute | solution.py:80
  55.4 0.2 add_convert_fusion.1
  55.6 1.6 %collective-permute-start.16 = (bf16[256,1536]{1,0:T(8,128)(2,1)S(1)}, bf16[256,1536]{1,0:T(8,128)(2,1)S(1)}, u32[]{:S(2)}, u32[]{:S(2)}) collective-permute-start(bf16[256,1536]{1,0:T(8,128)(2,1)S(1)} %add_convert_fusion.1), channel_id=1, source_target_pairs={{0,16},{8,24},{16,0},{24,8},{1,17},{9,25},{17,1},{25,9},{2,18},{10... | collective-permute-start | bytes 2359304 | tf_op jit(solution)/shard_map/ppermute | solution.py:474
  57.1 3.3 %bands.5 = (bf16[256,1536]{1,0:T(8,128)(2,1)}, bf16[256,1536]{1,0:T(8,128)(2,1)S(1)}) custom-call(s32[4]{0:T(128)S(1)} %pad_add_fusion.owners_ref, bf16[2,384,1024]{2,1,0:T(8,128)(2,1)S(1)} %get-tuple-element.87.refs_0_.refs_3_, bf16[2,288,1024]{2,1,0:T(8,128)(2,1)S(1)} %get-tuple-element.95.refs_1_.refs_4_, ...), custom_call_target="tpu_custom_call" | custom-call | tf_op jit(solution)/shard_map/bands/pallas_call | solution.py:280
  60.4 6.6 %collective-permute-done.10.refs_4_ = bf16[128,1024]{1,0:T(8,128)(2,1)S(1)} collective-permute-done((bf16[128,1024]{1,0:T(8,128)(2,1)S(1)}, bf16[128,1024]{1,0:T(8,128)(2,1)S(1)}, u32[]{:S(2)}, u32[]{:S(2)}) %collective-permute-start.10) | collective-permute-done | bytes 262176 | tf_op jit(solution)/shard_map/ppermute | solution.py:76
  67.0 0.5 collective-permute-start.13
  67.6 6.8 %collective-permute-done.13.refs_7_ = bf16[128,1024]{1,0:T(8,128)(2,1)S(1)} collective-permute-done((bf16[128,1024]{1,0:T(8,128)(2,1)S(1)}, bf16[128,1024]{1,0:T(8,128)(2,1)S(1)}, u32[]{:S(2)}, u32[]{:S(2)}) %collective-permute-start.13) | collective-permute-done | bytes 262176 | tf_op jit(solution)/shard_map/ppermute | solution.py:80
  74.4 3.2 %route.1 = (bf16[128,1536]{1,0:T(8,128)(2,1)S(1)}, bf16[128,1536]{1,0:T(8,128)(2,1)S(1)}, bf16[2,768,1024]{2,1,0:T(8,128)(2,1)S(1)}) custom-call(s32[4]{0:T(128)S(1)} %pad_add_fusion.owners_ref, bf16[128,1024]{1,0:T(8,128)(2,1)S(1)} %copy-done.9, bf16[128,1024]{1,0:T(8,128)(2,1)S(1)} %collective-permute-done.1.refs_1_, ...), custom_call_target="tpu_custom_call" | custom-call | flops 2818572288 | bytes 10000000 | tf_op jit(solution)/shard_map/route/pallas_call | solution.py:327
  77.7 0.9 copy-done.4
  78.5 0.5 collective-permute-start.20
  79.0 1.8 %bands.7 = bf16[256,1536]{1,0:T(8,128)(2,1)S(1)} custom-call(s32[4]{0:T(128)S(1)} %pad_add_fusion.owners_ref, bf16[2,768,1024]{2,1,0:T(8,128)(2,1)S(1)} %get-tuple-element.125.routed_ref.refs_0_.refs_1_, bf16[2,384,768]{2,1,0:T(8,128)(2,1)S(1)} %get-tuple-element.98.refs_6_.refs_11_.refs_2_.refs_1_, ...), custom_call_target="tpu_custom_call" | custom-call | tf_op jit(solution)/shard_map/bands/pallas_call | solution.py:280
  80.8 0.5 collective-permute-done.20
  81.4 1.1 %add_convert_fusion = bf16[256,1536]{1,0:T(8,128)(2,1)} fusion(bf16[256,1536]{1,0:T(8,128)(2,1)S(1)} %bands.7, bf16[128,1536]{1,0:T(8,128)(2,1)S(1)} %collective-permute-done.20, bf16[128,1536]{1,0:T(8,128)(2,1)S(1)} %collective-permute-done.19), kind=kLoop, calls=%fused_computation | loop fusion | flops 2752512 | bytes 2359296 | tf_op jit(solution)/shard_map/convert_element_type | solution.py:479
  82.4 1.5 %collective-permute-start.21 = (bf16[256,1536]{1,0:T(8,128)(2,1)}, bf16[256,1536]{1,0:T(8,128)(2,1)S(1)}, u32[]{:S(2)}, u32[]{:S(2)}) collective-permute-start(bf16[256,1536]{1,0:T(8,128)(2,1)} %add_convert_fusion), channel_id=1, source_target_pairs={{0,16},{8,24},{16,0},{24,8},{1,17},{9,25},{17,1},{25,9},{2,18},{10... | collective-permute-start | bytes 2359304 | tf_op jit(solution)/shard_map/ppermute | solution.py:474
  84.0 3.2 %bands.6 = (bf16[256,1536]{1,0:T(8,128)(2,1)}, bf16[256,1536]{1,0:T(8,128)(2,1)S(1)}) custom-call(s32[4]{0:T(128)S(1)} %pad_add_fusion.owners_ref, bf16[2,768,1024]{2,1,0:T(8,128)(2,1)S(1)} %get-tuple-element.125.routed_ref.refs_0_.refs_1_, bf16[2,768,1024]{2,1,0:T(8,128)(2,1)S(1)} %get-tuple-element.125.routed_ref.refs_0_.refs_1_, ...), custom_call_target="tpu_custom_call" | custom-call | tf_op jit(solution)/shard_map/bands/pallas_call | solution.py:280
  87.2 5.2 %back.1 = (bf16[2,8,96,768]{3,2,1,0:T(8,128)(2,1)}, f32[8,2,128]{2,1,0:T(2,128)}) custom-call(s32[8]{0:T(128)S(1)} %stack.55.slots_ref, bf16[2,768,1024]{2,1,0:T(8,128)(2,1)S(1)} %get-tuple-element.125.routed_ref.refs_0_.refs_1_, bf16[2,768,2048]{2,1,0:T(8,128)(2,1)S(1)} %copy-done.1, bf16[2,768,2048]{2,1,0:T(8,128)(2,1)S(1)} %copy-done.1, ...), custom_call_target="tpu_custom_call" | custom-call | tf_op jit(solution)/shard_map/back/pallas_call | solution.py:387
  92.4 3.9 %all-to-all-start = ((f32[8,2,128]{2,1,0:T(2,128)}), f32[8,2,128]{2,1,0:T(2,128)S(1)}, u32[]{:S(2)}, u32[]{:S(2)}) async-start(f32[8,2,128]{2,1,0:T(2,128)} %get-tuple-element.130), calls=%async_computation | async-start | bytes 16384 | tf_op jit(solution)/shard_map/all_to_all | solution.py:529
  96.4 1.1 %copy-done.5 = bf16[256,1536]{1,0:T(8,128)(2,1)S(1)} copy-done((bf16[256,1536]{1,0:T(8,128)(2,1)S(1)}, bf16[256,1536]{1,0:T(8,128)(2,1)}, u32[]{:S(2)}) %copy-start.5) | copy-done | bytes 786456
  97.5 1.1 %copy-done.7 = bf16[256,1536]{1,0:T(8,128)(2,1)S(1)} copy-done((bf16[256,1536]{1,0:T(8,128)(2,1)S(1)}, bf16[256,1536]{1,0:T(8,128)(2,1)}, u32[]{:S(2)}) %copy-start.7) | copy-done | bytes 786456
  98.6 2.9 %rotate.2.refs_3_ = f32[512,2,768]{2,1,0:T(2,128)} custom-call(bf16[4,256,256]{2,1,0:T(8,128)(2,1)S(1)} %multiply_convert_fusion.turn_ref, bf16[256,1536]{1,0:T(8,128)(2,1)S(1)} %copy-done.7, bf16[256,1536]{1,0:T(8,128)(2,1)} %collective-permute-done.18.refs_1_, bf16[256,1536]{1,0:T(8,128)(2,1)S(1)} %copy-done.5), custom_call_target="tpu_custom_call" | custom-call | tf_op jit(solution)/shard_map/rotate/pallas_call | solution.py:426
  101.6 0.7 collective-permute-done.21.refs_2_
  102.2 1.9 %rotate.3 = f32[512,2,768]{2,1,0:T(2,128)} custom-call(bf16[4,256,256]{2,1,0:T(8,128)(2,1)S(1)} %multiply_convert_fusion.turn_ref, bf16[256,1536]{1,0:T(8,128)(2,1)S(1)} %get-tuple-element.132.refs_0_, bf16[256,1536]{1,0:T(8,128)(2,1)S(1)} %collective-permute-done.17.refs_1_, ...), custom_call_target="tpu_custom_call", output_to_operand_aliasing={{}: (4, {})} | custom-call | tf_op jit(solution)/shard_map/rotate/pallas_call | solution.py:426
  104.2 0.6 select_reduce_fusion
  (44 shorter events, 0.4 us)
Async XLA Ops:
  2.6 22.2 %copy-start.8 = (bf16[128,1152]{1,0:T(8,128)(2,1)S(1)}, bf16[128,1152]{1,0:T(8,128)(2,1)}, u32[]{:S(2)}) copy-start(bf16[128,1152]{1,0:T(8,128)(2,1)} %get-tuple-element.77.refs_0_) | copy-start | bytes 884740
  2.6 19.4 %collective-permute-start.3 = (bf16[128,1152]{1,0:T(8,128)(2,1)}, bf16[128,1152]{1,0:T(8,128)(2,1)S(1)}, u32[]{:S(2)}, u32[]{:S(2)}) collective-permute-start(bf16[128,1152]{1,0:T(8,128)(2,1)} %get-tuple-element.77.refs_0_), channel_id=1, source_target_pairs={{0,6},{1,7},{2,0},{3,1},{4,2},{5,3},{6,4},{7,5},{8,14},{9,15},{10,... | collective-permute-start | bytes 884744 | tf_op jit(solution)/shard_map/ppermute | solution.py:76
  7.7 14.3 %collective-permute-start.2 = (bf16[128,1152]{1,0:T(8,128)(2,1)}, bf16[128,1152]{1,0:T(8,128)(2,1)S(1)}, u32[]{:S(2)}, u32[]{:S(2)}) collective-permute-start(bf16[128,1152]{1,0:T(8,128)(2,1)} %get-tuple-element.77.refs_0_), channel_id=1, source_target_pairs={{0,2},{1,3},{2,4},{3,5},{4,6},{5,7},{6,0},{7,1},{8,10},{9,11},{10,... | collective-permute-start | bytes 884744 | tf_op jit(solution)/shard_map/ppermute | solution.py:76
  7.7 14.3 %collective-permute-start = (bf16[128,1152]{1,0:T(8,128)(2,1)}, bf16[128,1152]{1,0:T(8,128)(2,1)S(1)}, u32[]{:S(2)}, u32[]{:S(2)}) collective-permute-start(bf16[128,1152]{1,0:T(8,128)(2,1)} %get-tuple-element.77.refs_0_), channel_id=1, source_target_pairs={{0,1},{1,0},{2,3},{3,2},{4,5},{5,4},{6,7},{7,6},{8,9},{9,8},{10,11... | collective-permute-start | bytes 884744 | tf_op jit(solution)/shard_map/ppermute | solution.py:80
  9.2 12.8 %collective-permute-start.1 = (bf16[128,1024]{1,0:T(8,128)(2,1)}, bf16[128,1024]{1,0:T(8,128)(2,1)S(1)}, u32[]{:S(2)}, u32[]{:S(2)}) collective-permute-start(bf16[128,1024]{1,0:T(8,128)(2,1)} %get-tuple-element.105.refs_0_), channel_id=1, source_target_pairs={{0,1},{1,0},{2,3},{3,2},{4,5},{5,4},{6,7},{7,6},{8,9},{9,8},{10,11... | collective-permute-start | bytes 786440 | tf_op jit(solution)/shard_map/ppermute | solution.py:80
  22.0 15.1 %collective-permute-start.4 = (bf16[128,1152]{1,0:T(8,128)(2,1)}, bf16[128,1152]{1,0:T(8,128)(2,1)S(1)}, u32[]{:S(2)}, u32[]{:S(2)}) collective-permute-start(bf16[128,1152]{1,0:T(8,128)(2,1)} %get-tuple-element.77.refs_0_), channel_id=1, source_target_pairs={{0,4},{1,5},{2,6},{3,7},{4,0},{5,1},{6,2},{7,3},{8,12},{9,13},{10,... | collective-permute-start | bytes 884744 | tf_op jit(solution)/shard_map/ppermute | solution.py:76
  22.8 14.3 %collective-permute-start.5 = (bf16[128,1152]{1,0:T(8,128)(2,1)S(1)}, bf16[128,1152]{1,0:T(8,128)(2,1)S(1)}, u32[]{:S(2)}, u32[]{:S(2)}) collective-permute-start(bf16[128,1152]{1,0:T(8,128)(2,1)S(1)} %collective-permute-done.2.refs_2_), channel_id=1, source_target_pairs={{0,1},{1,0},{2,3},{3,2},{4,5},{5,4},{6,7},{7,6},{8,9},{9,8},{10,11... | collective-permute-start | bytes 884744 | tf_op jit(solution)/shard_map/ppermute | solution.py:80
  24.3 12.8 %collective-permute-start.6 = (bf16[128,1152]{1,0:T(8,128)(2,1)S(1)}, bf16[128,1152]{1,0:T(8,128)(2,1)S(1)}, u32[]{:S(2)}, u32[]{:S(2)}) collective-permute-start(bf16[128,1152]{1,0:T(8,128)(2,1)S(1)} %collective-permute-done.3.refs_3_), channel_id=1, source_target_pairs={{0,1},{1,0},{2,3},{3,2},{4,5},{5,4},{6,7},{7,6},{8,9},{9,8},{10,11... | collective-permute-start | bytes 884744 | tf_op jit(solution)/shard_map/ppermute | solution.py:80
  24.8 2.8 %copy-start = (bf16[2,768,2048]{2,1,0:T(8,128)(2,1)S(1)}, bf16[2,768,2048]{2,1,0:T(8,128)(2,1)}, u32[]{:S(2)}) copy-start(bf16[2,768,2048]{2,1,0:T(8,128)(2,1)} %refs_3_.5) | copy-start | bytes 18874372
  27.6 1.7 %copy-start.2 = (bf16[1,2,8,96,768]{4,3,2,1,0:T(8,128)(2,1)S(1)}, bf16[1,2,8,96,768]{4,3,2,1,0:T(8,128)(2,1)}, u32[]{:S(2)}) copy-start(bf16[1,2,8,96,768]{4,3,2,1,0:T(8,128)(2,1)} %param.9) | copy-start | bytes 7077892
  29.3 9.3 %copy-start.9 = (bf16[128,1024]{1,0:T(8,128)(2,1)S(1)}, bf16[128,1024]{1,0:T(8,128)(2,1)}, u32[]{:S(2)}) copy-start(bf16[128,1024]{1,0:T(8,128)(2,1)} %get-tuple-element.105.refs_0_) | copy-start | bytes 786436
  29.3 11.9 %copy-start.1 = (bf16[2,768,2048]{2,1,0:T(8,128)(2,1)S(1)}, bf16[2,768,2048]{2,1,0:T(8,128)(2,1)}, u32[]{:S(2)}) copy-start(bf16[2,768,2048]{2,1,0:T(8,128)(2,1)} %refs_3_.5) | copy-start | bytes 18874372
  29.3 11.9 %copy-start.3 = (bf16[1,2,8,96,768]{4,3,2,1,0:T(8,128)(2,1)S(1)}, bf16[1,2,8,96,768]{4,3,2,1,0:T(8,128)(2,1)}, u32[]{:S(2)}) copy-start(bf16[1,2,8,96,768]{4,3,2,1,0:T(8,128)(2,1)} %param.9) | copy-start | bytes 7077892
  37.0 8.1 %collective-permute-start.9 = (bf16[128,1152]{1,0:T(8,128)(2,1)S(1)}, bf16[128,1152]{1,0:T(8,128)(2,1)S(1)}, u32[]{:S(2)}, u32[]{:S(2)}) collective-permute-start(bf16[128,1152]{1,0:T(8,128)(2,1)S(1)} %collective-permute-done.4.refs_0_), channel_id=1, source_target_pairs={{0,1},{1,0},{2,3},{3,2},{4,5},{5,4},{6,7},{7,6},{8,9},{9,8},{10,11... | collective-permute-start | bytes 884744 | tf_op jit(solution)/shard_map/ppermute | solution.py:80
  38.5 11.9 %collective-permute-start.8 = (bf16[128,1024]{1,0:T(8,128)(2,1)S(1)}, bf16[128,1024]{1,0:T(8,128)(2,1)S(1)}, u32[]{:S(2)}, u32[]{:S(2)}) collective-permute-start(bf16[128,1024]{1,0:T(8,128)(2,1)S(1)} %copy-done.9), channel_id=1, source_target_pairs={{0,6},{1,7},{2,0},{3,1},{4,2},{5,3},{6,4},{7,5},{8,14},{9,15},{10,... | collective-permute-start | bytes 786440 | tf_op jit(solution)/shard_map/ppermute | solution.py:76
  40.8 11.0 %collective-permute-start.7 = (bf16[128,1024]{1,0:T(8,128)(2,1)S(1)}, bf16[128,1024]{1,0:T(8,128)(2,1)S(1)}, u32[]{:S(2)}, u32[]{:S(2)}) collective-permute-start(bf16[128,1024]{1,0:T(8,128)(2,1)S(1)} %copy-done.9), channel_id=1, source_target_pairs={{0,2},{1,3},{2,4},{3,5},{4,6},{5,7},{6,0},{7,1},{8,10},{9,11},{10,... | collective-permute-start | bytes 786440 | tf_op jit(solution)/shard_map/ppermute | solution.py:76
  51.8 3.6 %collective-permute-start.14 = (bf16[128,1536]{1,0:T(8,128)(2,1)S(1)}, bf16[128,1536]{1,0:T(8,128)(2,1)S(1)}, u32[]{:S(2)}, u32[]{:S(2)}) collective-permute-start(bf16[128,1536]{1,0:T(8,128)(2,1)S(1)} %get-tuple-element.122), channel_id=1, source_target_pairs={{0,8},{8,0},{16,24},{24,16},{1,9},{9,1},{17,25},{25,17},{2,10},{10... | collective-permute-start | bytes 1179656 | tf_op jit(solution)/shard_map/ppermute | solution.py:468
  51.8 3.6 %collective-permute-start.15 = (bf16[128,1536]{1,0:T(8,128)(2,1)S(1)}, bf16[128,1536]{1,0:T(8,128)(2,1)S(1)}, u32[]{:S(2)}, u32[]{:S(2)}) collective-permute-start(bf16[128,1536]{1,0:T(8,128)(2,1)S(1)} %get-tuple-element.123), channel_id=1, source_target_pairs={{0,8},{8,0},{16,24},{24,16},{1,9},{9,1},{17,25},{25,17},{2,10},{10... | collective-permute-start | bytes 1179656 | tf_op jit(solution)/shard_map/ppermute | solution.py:468
  52.3 14.7 %collective-permute-start.10 = (bf16[128,1024]{1,0:T(8,128)(2,1)S(1)}, bf16[128,1024]{1,0:T(8,128)(2,1)S(1)}, u32[]{:S(2)}, u32[]{:S(2)}) collective-permute-start(bf16[128,1024]{1,0:T(8,128)(2,1)S(1)} %copy-done.9), channel_id=1, source_target_pairs={{0,4},{1,5},{2,6},{3,7},{4,0},{5,1},{6,2},{7,3},{8,12},{9,13},{10,... | collective-permute-start | bytes 786440 | tf_op jit(solution)/shard_map/ppermute | solution.py:76
  53.3 13.7 %collective-permute-start.11 = (bf16[128,1024]{1,0:T(8,128)(2,1)S(1)}, bf16[128,1024]{1,0:T(8,128)(2,1)S(1)}, u32[]{:S(2)}, u32[]{:S(2)}) collective-permute-start(bf16[128,1024]{1,0:T(8,128)(2,1)S(1)} %collective-permute-done.7.refs_2_), channel_id=1, source_target_pairs={{0,1},{1,0},{2,3},{3,2},{4,5},{5,4},{6,7},{7,6},{8,9},{9,8},{10,11... | collective-permute-start | bytes 786440 | tf_op jit(solution)/shard_map/ppermute | solution.py:80
  53.9 13.2 %collective-permute-start.12 = (bf16[128,1024]{1,0:T(8,128)(2,1)S(1)}, bf16[128,1024]{1,0:T(8,128)(2,1)S(1)}, u32[]{:S(2)}, u32[]{:S(2)}) collective-permute-start(bf16[128,1024]{1,0:T(8,128)(2,1)S(1)} %collective-permute-done.8.refs_3_), channel_id=1, source_target_pairs={{0,1},{1,0},{2,3},{3,2},{4,5},{5,4},{6,7},{7,6},{8,9},{9,8},{10,11... | collective-permute-start | bytes 786440 | tf_op jit(solution)/shard_map/ppermute | solution.py:80
  55.6 22.1 %collective-permute-start.16 = (bf16[256,1536]{1,0:T(8,128)(2,1)S(1)}, bf16[256,1536]{1,0:T(8,128)(2,1)S(1)}, u32[]{:S(2)}, u32[]{:S(2)}) collective-permute-start(bf16[256,1536]{1,0:T(8,128)(2,1)S(1)} %add_convert_fusion.1), channel_id=1, source_target_pairs={{0,16},{8,24},{16,0},{24,8},{1,17},{9,25},{17,1},{25,9},{2,18},{10... | collective-permute-start | bytes 2359304 | tf_op jit(solution)/shard_map/ppermute | solution.py:474
  60.4 17.2 %copy-start.6 = (bf16[256,1536]{1,0:T(8,128)(2,1)}, bf16[256,1536]{1,0:T(8,128)(2,1)S(1)}, u32[]{:S(2)}) copy-start(bf16[256,1536]{1,0:T(8,128)(2,1)S(1)} %get-tuple-element.134.refs_0_) | copy-start | bytes 2359300
  67.0 7.4 %collective-permute-start.13 = (bf16[128,1024]{1,0:T(8,128)(2,1)S(1)}, bf16[128,1024]{1,0:T(8,128)(2,1)S(1)}, u32[]{:S(2)}, u32[]{:S(2)}) collective-permute-start(bf16[128,1024]{1,0:T(8,128)(2,1)S(1)} %collective-permute-done.10.refs_4_), channel_id=1, source_target_pairs={{0,1},{1,0},{2,3},{3,2},{4,5},{5,4},{6,7},{7,6},{8,9},{9,8},{10,11... | collective-permute-start | bytes 786440 | tf_op jit(solution)/shard_map/ppermute | solution.py:80
  77.6 0.9 copy-start.4
  78.5 2.3 %collective-permute-start.19 = (bf16[128,1536]{1,0:T(8,128)(2,1)S(1)}, bf16[128,1536]{1,0:T(8,128)(2,1)S(1)}, u32[]{:S(2)}, u32[]{:S(2)}) collective-permute-start(bf16[128,1536]{1,0:T(8,128)(2,1)S(1)} %get-tuple-element.137), channel_id=1, source_target_pairs={{0,8},{8,0},{16,24},{24,16},{1,9},{9,1},{17,25},{25,17},{2,10},{10... | collective-permute-start | bytes 1179656 | tf_op jit(solution)/shard_map/ppermute | solution.py:468
  78.5 2.8 %collective-permute-start.20 = (bf16[128,1536]{1,0:T(8,128)(2,1)S(1)}, bf16[128,1536]{1,0:T(8,128)(2,1)S(1)}, u32[]{:S(2)}, u32[]{:S(2)}) collective-permute-start(bf16[128,1536]{1,0:T(8,128)(2,1)S(1)} %get-tuple-element.138), channel_id=1, source_target_pairs={{0,8},{8,0},{16,24},{24,16},{1,9},{9,1},{17,25},{25,17},{2,10},{10... | collective-permute-start | bytes 1179656 | tf_op jit(solution)/shard_map/ppermute | solution.py:468
  79.0 17.3 %collective-permute-start.18 = (bf16[256,1536]{1,0:T(8,128)(2,1)}, bf16[256,1536]{1,0:T(8,128)(2,1)}, u32[]{:S(2)}, u32[]{:S(2)}) collective-permute-start(bf16[256,1536]{1,0:T(8,128)(2,1)} %get-tuple-element.135), channel_id=1, source_target_pairs={{0,8},{8,0},{16,24},{24,16},{1,9},{9,1},{17,25},{25,17},{2,10},{10... | collective-permute-start | bytes 2359304 | tf_op jit(solution)/shard_map/ppermute | solution.py:468
  82.4 19.8 %collective-permute-start.21 = (bf16[256,1536]{1,0:T(8,128)(2,1)}, bf16[256,1536]{1,0:T(8,128)(2,1)S(1)}, u32[]{:S(2)}, u32[]{:S(2)}) collective-permute-start(bf16[256,1536]{1,0:T(8,128)(2,1)} %add_convert_fusion), channel_id=1, source_target_pairs={{0,16},{8,24},{16,0},{24,8},{1,17},{9,25},{17,1},{25,9},{2,18},{10... | collective-permute-start | bytes 2359304 | tf_op jit(solution)/shard_map/ppermute | solution.py:474
  87.2 15.1 %collective-permute-start.17 = (bf16[256,1536]{1,0:T(8,128)(2,1)}, bf16[256,1536]{1,0:T(8,128)(2,1)S(1)}, u32[]{:S(2)}, u32[]{:S(2)}) collective-permute-start(bf16[256,1536]{1,0:T(8,128)(2,1)} %get-tuple-element.133), channel_id=1, source_target_pairs={{0,8},{8,0},{16,24},{24,16},{1,9},{9,1},{17,25},{25,17},{2,10},{10... | collective-permute-start | bytes 2359304 | tf_op jit(solution)/shard_map/ppermute | solution.py:468
  92.4 11.7 %all-to-all-start = ((f32[8,2,128]{2,1,0:T(2,128)}), f32[8,2,128]{2,1,0:T(2,128)S(1)}, u32[]{:S(2)}, u32[]{:S(2)}) async-start(f32[8,2,128]{2,1,0:T(2,128)} %get-tuple-element.130), calls=%async_computation | async-start | bytes 16384 | tf_op jit(solution)/shard_map/all_to_all | solution.py:529
  96.4 1.1 %copy-start.5 = (bf16[256,1536]{1,0:T(8,128)(2,1)S(1)}, bf16[256,1536]{1,0:T(8,128)(2,1)}, u32[]{:S(2)}) copy-start(bf16[256,1536]{1,0:T(8,128)(2,1)} %copy-done.4) | copy-start | bytes 2359300
  97.5 1.1 %copy-start.7 = (bf16[256,1536]{1,0:T(8,128)(2,1)S(1)}, bf16[256,1536]{1,0:T(8,128)(2,1)}, u32[]{:S(2)}) copy-start(bf16[256,1536]{1,0:T(8,128)(2,1)} %copy-done.6) | copy-start | bytes 2359300
  102.2 1.9 %copy-start.10 = (s32[128,8]{0,1:T(8,128)S(1)}, s32[128,8]{0,1:T(8,128)}, u32[]{:S(2)}) copy-start(s32[128,8]{0,1:T(8,128)} %param.8) | copy-start | bytes 12292
